TPU v7x, 768 devices: a whole 4x8x12 slice. The times are simulated.
768 devices in a mesh: rep: 64 (over y, x, core), row: 6 (over z_lo), col: 2 (over z_hi).
Axes of the slice: x: 4, y: 8, z: 12 (z_hi: 2, z_lo: 6; z = z_hi * 6 + z_lo), core: 2. Of those that a mesh axis runs over, the one named last changes fastest.
Arguments:
- activations: bfloat16 [49152, 2048], P(('rep', 'row'), 'col'), may hold values from -6 to 6
- out_grads: bfloat16 [49152, 2304], P(('rep', 'col'), 'row'), may hold values from -0.21875 to 0.21875
- error_buffer: float32 [131072, 2304], P(('rep', 'col'), 'row'), may hold values from -6 to 6
- right_factor: float32 [2304, 16], P('row'), may hold values from -6 to 6
Outputs:
- new_error: float32 [131072, 2304], P(('rep', 'col'), 'row')
- new_right: float32 [2304, 16], P('row')
All inputs are finite; a program needn't handle non-finite values.
Results may differ from a plain program's by a relative error of at most 0.0003.
Values may be sent and summed in bfloat16 or wider, within the bound.
No kernel may reach another device: no remote copies, remote signals or barrier semaphores. Data moves between devices by JAX's collectives and lax.ppermute only.
A program may use at most 32 MiB of HBM per device.

v0:
```python
import jax
import jax.numpy as jnp
from jax import lax
from jax.sharding import PartitionSpec as P


def sent_to_all(array, axis):
    copies = jnp.broadcast_to(array, (lax.axis_size(axis), *array.shape))
    return lax.all_to_all(copies, axis, split_axis=0, concat_axis=0, tiled=True)


def in_order(blocks, dim):
    shape = list(blocks.shape[1:])
    shape[dim] *= blocks.shape[0]
    return jnp.moveaxis(blocks, 0, dim).reshape(shape)


def gather_directly(array, axis, dim):
    blocks = sent_to_all(array, axis)
    return in_order(blocks, dim)


def split_up(array, dim, length):
    shape = array.shape
    blocks = array.reshape(*shape[:dim], length, shape[dim] // length, *shape[dim + 1 :])
    return jnp.moveaxis(blocks, dim, 0)


def sent_and_summed(array, axis, dim):
    blocks = split_up(array, dim, lax.axis_size(axis))
    arrived = lax.all_to_all(blocks, axis, split_axis=0, concat_axis=0, tiled=True)
    return arrived.sum(axis=0)


def taken_together(array, axis):
    everything = sent_to_all(array, axis)
    return jnp.sum(everything, axis=0)


def body(activations, out_grads, error_buffer, right_factor):
    highest = lax.Precision.HIGHEST
    gathered_acts = gather_directly(activations, "row", 0)
    gathered_grads = gather_directly(out_grads, "col", 0)
    product = lax.dot_general(
        gathered_acts, gathered_grads, (((0,), (0,)), ((), ())), preferred_element_type=jnp.float32
    )
    target = product + error_buffer
    replicas = lax.axis_size("rep")
    block = target
    left_part = sent_and_summed(jnp.dot(block, right_factor, precision=highest), "rep", 0)
    left_part = taken_together(left_part, "row")
    left_whole = gather_directly(left_part, "rep", 0)
    gram = taken_together(jnp.dot(left_whole.T, left_whole, precision=highest), "col")
    lower = jnp.linalg.cholesky(gram)
    left_orth = jax.scipy.linalg.solve_triangular(lower, left_whole.T, lower=True).T
    block = target
    right_part = sent_and_summed(
        lax.dot_general(
            block,
            left_orth,
            (((0,), (0,)), ((), ())),
            precision=highest,
            preferred_element_type=jnp.float32,
        ),
        "rep",
        0,
    )
    right_part = taken_together(right_part, "col") / replicas
    new_right = gather_directly(right_part, "rep", 0)
    approx = jnp.dot(left_orth, new_right.T, precision=highest)
    return (target - approx, new_right)


def solution(mesh):
    return jax.shard_map(
        body,
        mesh=mesh,
        in_specs=(
            P(("rep", "row"), "col"),
            P(("rep", "col"), "row"),
            P(("rep", "col"), "row"),
            P("row", None),
        ),
        out_specs=(P(("rep", "col"), "row"), P("row", None)),
        check_vma=False,
    )
```

profile of v0, /device:TPU:1, one launch (start us, length us, event | category | flops | bytes accessed | tf_op | source)
XLA Modules:
  0.0 232.0 jit_solution(10083623147238136629)
XLA Ops:
  0.7 1.1 broadcast_in_dim.24
  1.7 29.0 %all_to_all.45 = bf16[2,384,384]{2,1,0:T(8,128)(2,1)S(1)} all-to-all(bf16[2,384,384]{2,1,0:T(8,128)(2,1)S(1)} %broadcast_in_dim.24), channel_id=1, replica_groups=mesh['rep'=64,'row'=6,'col'=2] {'col'}, dimensions={0} | all-to-all | bytes 1179648 | tf_op jit(solution)/shard_map/all_to_all | solution.py:9
  30.9 73.0 %all_to_all.46 = bf16[6,128,1024]{2,1,0:T(8,128)(2,1)S(1)} all-to-all(bf16[6,128,1024]{2,1,0:T(8,128)(2,1)S(1)} %broadcast_in_dim.23), channel_id=1, replica_groups=mesh['rep'=64,'row'=6,'col'=2] {'row'}, dimensions={0} | all-to-all | bytes 3145728 | tf_op jit(solution)/shard_map/all_to_all | solution.py:9
  103.8 1.0 convolution_add_fusion
  104.9 1.4 fusion.5
  107.1 22.0 %all_to_all.47 = f32[64,1,256]{2,1,0:T(1,128)S(1)} all-to-all(f32[64,1,256]{2,1,0:T(1,128)S(1)} %reshape.39), channel_id=1, replica_groups=mesh['rep'=64,'row'=6,'col'=2] {'rep'}, dimensions={0} | all-to-all | bytes 131072 | tf_op jit(solution)/shard_map/all_to_all | solution.py:31
  129.6 0.8 reduce.6
  130.9 11.3 %all_to_all.48 = f32[6,1,256]{2,1,0:T(1,128)S(1)} all-to-all(f32[6,1,256]{2,1,0:T(1,128)S(1)} %reshape.41), channel_id=1, replica_groups=mesh['rep'=64,'row'=6,'col'=2] {'row'}, dimensions={0} | all-to-all | bytes 12288 | tf_op jit(solution)/shard_map/all_to_all | solution.py:9
  142.2 0.7 reduce.7
  143.2 15.2 %all_to_all.49 = f32[64,1,256]{2,1,0:T(1,128)S(1)} all-to-all(f32[64,1,256]{2,1,0:T(1,128)S(1)} %reshape.43), channel_id=1, replica_groups=mesh['rep'=64,'row'=6,'col'=2] {'rep'}, dimensions={0} | all-to-all | bytes 131072 | tf_op jit(solution)/shard_map/all_to_all | solution.py:9
  158.4 0.8 reduce.8
  159.4 1.1 convolution_bitcast_fusion
  160.6 11.3 %all_to_all.50 = f32[2,1,256]{2,1,0:T(1,128)S(1)} all-to-all(f32[2,1,256]{2,1,0:T(1,128)S(1)} %reshape.45), channel_id=1, replica_groups=mesh['rep'=64,'row'=6,'col'=2] {'col'}, dimensions={0} | all-to-all | bytes 4096 | tf_op jit(solution)/shard_map/all_to_all | solution.py:9
  171.8 0.7 reduce.9
  172.7 1.5 cholesky.16
  174.2 0.6 compare_reduce_fusion
  174.8 0.6 fusion.1
  175.5 1.2 custom-call.7
  177.3 2.6 %fusion.6 = f32[384,16]{1,0:T(8,128)S(1)} fusion(f32[1024,384]{1,0:T(8,128)S(1)} %convolution_add_fusion, f32[16,1024]{1,0:T(8,128)S(1)} %fusion.2), kind=kOutput, calls=%fused_computation.18 | convolution fusion | flops 75497472 | bytes 1662976 | tf_op jit(solution)/shard_map/dot_general | solution.py:58
  179.9 18.0 %all_to_all.51 = f32[64,6,16]{2,1,0:T(8,128)S(1)} all-to-all(f32[64,6,16]{2,1,0:T(8,128)S(1)} %reshape.36), channel_id=1, replica_groups=mesh['rep'=64,'row'=6,'col'=2] {'rep'}, dimensions={0} | all-to-all | bytes 49152 | tf_op jit(solution)/shard_map/all_to_all | solution.py:31
  198.0 11.3 %all_to_all.52 = f32[2,6,16]{2,1,0:T(8,128)S(1)} all-to-all(f32[2,6,16]{2,1,0:T(8,128)S(1)} %broadcast_in_dim.28), channel_id=1, replica_groups=mesh['rep'=64,'row'=6,'col'=2] {'col'}, dimensions={0} | all-to-all | bytes 1536 | tf_op jit(solution)/shard_map/all_to_all | solution.py:9
  209.4 18.8 %all_to_all.53 = f32[64,6,16]{2,1,0:T(8,128)S(1)} all-to-all(f32[64,6,16]{2,1,0:T(8,128)S(1)} %broadcast_in_dim.29), channel_id=1, replica_groups=mesh['rep'=64,'row'=6,'col'=2] {'rep'}, dimensions={0} | all-to-all | bytes 49152 | tf_op jit(solution)/shard_map/all_to_all | solution.py:9
  228.3 3.1 %convolution_subtract_fusion = f32[1024,384]{1,0:T(8,128)} fusion(f32[1024,384]{1,0:T(8,128)S(1)} %convolution_add_fusion, f32[16,1024]{1,0:T(8,128)S(1)} %fusion.2, f32[384,16]{1,0:T(8,128)S(1)} %reshape.37), kind=kOutput, calls=%fused_computation | convolution fusion | flops 75890688 | bytes 3235840 | tf_op jit(solution)/shard_map/dot_general | solution.py:70
  231.3 0.7 copy.38
  (36 shorter events, 3.5 us)
Async XLA Ops:
  0.6 104.3 %copy-start = (f32[384,16]{0,1:T(8,128)S(1)}, f32[384,16]{0,1:T(8,128)}, u32[]{:S(2)}) copy-start(f32[384,16]{0,1:T(8,128)} %param.7) | copy-start | bytes 73732
  0.6 30.0 %copy-start.2 = (bf16[128,1024]{1,0:T(8,128)(2,1)S(1)}, bf16[128,1024]{1,0:T(8,128)(2,1)}, u32[]{:S(2)}) copy-start(bf16[128,1024]{1,0:T(8,128)(2,1)} %param.4) | copy-start | bytes 786436
  30.9 73.0 %copy-start.1 = (f32[1024,384]{1,0:T(8,128)S(1)}, f32[1024,384]{1,0:T(8,128)}, u32[]{:S(2)}) copy-start(f32[1024,384]{1,0:T(8,128)} %param.6) | copy-start | bytes 4718596
where the time goes:
time: 233 us; the launch traced here: 232 us
  blocking collectives  210 us (90%)
  matrix products  9.77 us (4%)
  other arithmetic  7.15 us (3%)
  local copies, waits for them, and re-layouts  4.44 us (2%)
    all_to_all x7, blocking collectives, sent_to_all(): return lax.all_to_all(copies, axis, split_axis=0, concat_axis=0, tiled=True)  170 us
    all_to_all x2, blocking collectives, sent_and_summed(): lax.all_to_all(blocks, axis, split_axis=0, concat_axis=0, tiled=True)  40.1 us

commit v1 on v0

v1 whole, which is shorter than its diff:
```python
import jax
import jax.numpy as jnp
from jax import lax
from jax.sharding import Mesh, PartitionSpec as P

REP = ("y", "x", "core")
NEAR = ("x", "core")
HIGHEST = lax.Precision.HIGHEST


def to_all(block, axes):
    copies = jnp.broadcast_to(block, (lax.axis_size(axes), *block.shape))
    return lax.all_to_all(copies, axes, split_axis=0, concat_axis=0, tiled=True)


def summed_over(block, axes):
    return jnp.sum(to_all(block, axes), axis=0)


def split_and_summed(blocks, axes):
    return jnp.sum(lax.all_to_all(blocks, axes, split_axis=0, concat_axis=0, tiled=True), axis=0)


def dot(a, b, dims, precision=HIGHEST):
    return lax.dot_general(
        a, b, (dims, ((), ())), precision=precision, preferred_element_type=jnp.float32
    )


def body(acts, grads, err, right):
    rank = right.shape[1]
    rows, cols = err.shape
    n_row, n_col, n_near = lax.axis_size("row"), lax.axis_size("col"), lax.axis_size(NEAR)
    row, col = lax.axis_index("row"), lax.axis_index("col")
    replicas = lax.axis_size(REP)
    tokens = acts.shape[0]
    right_t = right.T

    with jax.named_scope("gather_inputs"):
        all_acts = lax.all_gather(acts, "row", axis=0, tiled=True)
        other = lax.ppermute(grads, "col", [(0, 1), (1, 0)])
        first = jnp.where(col == 0, grads, other)
        second = jnp.where(col == 0, other, grads)
        all_grads = jnp.concatenate([first, second], axis=0)

    with jax.named_scope("left_terms"):
        proj = dot(right_t, grads.astype(jnp.float32), ((1,), (1,)))
        per = n_row // n_col
        chunks = jnp.moveaxis(proj.reshape(rank, per, tokens), 1, 0)
        empty = jnp.zeros_like(chunks)
        halves = jnp.stack([jnp.where(col == i, chunks, empty) for i in range(n_col)])
        sends = jnp.broadcast_to(
            halves.reshape(n_row, 1, rank, tokens), (n_row, n_col, rank, tokens)
        ).reshape(n_row * n_col, rank, tokens)
        mine = split_and_summed(sends, ("row", "col"))
        left_t = dot(mine, acts.astype(jnp.float32), ((1,), (0,)))
        left_t = left_t + dot(right_t, err, ((1,), (1,)))

    with jax.named_scope("left_sum"):
        wide = rows // n_near
        blocks = jnp.moveaxis(left_t.reshape(rank, n_near, wide), 1, 0)
        part = split_and_summed(blocks, NEAR)
        part = summed_over(part, ("y", "row"))
        left_t = jnp.moveaxis(to_all(part, NEAR), 0, 1).reshape(rank, rows)

    with jax.named_scope("target"):
        target = dot(all_acts, all_grads, ((0,), (0,)), None) + err

    with jax.named_scope("right_sum"):
        gram = dot(left_t, left_t, ((1,), (1,))) / replicas
        right_terms = dot(left_t, target, ((1,), (0,)))
        joint = jnp.concatenate([right_terms, jnp.pad(gram, ((0, 0), (0, 128 - rank)))], axis=1)
        tiles = (cols + 128) // 128
        blocks = joint.reshape(2, rank // 2, tiles, 128).transpose(2, 0, 1, 3)
        blocks = blocks.reshape(n_near, -1, 128)
        part = split_and_summed(blocks, NEAR)
        part = summed_over(part, ("y", "col"))
        joint = to_all(part, NEAR).reshape(tiles, 2, rank // 2, 128)
        joint = joint.transpose(1, 2, 0, 3).reshape(rank, tiles * 128)
        right_t, gram = joint[:, :cols], joint[:, cols : cols + rank]

    with jax.named_scope("finish"):
        lower = jnp.linalg.cholesky(gram)
        inverse = jax.scipy.linalg.solve_triangular(
            lower, jnp.eye(rank, dtype=jnp.float32), lower=True
        )
        new_right_t = dot(inverse, right_t, ((1,), (0,))) / replicas
        orth_t = dot(inverse, left_t, ((1,), (0,)))
        new_error = target - dot(orth_t, new_right_t, ((0,), (0,)))
    return new_error, new_right_t.T


def solution(mesh):
    rep, row, col = (mesh.shape[name] for name in ("rep", "row", "col"))
    fine = Mesh(mesh.devices.reshape(rep // 8, 4, 2, row, col), ("y", "x", "core", "row", "col"))
    return jax.shard_map(
        body,
        mesh=fine,
        in_specs=(
            P((*REP, "row"), "col"),
            P((*REP, "col"), "row"),
            P((*REP, "col"), "row"),
            P("row", None),
        ),
        out_specs=(P((*REP, "col"), "row"), P("row", None)),
        check_vma=False,
    )
```

time: 233 us -> 167 us (0.72)
  blocking collectives: 210 us -> 76.5 us
  waiting for transfers between devices: 0 us -> 32.9 us
  starting transfers between devices: 0 us -> 21.8 us
  between operations: 0.81 us -> 14.2 us
    all_to_all x9 -> x5, blocking collectives: 210 us -> 76.5 us  [the longest x3 44.7 us: split_and_summed(): lax.all_to_all(blocks, axes, split_axis=0, concat_axis=0, tiled=True)]
    all_to_all x0 -> x2, waiting for transfers between devices: none -> 32.1 us  [to_all(): return lax.all_to_all(copies, axes, split_axis=0, concat_axis=0, tiled=True)]
    all_to_all x0 -> x2, starting transfers between devices: none -> 14.4 us  [to_all(): return lax.all_to_all(copies, axes, split_axis=0, concat_axis=0, tiled=True)]
    ppermute x0 -> x1, starting transfers between devices: none -> 7.38 us  [body(): other = lax.ppermute(grads, 'col', [(0, 1), (1, 0)])]
    all_to_all x4 -> x0, other arithmetic: 2.95 us -> none  [the longest x3 2.14 us: sent_to_all(): return lax.all_to_all(copies, axis, split_axis=0, concat_axis=0, tiled=True)]
    dot_general x5 -> x9, matrix products: 9.21 us -> 9.68 us  [dot(): lax.dot_general(a, b, (dims, ((), ())), precision=precision, preferred_el...]
  transfers between devices with their start and end apart: 0 -> 4, of which waited for: 0 -> 2; matrix products, arithmetic and copies ran while one was open for 0% -> 5% of each run, Pallas kernels for 0% -> 0%
where the time goes in v1:
time: 167 us; the launch traced here: 166 us
  blocking collectives  76.5 us (46%)
  waiting for transfers between devices  32.9 us (20%)
  starting transfers between devices  21.8 us (13%)
  between operations  14.2 us (9%)
  matrix products  9.87 us (6%)
  other arithmetic  7 us (4%)
  local copies, waits for them, and re-layouts  3.67 us (2%)
    all_to_all x3, blocking collectives, split_and_summed(): lax.all_to_all(blocks, axes, split_axis=0, concat_axis=0, tiled=True)  44.7 us
    all_to_all x2, waiting for transfers between devices, to_all(): return lax.all_to_all(copies, axes, split_axis=0, concat_axis=0, tiled=True)  32.1 us
    all_to_all x2, blocking collectives, to_all(): return lax.all_to_all(copies, axes, split_axis=0, concat_axis=0, tiled=True)  31.8 us
    all_to_all x2, starting transfers between devices, to_all(): return lax.all_to_all(copies, axes, split_axis=0, concat_axis=0, tiled=True)  14.4 us
    dot_general x9, matrix products, dot(): lax.dot_general(a, b, (dims, ((), ())), precision=precision, preferred_el...  9.68 us
    ppermute x1, starting transfers between devices, body(): other = lax.ppermute(grads, 'col', [(0, 1), (1, 0)])  7.38 us
  transfers between devices with their start and end apart: 4, of which 2 were waited for; matrix products, arithmetic and copies ran while one was open for 5% of the time, Pallas kernels for 0%

profile of v1, /device:TPU:1, one launch (start us, length us, event | category | flops | bytes accessed | tf_op | source)
XLA Modules:
  0.0 165.9 jit_solution(1622161517070380634)
XLA Ops:
  7.2 0.7 all-gather.2.cloned.1.call-update
  7.9 1.3 broadcast_select_fusion.3
  9.4 24.9 %all_to_all.35 = f32[12,16,128]{2,1,0:T(8,128)S(1)} all-to-all(f32[12,16,128]{2,1,0:T(8,128)S(1)} %bitcast.70), channel_id=1, replica_groups=mesh['y'=8,'x'=4,'core'=2,'row'=6,'col'=2] {'row','col'}, dimensions={0} | all-to-all | bytes 196608 | tf_op jit(solution)/shard_map/left_terms/all_to_all | solution.py:21
  34.3 1.2 fusion.19
  35.5 1.4 fusion
  37.0 11.9 %all_to_all.36 = f32[8,16,128]{2,1,0:T(8,128)S(1)} all-to-all(f32[8,16,128]{2,1,0:T(8,128)S(1)} %bitcast.71), channel_id=1, replica_groups=mesh['y'=8,'x'=4,'core'=2,'row'=6,'col'=2] {'x','core'}, dimensions={0} | all-to-all | bytes 131072 | tf_op jit(solution)/shard_map/left_sum/all_to_all | solution.py:21
  48.9 0.8 broadcast_in_dim.27
  49.6 8.1 %all-to-all-start.2 = ((f32[48,16,128]{2,1,0:T(8,128)}), f32[48,16,128]{2,1,0:T(8,128)}, u32[]{:S(2)}, u32[]{:S(2)}) async-start(f32[48,16,128]{2,1,0:T(8,128)} %broadcast_in_dim.27), calls=%async_computation.2 | async-start | bytes 786432 | tf_op jit(solution)/shard_map/left_sum/all_to_all | solution.py:13
  57.8 7.4 %collective-permute-start = (bf16[384,384]{1,0:T(8,128)(2,1)S(1)}, bf16[384,384]{1,0:T(8,128)(2,1)}, u32[]{:S(2)}, u32[]{:S(2)}) collective-permute-start(bf16[384,384]{1,0:T(8,128)(2,1)S(1)} %copy-done.2), channel_id=1, source_target_pairs={{0,1},{1,0},{2,3},{3,2},{4,5},{5,4},{6,7},{7,6},{8,9},{9,8},{10,11... | collective-permute-start | bytes 884744 | tf_op jit(solution)/shard_map/gather_inputs/ppermute | solution.py:41
  65.7 29.1 %all-to-all-done.2 = f32[48,16,128]{2,1,0:T(8,128)} async-done(((f32[48,16,128]{2,1,0:T(8,128)}), f32[48,16,128]{2,1,0:T(8,128)}, u32[]{:S(2)}, u32[]{:S(2)}) %all-to-all-start.2) | async-done | bytes 393248 | tf_op jit(solution)/shard_map/left_sum/all_to_all | solution.py:13
  94.8 1.0 reduce_sum.47
  96.5 6.2 %all-to-all-start.3 = ((f32[8,16,128]{2,1,0:T(8,128)}), f32[8,16,128]{2,1,0:T(8,128)S(1)}, u32[]{:S(2)}, u32[]{:S(2)}) async-start(f32[8,16,128]{2,1,0:T(8,128)} %broadcast_in_dim.28), calls=%async_computation.3 | async-start | bytes 131072 | tf_op jit(solution)/shard_map/left_sum/all_to_all | solution.py:13
  102.7 1.9 %broadcast_select_fusion.1 = (bf16[384,384]{1,0:T(8,128)(2,1)}, bf16[384,384]{1,0:T(8,128)(2,1)}) fusion(bf16[384,384]{1,0:T(8,128)(2,1)S(1)} %copy-done.2, bf16[384,384]{1,0:T(8,128)(2,1)} %collective-permute-done, pred[]{:T(512)S(6)} %eq.4), kind=kLoop, calls=%fused_computation.11 | loop fusion | flops 294912 | bytes 1179649 | tf_op jit(solution)/shard_map/gather_inputs/jit(_where)/select_n | solution.py:42
  104.6 3.0 %all-to-all-done.3 = f32[8,16,128]{2,1,0:T(8,128)S(1)} async-done(((f32[8,16,128]{2,1,0:T(8,128)}), f32[8,16,128]{2,1,0:T(8,128)S(1)}, u32[]{:S(2)}, u32[]{:S(2)}) %all-to-all-start.3) | async-done | bytes 65568 | tf_op jit(solution)/shard_map/left_sum/all_to_all | solution.py:13
  107.8 2.4 %bitcast_add_fusion = f32[1024,384]{0,1:T(8,128)S(1)} fusion(f32[1024,384]{0,1:T(8,128)S(1)} %copy.29, bf16[768,1024]{1,0:T(8,128)(2,1)} %all-gather.2.cloned.1.call-done, bf16[384,384]{1,0:T(8,128)(2,1)} %get-tuple-element.11, bf16[384,384]{1,0:T(8,128)(2,1)} %get-tuple-element.10), kind=kOutput, calls=%fused_computation | convolution fusion | flops 605552640 | bytes 5308416 | tf_op jit(solution)/shard_map/target/dot_general | solution.py:25
  110.2 1.4 fusion.7
  111.6 7.9 %all_to_all.37 = f32[8,8,128]{2,1,0:T(8,128)S(1)} all-to-all(f32[8,8,128]{2,1,0:T(8,128)S(1)} %bitcast.78), channel_id=1, replica_groups=mesh['y'=8,'x'=4,'core'=2,'row'=6,'col'=2] {'x','core'}, dimensions={0} | all-to-all | bytes 65536 | tf_op jit(solution)/shard_map/right_sum/all_to_all | solution.py:21
  119.5 22.6 %all_to_all.38 = f32[16,8,128]{2,1,0:T(8,128)S(1)} all-to-all(f32[16,8,128]{2,1,0:T(8,128)S(1)} %broadcast_in_dim.29), channel_id=1, replica_groups=mesh['y'=8,'x'=4,'core'=2,'row'=6,'col'=2] {'y','col'}, dimensions={0} | all-to-all | bytes 131072 | tf_op jit(solution)/shard_map/right_sum/all_to_all | solution.py:13
  142.1 9.2 %all_to_all.39 = f32[8,8,128]{2,1,0:T(8,128)S(1)} all-to-all(f32[8,8,128]{2,1,0:T(8,128)S(1)} %broadcast_in_dim.30), channel_id=1, replica_groups=mesh['y'=8,'x'=4,'core'=2,'row'=6,'col'=2] {'x','core'}, dimensions={0} | all-to-all | bytes 65536 | tf_op jit(solution)/shard_map/right_sum/all_to_all | solution.py:13
  151.4 1.5 cholesky.17
  153.5 0.6 fusion.14
  154.2 1.2 custom-call.7
  156.0 1.4 convolution_subtract_fusion
  157.5 1.6 copy.38
  (37 shorter events, 2.9 us)
Async XLA Ops:
  7.2 0.8 copy-start
  7.2 28.3 %copy-start.1 = (f32[1024,384]{1,0:T(8,128)S(1)}, f32[1024,384]{1,0:T(8,128)}, u32[]{:S(2)}) copy-start(f32[1024,384]{1,0:T(8,128)} %param.6) | copy-start | bytes 4718596
  7.2 100.6 %all-gather.2.cloned.1.call-start = ((), (), s32[]{:S(2)}) async-start(), calls=%async_computation.7 | async-start | bytes 1835008 | tf_op jit(solution)/shard_map/gather_inputs/all_gather | solution.py:40
  35.5 22.3 %copy-start.2 = (bf16[384,384]{1,0:T(8,128)(2,1)S(1)}, bf16[384,384]{1,0:T(8,128)(2,1)}, u32[]{:S(2)}) copy-start(bf16[384,384]{1,0:T(8,128)(2,1)} %param.5) | copy-start | bytes 884740
  49.6 45.2 %all-to-all-start.2 = ((f32[48,16,128]{2,1,0:T(8,128)}), f32[48,16,128]{2,1,0:T(8,128)}, u32[]{:S(2)}, u32[]{:S(2)}) async-start(f32[48,16,128]{2,1,0:T(8,128)} %broadcast_in_dim.27), calls=%async_computation.2 | async-start | bytes 786432 | tf_op jit(solution)/shard_map/left_sum/all_to_all | solution.py:13
  57.8 44.9 %collective-permute-start = (bf16[384,384]{1,0:T(8,128)(2,1)S(1)}, bf16[384,384]{1,0:T(8,128)(2,1)}, u32[]{:S(2)}, u32[]{:S(2)}) collective-permute-start(bf16[384,384]{1,0:T(8,128)(2,1)S(1)} %copy-done.2), channel_id=1, source_target_pairs={{0,1},{1,0},{2,3},{3,2},{4,5},{5,4},{6,7},{7,6},{8,9},{9,8},{10,11... | collective-permute-start | bytes 884744 | tf_op jit(solution)/shard_map/gather_inputs/ppermute | solution.py:41
  96.5 11.1 %all-to-all-start.3 = ((f32[8,16,128]{2,1,0:T(8,128)}), f32[8,16,128]{2,1,0:T(8,128)S(1)}, u32[]{:S(2)}, u32[]{:S(2)}) async-start(f32[8,16,128]{2,1,0:T(8,128)} %broadcast_in_dim.28), calls=%async_computation.3 | async-start | bytes 131072 | tf_op jit(solution)/shard_map/left_sum/all_to_all | solution.py:13
  155.8 1.7 copy-start.3
Sparse Core Ops, SparseCore 0:
  10.4 73.2 all-gather.1

commit v2 on v1

v2 whole, which is shorter than its diff:
```python
import functools

import jax
import jax.numpy as jnp
from jax import lax
from jax.experimental import pallas as pl
from jax.experimental.pallas import tpu as pltpu
from jax.sharding import Mesh, PartitionSpec as P

REP = ("y", "x", "core")
NEAR = ("x", "core")
HIGHEST = lax.Precision.HIGHEST


def to_all(block, axes):
    copies = jnp.broadcast_to(block, (lax.axis_size(axes), *block.shape))
    return lax.all_to_all(copies, axes, split_axis=0, concat_axis=0, tiled=True)


def summed_over(block, axes):
    return jnp.sum(to_all(block, axes), axis=0)


def split_and_summed(blocks, axes):
    return jnp.sum(lax.all_to_all(blocks, axes, split_axis=0, concat_axis=0, tiled=True), axis=0)


def dot(a, b, dims, precision=HIGHEST):
    return lax.dot_general(
        a, b, (dims, ((), ())), precision=precision, preferred_element_type=jnp.float32
    )


def thirds(x):
    first = x.astype(jnp.bfloat16)
    rest = x - first.astype(jnp.float32)
    second = rest.astype(jnp.bfloat16)
    third = (rest - second.astype(jnp.float32)).astype(jnp.bfloat16)
    return first, second, third


def mxu(a, b, contract):
    return lax.dot_general(a, b, (contract, ((), ())), preferred_element_type=jnp.float32)


def lanes(ref, start, count):
    return jnp.concatenate([ref[start + k] for k in range(count)], axis=1)


def target_kernel(
    replicas, col_ref, acts_ref, mine_ref, other_ref, err_ref, left_ref, target_ref, joint_ref, sums
):
    step = pl.program_id(0)
    half = mine_ref.shape[0]
    mine_at = pl.multiple_of(col_ref[0] * half, half)
    other_at = pl.multiple_of((1 - col_ref[0]) * half, half)
    tile = mxu(acts_ref[pl.ds(mine_at, half), :], mine_ref[...], ((0,), (0,)))
    tile += mxu(acts_ref[pl.ds(other_at, half), :], other_ref[...], ((0,), (0,)))
    tile += err_ref[...]
    target_ref[...] = tile

    per = err_ref.shape[0] // left_ref.shape[2]
    rank = left_ref.shape[1]
    left = jnp.concatenate([left_ref[step * per + k] for k in range(per)], axis=1)
    stack = jnp.concatenate(thirds(left), axis=0)
    high, mid, low = thirds(tile)
    terms = mxu(stack, high, ((1,), (0,))) + mxu(stack, mid, ((1,), (0,)))
    right = terms[:rank] + terms[rank : 2 * rank] + terms[2 * rank :]
    right += mxu(stack[:rank], low, ((1,), (0,)))
    gram = lax.dot_general(
        left,
        left,
        (((1,), (1,)), ((), ())),
        precision=HIGHEST,
        preferred_element_type=jnp.float32,
    )
    gram = jnp.concatenate([gram, jnp.zeros((rank, 128 - rank), jnp.float32)], axis=1) / replicas
    both = jnp.concatenate([right, gram], axis=1)

    @pl.when(step == 0)
    def _():
        sums[...] = both

    @pl.when(step > 0)
    def _():
        sums[...] += both

    @pl.when(step == pl.num_programs(0) - 1)
    def _():
        for k in range(joint_ref.shape[0]):
            rows, at = (k % 2) * (rank // 2), (k // 2) * 128
            joint_ref[k] = sums[rows : rows + rank // 2, at : at + 128]


def target_and_terms(acts, mine, other, err, left, col, replicas):
    rows, cols = err.shape
    rank, wide = left.shape[1], 256
    tiles = cols // 128 + 1
    whole = lambda shape: pl.BlockSpec(shape, lambda i: (0,) * len(shape))
    return pl.pallas_call(
        functools.partial(target_kernel, replicas),
        grid=(rows // wide,),
        in_specs=[
            pl.BlockSpec(memory_space=pltpu.SMEM),
            pl.BlockSpec((acts.shape[0], wide), lambda i: (0, i)),
            whole(mine.shape),
            whole(other.shape),
            pl.BlockSpec((wide, cols), lambda i: (i, 0)),
            whole(left.shape),
        ],
        out_specs=[
            pl.BlockSpec((wide, cols), lambda i: (i, 0)),
            whole((2 * tiles, rank // 2, 128)),
        ],
        out_shape=[
            jax.ShapeDtypeStruct((rows, cols), jnp.float32),
            jax.ShapeDtypeStruct((2 * tiles, rank // 2, 128), jnp.float32),
        ],
        scratch_shapes=[pltpu.VMEM((rank, tiles * 128), jnp.float32)],
        compiler_params=pltpu.CompilerParams(vmem_limit_bytes=24 * 2**20),
    )(col.reshape(1), acts, mine, other, err, left)


def finish_kernel(replicas, joint_ref, left_ref, target_ref, error_ref, right_ref, orths, rights):
    step = pl.program_id(0)
    rank, cols = right_ref.shape

    @pl.when(step == 0)
    def _():
        halves = [
            jnp.concatenate([joint_ref[2 * c + h] for c in range(joint_ref.shape[0] // 2)], axis=1)
            for h in range(2)
        ]
        joint = jnp.concatenate(halves, axis=0)
        system = jnp.concatenate([joint, lanes(left_ref, 0, left_ref.shape[0])], axis=1)
        row_of = lax.broadcasted_iota(jnp.int32, (rank, 1), 0)
        for k in range(rank):
            column = system[:, cols + k : cols + k + 1]
            pivot = jnp.sqrt(column[k : k + 1])
            row = system[k : k + 1] / pivot
            factor = jnp.where(row_of > k, column / pivot, 0.0)
            system = jnp.where(row_of == k, row, system - factor * row)
        right = system[:, :cols] / replicas
        right_ref[...] = right
        first, second, third = thirds(right)
        rights[...] = jnp.concatenate([first, second, first, second, third, first], axis=0)
        first, second, third = thirds(system[:, cols + 128 :])
        orths[...] = jnp.concatenate([first, first, second, second, first, third], axis=0)

    wide = target_ref.shape[0]
    orth = orths[:, pl.ds(pl.multiple_of(step * wide, wide), wide)]
    error_ref[...] = target_ref[...] - mxu(orth, rights[...], ((0,), (0,)))


def finish(joint, left, target, replicas):
    rows, cols = target.shape
    rank, wide = left.shape[1], 256
    whole = lambda shape: pl.BlockSpec(shape, lambda i: (0,) * len(shape))
    return pl.pallas_call(
        functools.partial(finish_kernel, replicas),
        grid=(rows // wide,),
        in_specs=[
            whole(joint.shape),
            whole(left.shape),
            pl.BlockSpec((wide, cols), lambda i: (i, 0)),
        ],
        out_specs=[pl.BlockSpec((wide, cols), lambda i: (i, 0)), whole((rank, cols))],
        out_shape=[
            jax.ShapeDtypeStruct((rows, cols), jnp.float32),
            jax.ShapeDtypeStruct((rank, cols), jnp.float32),
        ],
        scratch_shapes=[
            pltpu.VMEM((6 * rank, rows), jnp.bfloat16),
            pltpu.VMEM((6 * rank, cols), jnp.bfloat16),
        ],
        compiler_params=pltpu.CompilerParams(vmem_limit_bytes=24 * 2**20),
    )(joint, left, target)


def body(acts, grads, err, right):
    rank = right.shape[1]
    rows = err.shape[0]
    n_row, n_col, n_near = lax.axis_size("row"), lax.axis_size("col"), lax.axis_size(NEAR)
    col = lax.axis_index("col")
    replicas = lax.axis_size(REP)
    tokens = acts.shape[0]
    right_t = right.T

    with jax.named_scope("gather_inputs"):
        all_acts = lax.all_gather(acts, "row", axis=0, tiled=True)
        other = lax.ppermute(grads, "col", [(0, 1), (1, 0)])

    with jax.named_scope("left_terms"):
        proj = dot(right_t, grads.astype(jnp.float32), ((1,), (1,)))
        per = n_row // n_col
        chunks = jnp.moveaxis(proj.reshape(rank, per, tokens), 1, 0)
        empty = jnp.zeros_like(chunks)
        halves = jnp.stack([jnp.where(col == i, chunks, empty) for i in range(n_col)])
        sends = jnp.broadcast_to(
            halves.reshape(n_row, 1, rank, tokens), (n_row, n_col, rank, tokens)
        ).reshape(n_row * n_col, rank, tokens)
        mine = split_and_summed(sends, ("row", "col"))
        left_t = dot(mine, acts.astype(jnp.float32), ((1,), (0,)))
        left_t = left_t + dot(right_t, err, ((1,), (1,)))

    with jax.named_scope("left_sum"):
        wide = rows // n_near
        blocks = jnp.moveaxis(left_t.reshape(rank, n_near, wide), 1, 0)
        part = split_and_summed(blocks, NEAR)
        part = summed_over(part, "y")
        part = summed_over(part, "row")
        left = to_all(part, NEAR)

    with jax.named_scope("target"):
        target, joint = target_and_terms(all_acts, grads, other, err, left, col, replicas)

    with jax.named_scope("right_sum"):
        part = split_and_summed(joint, NEAR)
        part = summed_over(part, ("y", "col"))
        joint = to_all(part, NEAR)

    with jax.named_scope("finish"):
        new_error, new_right_t = finish(joint, left, target, replicas)
    return new_error, new_right_t.T


def solution(mesh):
    rep, row, col = (mesh.shape[name] for name in ("rep", "row", "col"))
    fine = Mesh(mesh.devices.reshape(rep // 8, 4, 2, row, col), ("y", "x", "core", "row", "col"))
    return jax.shard_map(
        body,
        mesh=fine,
        in_specs=(
            P((*REP, "row"), "col"),
            P((*REP, "col"), "row"),
            P((*REP, "col"), "row"),
            P("row", None),
        ),
        out_specs=(P((*REP, "col"), "row"), P("row", None)),
        check_vma=False,
    )
```

time: 167 us -> 159 us (0.952)
  blocking collectives: 76.5 us -> 104 us
  waiting for transfers between devices: 32.9 us -> 8.87 us
  other arithmetic: 7 us -> 0.09 us
  Pallas kernels: 0 us -> 6.88 us
  starting transfers between devices: 21.8 us -> 15.6 us
  matrix products: 9.87 us -> 3.92 us
    all_to_all x2 -> x3, blocking collectives: 31.8 us -> 59.7 us  [to_all(): return lax.all_to_all(copies, axes, split_axis=0, concat_axis=0, tiled=True)]
    all_to_all x2, waiting for transfers between devices: 32.1 us -> 8.19 us  [to_all(): return lax.all_to_all(copies, axes, split_axis=0, concat_axis=0, tiled=True)]
    pallas_call x0 -> x2, Pallas kernels: none -> 6.88 us  [the longest x1 3.77 us: finish(): pl.pallas_call(functools.partial(finish_kernel, replicas), grid=(rows //...]
    dot_general x9 -> x3, matrix products: 9.68 us -> 3.92 us  [dot(): lax.dot_general(a, b, (dims, ((), ())), precision=precision, preferred_el...]
    another operation x5 -> x0, other arithmetic: 4.01 us -> none  [the longest x3 2.13 us: body(): lower = jnp.linalg.cholesky(gram)]
    ppermute x1, starting transfers between devices: 7.38 us -> 3.56 us  [body(): other = lax.ppermute(grads, 'col', [(0, 1), (1, 0)])]
    all_to_all x2, starting transfers between devices: 14.4 us -> 12 us  [to_all(): return lax.all_to_all(copies, axes, split_axis=0, concat_axis=0, tiled=True)]
    select_n x1 -> x0, other arithmetic: 1.85 us -> none  [body(): first = jnp.where(col == 0, grads, other)]
  transfers between devices with their start and end apart: 4 -> 4, of which waited for: 2 -> 2; matrix products, arithmetic and copies ran while one was open for 5% -> 3% of each run, Pallas kernels for 0% -> 0%
where the time goes in v2:
time: 159 us; the launch traced here: 158 us
  blocking collectives  104 us (65%)
  starting transfers between devices  15.6 us (10%)
  between operations  14.2 us (9%)
  waiting for transfers between devices  8.87 us (6%)
  Pallas kernels  6.88 us (4%)
  local copies, waits for them, and re-layouts  4.45 us (3%)
  matrix products  3.92 us (2%)
    all_to_all x3, blocking collectives, to_all(): return lax.all_to_all(copies, axes, split_axis=0, concat_axis=0, tiled=True)  59.7 us
    all_to_all x3, blocking collectives, split_and_summed(): lax.all_to_all(blocks, axes, split_axis=0, concat_axis=0, tiled=True)  44.8 us
    all_to_all x2, starting transfers between devices, to_all(): return lax.all_to_all(copies, axes, split_axis=0, concat_axis=0, tiled=True)  12 us
    all_to_all x2, waiting for transfers between devices, to_all(): return lax.all_to_all(copies, axes, split_axis=0, concat_axis=0, tiled=True)  8.19 us
    dot_general x3, matrix products, dot(): lax.dot_general(a, b, (dims, ((), ())), precision=precision, preferred_el...  3.92 us
    pallas_call x1, Pallas kernels, finish(): pl.pallas_call(functools.partial(finish_kernel, replicas), grid=(rows //...  3.77 us
    ppermute x1, starting transfers between devices, body(): other = lax.ppermute(grads, 'col', [(0, 1), (1, 0)])  3.56 us
  transfers between devices with their start and end apart: 4, of which 2 were waited for; matrix products, arithmetic and copies ran while one was open for 3% of the time, Pallas kernels for 0%

profile of v2, /device:TPU:1, one launch (start us, length us, event | category | flops | bytes accessed | tf_op | source)
XLA Modules:
  0.0 158.5 jit_solution(9391887293252741768)
XLA Ops:
  7.2 0.0 copy-start
  7.2 0.0 all-gather.2.cloned.1.call-start
  7.2 0.7 all-gather.2.cloned.1.call-update
  7.9 1.3 broadcast_select_fusion.1
  9.4 25.1 %all_to_all.40 = f32[12,16,128]{2,1,0:T(8,128)S(1)} all-to-all(f32[12,16,128]{2,1,0:T(8,128)S(1)} %bitcast.24), channel_id=1, replica_groups=mesh['y'=8,'x'=4,'core'=2,'row'=6,'col'=2] {'row','col'}, dimensions={0} | all-to-all | bytes 196608 | tf_op jit(solution)/shard_map/left_terms/all_to_all | solution.py:25
  34.5 1.2 fusion.1
  35.7 1.4 fusion
  37.1 11.9 %all_to_all.41 = f32[8,16,128]{2,1,0:T(8,128)S(1)} all-to-all(f32[8,16,128]{2,1,0:T(8,128)S(1)} %bitcast.25), channel_id=1, replica_groups=mesh['y'=8,'x'=4,'core'=2,'row'=6,'col'=2] {'x','core'}, dimensions={0} | all-to-all | bytes 131072 | tf_op jit(solution)/shard_map/left_sum/all_to_all | solution.py:25
  49.0 0.6 broadcast_in_dim.28
  49.6 6.8 %all-to-all-start.2 = ((f32[8,16,128]{2,1,0:T(8,128)}), f32[8,16,128]{2,1,0:T(8,128)S(1)}, u32[]{:S(2)}, u32[]{:S(2)}) async-start(f32[8,16,128]{2,1,0:T(8,128)} %broadcast_in_dim.28), calls=%async_computation.2 | async-start | bytes 131072 | tf_op jit(solution)/shard_map/left_sum/all_to_all | solution.py:17
  56.5 3.6 %collective-permute-start = (bf16[384,384]{1,0:T(8,128)(2,1)S(1)}, bf16[384,384]{1,0:T(8,128)(2,1)S(1)}, u32[]{:S(2)}, u32[]{:S(2)}) collective-permute-start(bf16[384,384]{1,0:T(8,128)(2,1)S(1)} %copy-done.3), channel_id=1, source_target_pairs={{0,1},{1,0},{2,3},{3,2},{4,5},{5,4},{6,7},{7,6},{8,9},{9,8},{10,11... | collective-permute-start | bytes 884744 | tf_op jit(solution)/shard_map/gather_inputs/ppermute | solution.py:191
  60.0 4.1 %all-to-all-done.2 = f32[8,16,128]{2,1,0:T(8,128)S(1)} async-done(((f32[8,16,128]{2,1,0:T(8,128)}), f32[8,16,128]{2,1,0:T(8,128)S(1)}, u32[]{:S(2)}, u32[]{:S(2)}) %all-to-all-start.2) | async-done | bytes 65568 | tf_op jit(solution)/shard_map/left_sum/all_to_all | solution.py:17
  64.1 25.0 %all_to_all.42 = f32[6,16,128]{2,1,0:T(8,128)S(1)} all-to-all(f32[6,16,128]{2,1,0:T(8,128)S(1)} %broadcast_in_dim.29), channel_id=1, replica_groups=mesh['y'=8,'x'=4,'core'=2,'row'=6,'col'=2] {'row'}, dimensions={0} | all-to-all | bytes 98304 | tf_op jit(solution)/shard_map/left_sum/all_to_all | solution.py:17
  89.1 0.6 broadcast_in_dim.30
  89.7 5.2 %all-to-all-start.4 = ((f32[8,16,128]{2,1,0:T(8,128)}), f32[8,16,128]{2,1,0:T(8,128)S(1)}, u32[]{:S(2)}, u32[]{:S(2)}) async-start(f32[8,16,128]{2,1,0:T(8,128)} %broadcast_in_dim.30), calls=%async_computation.4 | async-start | bytes 131072 | tf_op jit(solution)/shard_map/left_sum/all_to_all | solution.py:17
  94.9 0.7 copy-done.4
  95.6 4.1 %all-to-all-done.4.left_ref = f32[8,16,128]{2,1,0:T(8,128)S(1)} async-done(((f32[8,16,128]{2,1,0:T(8,128)}), f32[8,16,128]{2,1,0:T(8,128)S(1)}, u32[]{:S(2)}, u32[]{:S(2)}) %all-to-all-start.4) | async-done | bytes 65568 | tf_op jit(solution)/shard_map/left_sum/all_to_all | solution.py:17
  99.7 1.4 copy-done.2
  101.1 1.0 copy-done.5
  102.1 3.1 %target.1 = (f32[1024,384]{1,0:T(8,128)S(1)}, f32[8,8,128]{2,1,0:T(8,128)S(1)}) custom-call(s32[1]{0:T(128)} %bitcast.col_ref, bf16[768,1024]{1,0:T(8,128)(2,1)S(1)} %copy-done.2, bf16[384,384]{1,0:T(8,128)(2,1)S(1)} %copy-done.3, bf16[384,384]{1,0:T(8,128)(2,1)S(1)} %copy-done.5, f32[1024,384]{1,0:T(8,128)S(1)} %copy-done.1, ...), custom_call_target="tpu_custom_call" | custom-call | tf_op jit(solution)/shard_map/target/pallas_call | solution.py:100
  105.2 7.9 %all_to_all.43 = f32[8,8,128]{2,1,0:T(8,128)S(1)} all-to-all(f32[8,8,128]{2,1,0:T(8,128)S(1)} %get-tuple-element.6), channel_id=1, replica_groups=mesh['y'=8,'x'=4,'core'=2,'row'=6,'col'=2] {'x','core'}, dimensions={0} | all-to-all | bytes 65536 | tf_op jit(solution)/shard_map/right_sum/all_to_all | solution.py:25
  113.1 25.5 %all_to_all.44 = f32[16,8,128]{2,1,0:T(8,128)S(1)} all-to-all(f32[16,8,128]{2,1,0:T(8,128)S(1)} %broadcast_in_dim.31), channel_id=1, replica_groups=mesh['y'=8,'x'=4,'core'=2,'row'=6,'col'=2] {'y','col'}, dimensions={0} | all-to-all | bytes 131072 | tf_op jit(solution)/shard_map/right_sum/all_to_all | solution.py:17
  138.6 9.2 %all_to_all.45.joint_ref = f32[8,8,128]{2,1,0:T(8,128)S(1)} all-to-all(f32[8,8,128]{2,1,0:T(8,128)S(1)} %broadcast_in_dim.32), channel_id=1, replica_groups=mesh['y'=8,'x'=4,'core'=2,'row'=6,'col'=2] {'x','core'}, dimensions={0} | all-to-all | bytes 65536 | tf_op jit(solution)/shard_map/right_sum/all_to_all | solution.py:17
  147.8 3.8 %finish.1 = (f32[1024,384]{1,0:T(8,128)}, f32[16,384]{1,0:T(8,128)}) custom-call(f32[8,8,128]{2,1,0:T(8,128)S(1)} %all_to_all.45.joint_ref, f32[8,16,128]{2,1,0:T(8,128)S(1)} %all-to-all-done.4.left_ref, f32[1024,384]{1,0:T(8,128)S(1)} %get-tuple-element.7.target_ref), custom_call_target="tpu_custom_call" | custom-call | tf_op jit(solution)/shard_map/finish/pallas_call | solution.py:159
  (25 shorter events, 0.2 us)
Async XLA Ops:
  7.2 0.8 copy-start
  7.2 28.5 %copy-start.1 = (f32[1024,384]{1,0:T(8,128)S(1)}, f32[1024,384]{1,0:T(8,128)}, u32[]{:S(2)}) copy-start(f32[1024,384]{1,0:T(8,128)} %err_ref.1) | copy-start | bytes 4718596
  7.2 92.5 %all-gather.2.cloned.1.call-start = ((), (), s32[]{:S(2)}) async-start(), calls=%async_computation.8 | async-start | bytes 1835008 | tf_op jit(solution)/shard_map/gather_inputs/all_gather | solution.py:190
  9.4 47.1 %copy-start.3 = (bf16[384,384]{1,0:T(8,128)(2,1)S(1)}, bf16[384,384]{1,0:T(8,128)(2,1)}, u32[]{:S(2)}) copy-start(bf16[384,384]{1,0:T(8,128)(2,1)} %mine_ref.1) | copy-start | bytes 884740
  49.6 14.4 %all-to-all-start.2 = ((f32[8,16,128]{2,1,0:T(8,128)}), f32[8,16,128]{2,1,0:T(8,128)S(1)}, u32[]{:S(2)}, u32[]{:S(2)}) async-start(f32[8,16,128]{2,1,0:T(8,128)} %broadcast_in_dim.28), calls=%async_computation.2 | async-start | bytes 131072 | tf_op jit(solution)/shard_map/left_sum/all_to_all | solution.py:17
  56.5 38.4 %collective-permute-start = (bf16[384,384]{1,0:T(8,128)(2,1)S(1)}, bf16[384,384]{1,0:T(8,128)(2,1)S(1)}, u32[]{:S(2)}, u32[]{:S(2)}) collective-permute-start(bf16[384,384]{1,0:T(8,128)(2,1)S(1)} %copy-done.3), channel_id=1, source_target_pairs={{0,1},{1,0},{2,3},{3,2},{4,5},{5,4},{6,7},{7,6},{8,9},{9,8},{10,11... | collective-permute-start | bytes 884744 | tf_op jit(solution)/shard_map/gather_inputs/ppermute | solution.py:191
  89.7 10.0 %all-to-all-start.4 = ((f32[8,16,128]{2,1,0:T(8,128)}), f32[8,16,128]{2,1,0:T(8,128)S(1)}, u32[]{:S(2)}, u32[]{:S(2)}) async-start(f32[8,16,128]{2,1,0:T(8,128)} %broadcast_in_dim.30), calls=%async_computation.4 | async-start | bytes 131072 | tf_op jit(solution)/shard_map/left_sum/all_to_all | solution.py:17
  94.9 0.7 copy-start.4
  99.7 1.4 copy-start.2
  101.1 1.0 copy-start.5
Sparse Core Ops, SparseCore 0:
  10.4 69.5 all-gather.1

commit v3 on v2

--- a/solution.py
+++ b/solution.py
@@ -47,26 +47,82 @@
     return jnp.concatenate([ref[start + k] for k in range(count)], axis=1)
 
 
+def joined(terms, rank):
+    return terms[:rank] + terms[rank : 2 * rank] + terms[2 * rank :]
+
+
+def projection_kernel(n_col, col_ref, right_ref, grads_ref, sends_ref):
+    rank = right_ref.shape[0]
+    per = sends_ref.shape[0] // n_col // n_col
+    wide = sends_ref.shape[2]
+    stack = jnp.concatenate(thirds(right_ref[...]), axis=0)
+    proj = joined(mxu(stack, grads_ref[...], ((1,), (1,))), rank)
+    for k in range(sends_ref.shape[0]):
+        owner = k // n_col
+        at = owner % per * wide
+        keep = (col_ref[0] == owner // per).astype(jnp.float32)
+        sends_ref[k] = proj[:, at : at + wide] * keep
+
+
+def error_kernel(right_ref, err_ref, out_ref):
+    rank = right_ref.shape[0]
+    stack = jnp.concatenate(thirds(right_ref[...]), axis=0)
+    wide = 256
+    for k in range(err_ref.shape[0] // wide):
+        high, mid, low = thirds(err_ref[k * wide : (k + 1) * wide])
+        terms = joined(mxu(stack, high, ((1,), (1,))) + mxu(stack, mid, ((1,), (1,))), rank)
+        out_ref[:, k * wide : (k + 1) * wide] = terms + mxu(stack[:rank], low, ((1,), (1,)))
+
+
+def left_kernel(mine_ref, acts_ref, part_ref, out_ref):
+    rank = mine_ref.shape[1]
+    mine = mine_ref[0]
+    for k in range(1, mine_ref.shape[0]):
+        mine += mine_ref[k]
+    stack = jnp.concatenate(thirds(mine), axis=0)
+    left = joined(mxu(stack, acts_ref[...], ((1,), (0,))), rank) + part_ref[...]
+    wide = out_ref.shape[2]
+    for k in range(out_ref.shape[0]):
+        out_ref[k] = left[:, k * wide : (k + 1) * wide]
+
+
+def local_call(kernel, out_shape, *args, scalars=0):
+    return pl.pallas_call(
+        kernel,
+        in_specs=[pl.BlockSpec(memory_space=pltpu.SMEM)] * scalars
+        + [pl.BlockSpec(memory_space=pltpu.VMEM)] * (len(args) - scalars),
+        out_specs=pl.BlockSpec(memory_space=pltpu.VMEM),
+        out_shape=jax.ShapeDtypeStruct(out_shape, jnp.float32),
+        compiler_params=pltpu.CompilerParams(vmem_limit_bytes=16 * 2**20),
+    )(*args)
+
+
 def target_kernel(
-    replicas, col_ref, acts_ref, mine_ref, other_ref, err_ref, left_ref, target_ref, joint_ref, sums
+    replicas, col_ref, acts_ref, mine_ref, other_ref, err_ref, left_ref,
+    target_ref, joint_ref, acts, other, err, target, sems, err_sems, out_sems,
 ):
-    step = pl.program_id(0)
     half = mine_ref.shape[0]
+    rows = err_ref.shape[0]
+    rank = left_ref.shape[1]
+    wide = rows // sems.shape[0]
     mine_at = pl.multiple_of(col_ref[0] * half, half)
     other_at = pl.multiple_of((1 - col_ref[0]) * half, half)
-    tile = mxu(acts_ref[pl.ds(mine_at, half), :], mine_ref[...], ((0,), (0,)))
-    tile += mxu(acts_ref[pl.ds(other_at, half), :], other_ref[...], ((0,), (0,)))
-    tile += err_ref[...]
-    target_ref[...] = tile
-
-    per = err_ref.shape[0] // left_ref.shape[2]
-    rank = left_ref.shape[1]
-    left = jnp.concatenate([left_ref[step * per + k] for k in range(per)], axis=1)
+    spans = [slice(k * wide, (k + 1) * wide) for k in range(rows // wide)]
+    other_copy = pltpu.make_async_copy(other_ref, other, out_sems.at[len(spans)])
+    other_copy.start()
+    in_copies = []
+    for k, span in enumerate(spans):
+        in_copies.append(
+            (
+                pltpu.make_async_copy(acts_ref.at[:, span], acts.at[:, span], sems.at[k]),
+                pltpu.make_async_copy(err_ref.at[span], err.at[span], err_sems.at[k]),
+            )
+        )
+        for copy in in_copies[-1]:
+            copy.start()
+
+    left = lanes(left_ref, 0, left_ref.shape[0])
     stack = jnp.concatenate(thirds(left), axis=0)
-    high, mid, low = thirds(tile)
-    terms = mxu(stack, high, ((1,), (0,))) + mxu(stack, mid, ((1,), (0,)))
-    right = terms[:rank] + terms[rank : 2 * rank] + terms[2 * rank :]
-    right += mxu(stack[:rank], low, ((1,), (0,)))
     gram = lax.dot_general(
         left,
         left,
@@ -74,50 +130,62 @@
         precision=HIGHEST,
         preferred_element_type=jnp.float32,
     )
+    other_copy.wait()
+    sums, out_copies = None, []
+    for k, span in enumerate(spans):
+        for copy in in_copies[k]:
+            copy.wait()
+        tile = mxu(acts[pl.ds(mine_at, half), span], mine_ref[...], ((0,), (0,)))
+        tile += mxu(acts[pl.ds(other_at, half), span], other[...], ((0,), (0,)))
+        tile += err[span]
+        target[span] = tile
+        out_copies.append(pltpu.make_async_copy(target.at[span], target_ref.at[span], out_sems.at[k]))
+        out_copies[-1].start()
+        high, mid, low = thirds(tile)
+        terms = mxu(stack[:, span], high, ((1,), (0,))) + mxu(stack[:, span], mid, ((1,), (0,)))
+        right = joined(terms, rank) + mxu(stack[:rank, span], low, ((1,), (0,)))
+        sums = right if sums is None else sums + right
     gram = jnp.concatenate([gram, jnp.zeros((rank, 128 - rank), jnp.float32)], axis=1) / replicas
-    both = jnp.concatenate([right, gram], axis=1)
-
-    @pl.when(step == 0)
-    def _():
-        sums[...] = both
-
-    @pl.when(step > 0)
-    def _():
-        sums[...] += both
-
-    @pl.when(step == pl.num_programs(0) - 1)
-    def _():
-        for k in range(joint_ref.shape[0]):
-            rows, at = (k % 2) * (rank // 2), (k // 2) * 128
-            joint_ref[k] = sums[rows : rows + rank // 2, at : at + 128]
+    both = jnp.concatenate([sums, gram], axis=1)
+    for k in range(joint_ref.shape[0]):
+        first, at = (k % 2) * (rank // 2), (k // 2) * 128
+        joint_ref[k] = both[first : first + rank // 2, at : at + 128]
+    for copy in out_copies:
+        copy.wait()
 
 
 def target_and_terms(acts, mine, other, err, left, col, replicas):
     rows, cols = err.shape
-    rank, wide = left.shape[1], 256
+    rank = left.shape[1]
     tiles = cols // 128 + 1
-    whole = lambda shape: pl.BlockSpec(shape, lambda i: (0,) * len(shape))
+    steps = 4
+    in_vmem = pl.BlockSpec(memory_space=pltpu.VMEM)
+    in_hbm = pl.BlockSpec(memory_space=pltpu.HBM)
     return pl.pallas_call(
         functools.partial(target_kernel, replicas),
-        grid=(rows // wide,),
         in_specs=[
             pl.BlockSpec(memory_space=pltpu.SMEM),
-            pl.BlockSpec((acts.shape[0], wide), lambda i: (0, i)),
-            whole(mine.shape),
-            whole(other.shape),
-            pl.BlockSpec((wide, cols), lambda i: (i, 0)),
-            whole(left.shape),
-        ],
-        out_specs=[
-            pl.BlockSpec((wide, cols), lambda i: (i, 0)),
-            whole((2 * tiles, rank // 2, 128)),
-        ],
+            in_hbm,
+            in_vmem,
+            in_hbm,
+            in_hbm,
+            in_vmem,
+        ],
+        out_specs=[in_hbm, in_vmem],
         out_shape=[
             jax.ShapeDtypeStruct((rows, cols), jnp.float32),
             jax.ShapeDtypeStruct((2 * tiles, rank // 2, 128), jnp.float32),
         ],
-        scratch_shapes=[pltpu.VMEM((rank, tiles * 128), jnp.float32)],
-        compiler_params=pltpu.CompilerParams(vmem_limit_bytes=24 * 2**20),
+        scratch_shapes=[
+            pltpu.VMEM(acts.shape, acts.dtype),
+            pltpu.VMEM(other.shape, other.dtype),
+            pltpu.VMEM(err.shape, err.dtype),
+            pltpu.VMEM(err.shape, err.dtype),
+            pltpu.SemaphoreType.DMA((steps,)),
+            pltpu.SemaphoreType.DMA((steps,)),
+            pltpu.SemaphoreType.DMA((steps + 1,)),
+        ],
+        compiler_params=pltpu.CompilerParams(vmem_limit_bytes=56 * 2**20),
     )(col.reshape(1), acts, mine, other, err, left)
 
 
@@ -134,12 +202,14 @@
         joint = jnp.concatenate(halves, axis=0)
         system = jnp.concatenate([joint, lanes(left_ref, 0, left_ref.shape[0])], axis=1)
         row_of = lax.broadcasted_iota(jnp.int32, (rank, 1), 0)
-        for k in range(rank):
+        for k in range(rank - 1):
             column = system[:, cols + k : cols + k + 1]
-            pivot = jnp.sqrt(column[k : k + 1])
-            row = system[k : k + 1] / pivot
-            factor = jnp.where(row_of > k, column / pivot, 0.0)
-            system = jnp.where(row_of == k, row, system - factor * row)
+            factor = jnp.where(row_of > k, column / column[k : k + 1], 0.0)
+            system = system - factor * system[k : k + 1]
+        square = system[:, cols : cols + 128]
+        diagonal = lax.broadcasted_iota(jnp.int32, square.shape, 1) == row_of
+        pivots = jnp.sum(jnp.where(diagonal, square, 0.0), axis=1, keepdims=True)
+        system = system / jnp.sqrt(pivots)
         right = system[:, :cols] / replicas
         right_ref[...] = right
         first, second, third = thirds(right)
@@ -191,22 +261,21 @@
         other = lax.ppermute(grads, "col", [(0, 1), (1, 0)])
 
     with jax.named_scope("left_terms"):
-        proj = dot(right_t, grads.astype(jnp.float32), ((1,), (1,)))
-        per = n_row // n_col
-        chunks = jnp.moveaxis(proj.reshape(rank, per, tokens), 1, 0)
-        empty = jnp.zeros_like(chunks)
-        halves = jnp.stack([jnp.where(col == i, chunks, empty) for i in range(n_col)])
-        sends = jnp.broadcast_to(
-            halves.reshape(n_row, 1, rank, tokens), (n_row, n_col, rank, tokens)
-        ).reshape(n_row * n_col, rank, tokens)
-        mine = split_and_summed(sends, ("row", "col"))
-        left_t = dot(mine, acts.astype(jnp.float32), ((1,), (0,)))
-        left_t = left_t + dot(right_t, err, ((1,), (1,)))
+        sends = local_call(
+            functools.partial(projection_kernel, n_col),
+            (n_row * n_col, rank, tokens),
+            col.reshape(1),
+            right_t,
+            grads,
+            scalars=1,
+        )
+        mine = lax.all_to_all(sends, ("row", "col"), split_axis=0, concat_axis=0, tiled=True)
+        part = local_call(error_kernel, (rank, rows), right_t, err)
+        blocks = local_call(left_kernel, (n_near, rank, rows // n_near), mine, acts, part)
 
     with jax.named_scope("left_sum"):
-        wide = rows // n_near
-        blocks = jnp.moveaxis(left_t.reshape(rank, n_near, wide), 1, 0)
         part = split_and_summed(blocks, NEAR)
+        part, other = lax.optimization_barrier((part, other))
         part = summed_over(part, "y")
         part = summed_over(part, "row")
         left = to_all(part, NEAR)

time: 159 us -> 165 us (1.038)
  starting transfers between devices: 15.6 us -> 25.4 us
  blocking collectives: 104 us -> 98.6 us
  Pallas kernels: 6.88 us -> 12 us
  matrix products: 3.92 us -> 0 us
    all_to_all x3 -> x2, blocking collectives: 44.8 us -> 19.5 us  [split_and_summed(): lax.all_to_all(blocks, axes, split_axis=0, concat_axis=0, tiled=True)]
    all_to_all x3 -> x5, blocking collectives: 59.7 us -> 79.1 us  [to_all(): return lax.all_to_all(copies, axes, split_axis=0, concat_axis=0, tiled=True)]
    all_to_all x2 -> x1, waiting for transfers between devices: 8.19 us -> 0.01 us  [body(): lax.all_to_all(sends, ('row', 'col'), split_axis=0, concat_axis=0, tiled=...]
    ppermute x1, waiting for transfers between devices: 0.01 us -> 7.92 us  [body(): other = lax.ppermute(grads, 'col', [(0, 1), (1, 0)])]
    ppermute x1, starting transfers between devices: 3.56 us -> 9.64 us  [body(): other = lax.ppermute(grads, 'col', [(0, 1), (1, 0)])]
    pallas_call x1 -> x4, Pallas kernels: 3.11 us -> 8.47 us  [the longest x1 6.68 us: target_and_terms(): pl.pallas_call(functools.partial(target_kernel, replicas), in_specs=[pl.B...]
    dot_general x3 -> x0, matrix products: 3.92 us -> none  [dot(): lax.dot_general(a, b, (dims, ((), ())), precision=precision, preferred_el...]
    all_to_all x2 -> x1, starting transfers between devices: 12 us -> 15.7 us  [body(): lax.all_to_all(sends, ('row', 'col'), split_axis=0, concat_axis=0, tiled=...]
  transfers between devices with their start and end apart: 4 -> 3, of which waited for: 2 -> 1; matrix products, arithmetic and copies ran while one was open for 3% -> 0% of each run, Pallas kernels for 0% -> 1%
where the time goes in v3:
time: 165 us; the launch traced here: 164 us
  blocking collectives  98.6 us (60%)
  starting transfers between devices  25.4 us (15%)
  between operations  14.1 us (9%)
  Pallas kernels  12 us (7%)
  waiting for transfers between devices  8.61 us (5%)
  local copies, waits for them, and re-layouts  5.38 us (3%)
    all_to_all x5, blocking collectives, to_all(): return lax.all_to_all(copies, axes, split_axis=0, concat_axis=0, tiled=True)  79.1 us
    all_to_all x2, blocking collectives, split_and_summed(): lax.all_to_all(blocks, axes, split_axis=0, concat_axis=0, tiled=True)  19.5 us
    all_to_all x1, starting transfers between devices, body(): lax.all_to_all(sends, ('row', 'col'), split_axis=0, concat_axis=0, tiled=...  15.7 us
    ppermute x1, starting transfers between devices, body(): other = lax.ppermute(grads, 'col', [(0, 1), (1, 0)])  9.64 us
    ppermute x1, waiting for transfers between devices, body(): other = lax.ppermute(grads, 'col', [(0, 1), (1, 0)])  7.92 us
    pallas_call x1, Pallas kernels, target_and_terms(): pl.pallas_call(functools.partial(target_kernel, replicas), in_specs=[pl.B...  6.68 us
    unnamed x16, local copies, waits for them, and re-layouts  5.35 us
    pallas_call x1, Pallas kernels, finish(): pl.pallas_call(functools.partial(finish_kernel, replicas), grid=(rows //...  3.57 us
  transfers between devices with their start and end apart: 3, of which 1 were waited for; matrix products, arithmetic and copies ran while one was open for 0% of the time, Pallas kernels for 1%

profile of v3, /device:TPU:1, one launch (start us, length us, event | category | flops | bytes accessed | tf_op | source)
XLA Modules:
  0.0 164.2 jit_solution(16410301136855637976)
XLA Ops:
  7.2 0.0 all-gather.2.cloned.1.call-start
  7.2 0.7 all-gather.2.cloned.1.call-update
  7.9 1.0 copy-done.2
  8.9 0.7 copy-done.5
  9.6 0.9 left_terms.3
  10.5 15.7 %all-to-all-start = ((f32[12,16,128]{2,1,0:T(8,128)}), f32[12,16,128]{2,1,0:T(8,128)S(1)}, u32[]{:S(2)}, u32[]{:S(2)}) async-start(f32[12,16,128]{2,1,0:T(8,128)} %left_terms.3), calls=%async_computation | async-start | bytes 196608 | tf_op jit(solution)/shard_map/left_terms/all_to_all | solution.py:272
  26.2 9.6 %collective-permute-start = (bf16[384,384]{1,0:T(8,128)(2,1)}, bf16[384,384]{1,0:T(8,128)(2,1)S(1)}, u32[]{:S(2)}, u32[]{:S(2)}) collective-permute-start(bf16[384,384]{1,0:T(8,128)(2,1)} %mine_ref.1), channel_id=1, source_target_pairs={{0,1},{1,0},{2,3},{3,2},{4,5},{5,4},{6,7},{7,6},{8,9},{9,8},{10,11... | collective-permute-start | bytes 884744 | tf_op jit(solution)/shard_map/gather_inputs/ppermute | solution.py:261
  35.8 0.0 copy-start
  35.9 1.5 copy-done
  37.3 0.7 copy-done.6
  38.1 0.8 left_terms.4.part_ref
  38.9 0.0 copy-done.3
  38.9 0.2 left_terms.5
  39.0 10.8 %all_to_all.40 = f32[8,16,128]{2,1,0:T(8,128)S(1)} all-to-all(f32[8,16,128]{2,1,0:T(8,128)S(1)} %left_terms.5), channel_id=1, replica_groups=mesh['y'=8,'x'=4,'core'=2,'row'=6,'col'=2] {'x','core'}, dimensions={0} | all-to-all | bytes 131072 | tf_op jit(solution)/shard_map/left_sum/all_to_all | solution.py:25
  49.8 7.9 %collective-permute-done.other_ref = bf16[384,384]{1,0:T(8,128)(2,1)S(1)} collective-permute-done((bf16[384,384]{1,0:T(8,128)(2,1)}, bf16[384,384]{1,0:T(8,128)(2,1)S(1)}, u32[]{:S(2)}, u32[]{:S(2)}) %collective-permute-start) | collective-permute-done | bytes 294944 | tf_op jit(solution)/shard_map/gather_inputs/ppermute | solution.py:261
  57.8 14.3 %all_to_all.41 = f32[8,16,128]{2,1,0:T(8,128)S(1)} all-to-all(f32[8,16,128]{2,1,0:T(8,128)S(1)} %broadcast_in_dim.15), channel_id=1, replica_groups=mesh['y'=8,'x'=4,'core'=2,'row'=6,'col'=2] {'y'}, dimensions={0} | all-to-all | bytes 131072 | tf_op jit(solution)/shard_map/left_sum/all_to_all | solution.py:17
  72.1 17.8 %all_to_all.42 = f32[6,16,128]{2,1,0:T(8,128)S(1)} all-to-all(f32[6,16,128]{2,1,0:T(8,128)S(1)} %broadcast_in_dim.16), channel_id=1, replica_groups=mesh['y'=8,'x'=4,'core'=2,'row'=6,'col'=2] {'row'}, dimensions={0} | all-to-all | bytes 98304 | tf_op jit(solution)/shard_map/left_sum/all_to_all | solution.py:17
  89.9 15.9 %all_to_all.43.left_ref = f32[8,16,128]{2,1,0:T(8,128)} all-to-all(f32[8,16,128]{2,1,0:T(8,128)S(1)} %broadcast_in_dim.17), channel_id=1, replica_groups=mesh['y'=8,'x'=4,'core'=2,'row'=6,'col'=2] {'x','core'}, dimensions={0} | all-to-all | bytes 131072 | tf_op jit(solution)/shard_map/left_sum/all_to_all | solution.py:17
  105.8 6.7 %target.1 = (f32[1024,384]{1,0:T(8,128)}, f32[8,8,128]{2,1,0:T(8,128)}) custom-call(s32[1]{0:T(128)} %bitcast.col_ref, bf16[768,1024]{1,0:T(8,128)(2,1)} %all-gather.2.cloned.1.call-done.acts_ref, bf16[384,384]{1,0:T(8,128)(2,1)} %mine_ref.1, bf16[384,384]{1,0:T(8,128)(2,1)} %copy-done.7, f32[1024,384]{1,0:T(8,128)} %err_ref.3, ...), custom_call_target="tpu_custom_call" | custom-call | tf_op jit(solution)/shard_map/target/pallas_call | solution.py:164
  112.5 8.7 %all_to_all.44 = f32[8,8,128]{2,1,0:T(8,128)S(1)} all-to-all(f32[8,8,128]{2,1,0:T(8,128)} %get-tuple-element.10), channel_id=1, replica_groups=mesh['y'=8,'x'=4,'core'=2,'row'=6,'col'=2] {'x','core'}, dimensions={0} | all-to-all | bytes 65536 | tf_op jit(solution)/shard_map/right_sum/all_to_all | solution.py:25
  121.2 21.8 %all_to_all.45 = f32[16,8,128]{2,1,0:T(8,128)S(1)} all-to-all(f32[16,8,128]{2,1,0:T(8,128)S(1)} %broadcast_in_dim.18), channel_id=1, replica_groups=mesh['y'=8,'x'=4,'core'=2,'row'=6,'col'=2] {'y','col'}, dimensions={0} | all-to-all | bytes 131072 | tf_op jit(solution)/shard_map/right_sum/all_to_all | solution.py:17
  143.1 9.2 %all_to_all.46.joint_ref = f32[8,8,128]{2,1,0:T(8,128)S(1)} all-to-all(f32[8,8,128]{2,1,0:T(8,128)S(1)} %broadcast_in_dim.19), channel_id=1, replica_groups=mesh['y'=8,'x'=4,'core'=2,'row'=6,'col'=2] {'x','core'}, dimensions={0} | all-to-all | bytes 65536 | tf_op jit(solution)/shard_map/right_sum/all_to_all | solution.py:17
  152.4 1.4 copy-done.1
  153.8 3.6 %finish.1 = (f32[1024,384]{1,0:T(8,128)}, f32[16,384]{1,0:T(8,128)}) custom-call(f32[8,8,128]{2,1,0:T(8,128)S(1)} %all_to_all.46.joint_ref, f32[8,16,128]{2,1,0:T(8,128)S(1)} %copy-done.4, f32[1024,384]{1,0:T(8,128)S(1)} %copy-done.1), custom_call_target="tpu_custom_call" | custom-call | tf_op jit(solution)/shard_map/finish/pallas_call | solution.py:229
  (21 shorter events, 0.1 us)
Async XLA Ops:
  7.2 31.7 %copy-start.3 = (bf16[128,1024]{1,0:T(8,128)(2,1)S(1)}, bf16[128,1024]{1,0:T(8,128)(2,1)}, u32[]{:S(2)}) copy-start(bf16[128,1024]{1,0:T(8,128)(2,1)} %acts_ref.1) | copy-start | bytes 786436
  7.2 98.6 %all-gather.2.cloned.1.call-start = ((), (), s32[]{:S(2)}) async-start(), calls=%async_computation.8 | async-start | bytes 1835008 | tf_op jit(solution)/shard_map/gather_inputs/all_gather | solution.py:260
  7.9 1.0 copy-start.2
  8.9 0.7 copy-start.5
  10.5 28.4 %all-to-all-start = ((f32[12,16,128]{2,1,0:T(8,128)}), f32[12,16,128]{2,1,0:T(8,128)S(1)}, u32[]{:S(2)}, u32[]{:S(2)}) async-start(f32[12,16,128]{2,1,0:T(8,128)} %left_terms.3), calls=%async_computation | async-start | bytes 196608 | tf_op jit(solution)/shard_map/left_terms/all_to_all | solution.py:272
  26.2 31.5 %collective-permute-start = (bf16[384,384]{1,0:T(8,128)(2,1)}, bf16[384,384]{1,0:T(8,128)(2,1)S(1)}, u32[]{:S(2)}, u32[]{:S(2)}) collective-permute-start(bf16[384,384]{1,0:T(8,128)(2,1)} %mine_ref.1), channel_id=1, source_target_pairs={{0,1},{1,0},{2,3},{3,2},{4,5},{5,4},{6,7},{7,6},{8,9},{9,8},{10,11... | collective-permute-start | bytes 884744 | tf_op jit(solution)/shard_map/gather_inputs/ppermute | solution.py:261
  35.8 1.5 copy-start
  37.3 0.7 copy-start.6
  57.7 48.1 %copy-start.7 = (bf16[384,384]{1,0:T(8,128)(2,1)}, bf16[384,384]{1,0:T(8,128)(2,1)S(1)}, u32[]{:S(2)}) copy-start(bf16[384,384]{1,0:T(8,128)(2,1)S(1)} %collective-permute-done.other_ref) | copy-start | bytes 884740
  105.8 46.6 %copy-start.4 = (f32[8,16,128]{2,1,0:T(8,128)S(1)}, f32[8,16,128]{2,1,0:T(8,128)}, u32[]{:S(2)}) copy-start(f32[8,16,128]{2,1,0:T(8,128)} %all_to_all.43.left_ref) | copy-start | bytes 196612
  152.4 1.4 copy-start.1
Sparse Core Ops, SparseCore 0:
  10.4 74.8 all-gather.1

commit v4 on v3

v4 whole, which is shorter than its diff:
```python
import functools

import jax
import jax.numpy as jnp
from jax import lax
from jax.experimental import pallas as pl
from jax.experimental.pallas import tpu as pltpu
from jax.sharding import Mesh, PartitionSpec as P

REP = ("y", "x", "core")
NEAR = ("x", "core")
HIGHEST = lax.Precision.HIGHEST


def to_all(block, axes):
    copies = jnp.broadcast_to(block, (lax.axis_size(axes), *block.shape))
    return lax.all_to_all(copies, axes, split_axis=0, concat_axis=0, tiled=True)


def summed_over(block, axes):
    return jnp.sum(to_all(block, axes), axis=0)


def split_and_summed(blocks, axes):
    return jnp.sum(lax.all_to_all(blocks, axes, split_axis=0, concat_axis=0, tiled=True), axis=0)


def dot(a, b, dims, precision=HIGHEST):
    return lax.dot_general(
        a, b, (dims, ((), ())), precision=precision, preferred_element_type=jnp.float32
    )


def thirds(x):
    first = x.astype(jnp.bfloat16)
    rest = x - first.astype(jnp.float32)
    second = rest.astype(jnp.bfloat16)
    third = (rest - second.astype(jnp.float32)).astype(jnp.bfloat16)
    return first, second, third


def mxu(a, b, contract):
    return lax.dot_general(a, b, (contract, ((), ())), preferred_element_type=jnp.float32)


def lanes(ref, start, count):
    return jnp.concatenate([ref[start + k] for k in range(count)], axis=1)


def joined(terms, rank):
    return terms[:rank] + terms[rank : 2 * rank] + terms[2 * rank :]


def projection_kernel(n_col, col_ref, right_ref, grads_ref, sends_ref):
    rank = right_ref.shape[0]
    per = sends_ref.shape[0] // n_col // n_col
    wide = sends_ref.shape[2]
    stack = jnp.concatenate(thirds(right_ref[...]), axis=0)
    proj = joined(mxu(stack, grads_ref[...], ((1,), (1,))), rank)
    for k in range(sends_ref.shape[0]):
        owner = k // n_col
        at = owner % per * wide
        keep = (col_ref[0] == owner // per).astype(jnp.float32)
        sends_ref[k] = proj[:, at : at + wide] * keep


def error_kernel(right_ref, err_ref, out_ref):
    rank = right_ref.shape[0]
    stack = jnp.concatenate(thirds(right_ref[...]), axis=0)
    wide = 256
    for k in range(err_ref.shape[0] // wide):
        high, mid, low = thirds(err_ref[k * wide : (k + 1) * wide])
        terms = joined(mxu(stack, high, ((1,), (1,))) + mxu(stack, mid, ((1,), (1,))), rank)
        out_ref[:, k * wide : (k + 1) * wide] = terms + mxu(stack[:rank], low, ((1,), (1,)))


def left_kernel(mine_ref, acts_ref, part_ref, out_ref):
    rank = mine_ref.shape[1]
    mine = mine_ref[0]
    for k in range(1, mine_ref.shape[0]):
        mine += mine_ref[k]
    stack = jnp.concatenate(thirds(mine), axis=0)
    left = joined(mxu(stack, acts_ref[...], ((1,), (0,))), rank) + part_ref[...]
    wide = out_ref.shape[2]
    for k in range(out_ref.shape[0]):
        out_ref[k] = left[:, k * wide : (k + 1) * wide]


def local_call(kernel, out_shape, *args, scalars=0, limit=16):
    return pl.pallas_call(
        kernel,
        in_specs=[pl.BlockSpec(memory_space=pltpu.SMEM)] * scalars
        + [pl.BlockSpec(memory_space=pltpu.VMEM)] * (len(args) - scalars),
        out_specs=pl.BlockSpec(memory_space=pltpu.VMEM),
        out_shape=jax.ShapeDtypeStruct(out_shape, jnp.float32),
        compiler_params=pltpu.CompilerParams(vmem_limit_bytes=limit * 2**20),
    )(*args)


def target_kernel(replicas, n_acts, col_ref, *refs):
    acts_refs, refs = refs[:n_acts], refs[n_acts:]
    mine_ref, other_ref, err_ref, left_ref, target_ref, joint_ref = refs
    half = mine_ref.shape[0]
    rank = left_ref.shape[1]
    wide = 256
    mine_at = pl.multiple_of(col_ref[0] * half, half)
    other_at = pl.multiple_of((1 - col_ref[0]) * half, half)
    left = lanes(left_ref, 0, left_ref.shape[0])
    stack = jnp.concatenate(thirds(left), axis=0)
    gram = lax.dot_general(
        left,
        left,
        (((1,), (1,)), ((), ())),
        precision=HIGHEST,
        preferred_element_type=jnp.float32,
    )
    sums = None
    for k in range(err_ref.shape[0] // wide):
        span = slice(k * wide, (k + 1) * wide)
        acts_ref = acts_refs[k * wide // acts_refs[0].shape[1]]
        at = k * wide % acts_ref.shape[1]
        tile = mxu(acts_ref[pl.ds(mine_at, half), at : at + wide], mine_ref[...], ((0,), (0,)))
        tile += mxu(acts_ref[pl.ds(other_at, half), at : at + wide], other_ref[...], ((0,), (0,)))
        tile += err_ref[span]
        target_ref[span] = tile
        high, mid, low = thirds(tile)
        terms = mxu(stack[:, span], high, ((1,), (0,))) + mxu(stack[:, span], mid, ((1,), (0,)))
        right = joined(terms, rank) + mxu(stack[:rank, span], low, ((1,), (0,)))
        sums = right if sums is None else sums + right
    gram = jnp.concatenate([gram, jnp.zeros((rank, 128 - rank), jnp.float32)], axis=1) / replicas
    both = jnp.concatenate([sums, gram], axis=1)
    for k in range(joint_ref.shape[0]):
        first, at = (k % 2) * (rank // 2), (k // 2) * 128
        joint_ref[k] = both[first : first + rank // 2, at : at + 128]


def target_and_terms(acts, mine, other, err, left, col, replicas):
    rows, cols = err.shape
    rank = left.shape[1]
    tiles = cols // 128 + 1
    in_vmem = pl.BlockSpec(memory_space=pltpu.VMEM)
    return pl.pallas_call(
        functools.partial(target_kernel, replicas, len(acts)),
        in_specs=[pl.BlockSpec(memory_space=pltpu.SMEM)] + [in_vmem] * (4 + len(acts)),
        out_specs=[in_vmem, in_vmem],
        out_shape=[
            jax.ShapeDtypeStruct((rows, cols), jnp.float32),
            jax.ShapeDtypeStruct((2 * tiles, rank // 2, 128), jnp.float32),
        ],
        compiler_params=pltpu.CompilerParams(vmem_limit_bytes=24 * 2**20),
    )(col.reshape(1), *acts, mine, other, err, left)


def finish_kernel(replicas, joint_ref, left_ref, target_ref, error_ref, right_ref, error, sems):
    rank, cols = right_ref.shape
    halves = [
        jnp.concatenate([joint_ref[2 * c + h] for c in range(joint_ref.shape[0] // 2)], axis=1)
        for h in range(2)
    ]
    joint = jnp.concatenate(halves, axis=0)
    system = jnp.concatenate([joint, lanes(left_ref, 0, left_ref.shape[0])], axis=1)
    row_of = lax.broadcasted_iota(jnp.int32, (rank, 1), 0)
    for k in range(rank - 1):
        column = system[:, cols + k : cols + k + 1]
        factor = jnp.where(row_of > k, column / column[k : k + 1], 0.0)
        system = system - factor * system[k : k + 1]
    square = system[:, cols : cols + 128]
    diagonal = lax.broadcasted_iota(jnp.int32, square.shape, 1) == row_of
    pivots = jnp.sum(jnp.where(diagonal, square, 0.0), axis=1, keepdims=True)
    system = system / jnp.sqrt(pivots)
    right = system[:, :cols] / replicas
    right_ref[...] = right
    first, second, third = thirds(right)
    rights = jnp.concatenate([first, second, first, second, third, first], axis=0)
    first, second, third = thirds(system[:, cols + 128 :])
    orths = jnp.concatenate([first, first, second, second, first, third], axis=0)
    wide = target_ref.shape[0] // sems.shape[0]
    copies = []
    for k in range(sems.shape[0]):
        span = slice(k * wide, (k + 1) * wide)
        error[span] = target_ref[span] - mxu(orths[:, span], rights, ((0,), (0,)))
        copies.append(pltpu.make_async_copy(error.at[span], error_ref.at[span], sems.at[k]))
        copies[-1].start()
    for copy in copies:
        copy.wait()


def finish(joint, left, target, replicas):
    rows, cols = target.shape
    rank = left.shape[1]
    in_vmem = pl.BlockSpec(memory_space=pltpu.VMEM)
    return pl.pallas_call(
        functools.partial(finish_kernel, replicas),
        in_specs=[in_vmem] * 3,
        out_specs=[pl.BlockSpec(memory_space=pl.ANY), in_vmem],
        out_shape=[
            jax.ShapeDtypeStruct((rows, cols), jnp.float32),
            jax.ShapeDtypeStruct((rank, cols), jnp.float32),
        ],
        scratch_shapes=[
            pltpu.VMEM((rows, cols), jnp.float32),
            pltpu.SemaphoreType.DMA((4,)),
        ],
        compiler_params=pltpu.CompilerParams(vmem_limit_bytes=24 * 2**20),
    )(joint, left, target)


def body(acts, grads, err, right):
    rank = right.shape[1]
    rows = err.shape[0]
    n_row, n_col, n_near = lax.axis_size("row"), lax.axis_size("col"), lax.axis_size(NEAR)
    col = lax.axis_index("col")
    replicas = lax.axis_size(REP)
    tokens = acts.shape[0]
    right_t = right.T

    with jax.named_scope("gather_inputs"):
        all_acts = [lax.all_gather(acts, "row", axis=0, tiled=True)]
        other = lax.ppermute(grads, "col", [(0, 1), (1, 0)])

    with jax.named_scope("left_terms"):
        sends = local_call(
            functools.partial(projection_kernel, n_col),
            (n_row * n_col, rank, tokens),
            col.reshape(1),
            right_t,
            grads,
            scalars=1,
            limit=56,
        )
        mine = lax.all_to_all(sends, ("row", "col"), split_axis=0, concat_axis=0, tiled=True)
        part = local_call(error_kernel, (rank, rows), right_t, err, limit=56)
        blocks = local_call(left_kernel, (n_near, rank, rows // n_near), mine, acts, part)

    with jax.named_scope("left_sum"):
        part = split_and_summed(blocks, NEAR)
        part = summed_over(part, "y")
        part = summed_over(part, "row")
        part, other = lax.optimization_barrier((part, other))
        left = to_all(part, NEAR)

    with jax.named_scope("target"):
        target, joint = target_and_terms(all_acts, grads, other, err, left, col, replicas)

    with jax.named_scope("right_sum"):
        part = split_and_summed(joint, NEAR)
        part = summed_over(part, ("y", "col"))
        joint = to_all(part, NEAR)

    with jax.named_scope("finish"):
        new_error, new_right_t = finish(joint, left, target, replicas)
    return new_error, new_right_t.T


def solution(mesh):
    rep, row, col = (mesh.shape[name] for name in ("rep", "row", "col"))
    fine = Mesh(mesh.devices.reshape(rep // 8, 4, 2, row, col), ("y", "x", "core", "row", "col"))
    return jax.shard_map(
        body,
        mesh=fine,
        in_specs=(
            P((*REP, "row"), "col"),
            P((*REP, "col"), "row"),
            P((*REP, "col"), "row"),
            P("row", None),
        ),
        out_specs=(P((*REP, "col"), "row"), P("row", None)),
        check_vma=False,
    )
```

time: 165 us -> 154 us (0.933)
  blocking collectives: 98.6 us -> 89 us
    all_to_all x2 -> x1, blocking collectives: 19.5 us -> 7.85 us  [split_and_summed(): lax.all_to_all(blocks, axes, split_axis=0, concat_axis=0, tiled=True)]
    ppermute x1, waiting for transfers between devices: 7.92 us -> 0.01 us  [body(): other = lax.ppermute(grads, 'col', [(0, 1), (1, 0)])]
    all_to_all x0 -> x1, starting transfers between devices: none -> 6.83 us  [split_and_summed(): lax.all_to_all(blocks, axes, split_axis=0, concat_axis=0, tiled=True)]
    all_to_all x1, waiting for transfers between devices: 0.01 us -> 6.46 us  [body(): lax.all_to_all(sends, ('row', 'col'), split_axis=0, concat_axis=0, tiled=...]
    ppermute x1, starting transfers between devices: 9.64 us -> 3.55 us  [body(): other = lax.ppermute(grads, 'col', [(0, 1), (1, 0)])]
    pallas_call x2, Pallas kernels: 10.2 us -> 5.46 us  [the longest x1 3.31 us: finish(): pl.pallas_call(functools.partial(finish_kernel, replicas), in_specs=[in_v...]
    pallas_call x3, Pallas kernels: 1.79 us -> 5.61 us  [local_call(): pl.pallas_call(kernel, in_specs=[pl.BlockSpec(memory_space=pltpu.SMEM)] *...]
    all_to_all x5, blocking collectives: 79.1 us -> 81.2 us  [to_all(): return lax.all_to_all(copies, axes, split_axis=0, concat_axis=0, tiled=True)]
  transfers between devices with their start and end apart: 3 -> 4, of which waited for: 1 -> 2; matrix products, arithmetic and copies ran while one was open for 0% -> 0% of each run, Pallas kernels for 1% -> 4%
where the time goes in v4:
time: 154 us; the launch traced here: 153 us
  blocking collectives  89 us (58%)
  starting transfers between devices  26.1 us (17%)
  between operations  14.1 us (9%)
  Pallas kernels  11.1 us (7%)
  waiting for transfers between devices  8.83 us (6%)
  local copies, waits for them, and re-layouts  3.97 us (3%)
    all_to_all x5, blocking collectives, to_all(): return lax.all_to_all(copies, axes, split_axis=0, concat_axis=0, tiled=True)  81.2 us
    all_to_all x1, starting transfers between devices, body(): lax.all_to_all(sends, ('row', 'col'), split_axis=0, concat_axis=0, tiled=...  15.7 us
    all_to_all x1, blocking collectives, split_and_summed(): lax.all_to_all(blocks, axes, split_axis=0, concat_axis=0, tiled=True)  7.85 us
    all_to_all x1, starting transfers between devices, split_and_summed(): lax.all_to_all(blocks, axes, split_axis=0, concat_axis=0, tiled=True)  6.83 us
    all_to_all x1, waiting for transfers between devices, body(): lax.all_to_all(sends, ('row', 'col'), split_axis=0, concat_axis=0, tiled=...  6.46 us
    pallas_call x3, Pallas kernels, local_call(): pl.pallas_call(kernel, in_specs=[pl.BlockSpec(memory_space=pltpu.SMEM)] *...  5.61 us
    unnamed x14, local copies, waits for them, and re-layouts  3.94 us
    ppermute x1, starting transfers between devices, body(): other = lax.ppermute(grads, 'col', [(0, 1), (1, 0)])  3.55 us
  transfers between devices with their start and end apart: 4, of which 2 were waited for; matrix products, arithmetic and copies ran while one was open for 0% of the time, Pallas kernels for 4%

profile of v4, /device:TPU:1, one launch (start us, length us, event | category | flops | bytes accessed | tf_op | source)
XLA Modules:
  0.0 153.2 jit_solution(5360887831037667062)
XLA Ops:
  7.2 0.0 all-gather.2.cloned.1.call-start
  7.2 0.7 all-gather.2.cloned.1.call-update
  7.9 1.9 %left_terms.3 = f32[12,16,128]{2,1,0:T(8,128)} custom-call(s32[1]{0:T(128)} %bitcast.col_ref, f32[16,384]{1,0:T(8,128)} %bitcast.3, bf16[384,384]{1,0:T(8,128)(2,1)} %refs_1_.1), custom_call_target="tpu_custom_call" | custom-call | tf_op jit(solution)/shard_map/left_terms/pallas_call | solution.py:90
  9.8 15.7 %all-to-all-start = ((f32[12,16,128]{2,1,0:T(8,128)}), f32[12,16,128]{2,1,0:T(8,128)S(1)}, u32[]{:S(2)}, u32[]{:S(2)}) async-start(f32[12,16,128]{2,1,0:T(8,128)} %left_terms.3), calls=%async_computation | async-start | bytes 196608 | tf_op jit(solution)/shard_map/left_terms/all_to_all | solution.py:231
  25.5 0.0 copy-start
  25.5 2.9 %left_terms.4.part_ref = f32[16,1024]{1,0:T(8,128)} custom-call(f32[16,384]{1,0:T(8,128)} %bitcast.4, f32[1024,384]{1,0:T(8,128)} %refs_3_.1), custom_call_target="tpu_custom_call" | custom-call | tf_op jit(solution)/shard_map/left_terms/pallas_call | solution.py:90
  28.5 6.5 %all-to-all-done.mine_ref = f32[12,16,128]{2,1,0:T(8,128)S(1)} async-done(((f32[12,16,128]{2,1,0:T(8,128)}), f32[12,16,128]{2,1,0:T(8,128)S(1)}, u32[]{:S(2)}, u32[]{:S(2)}) %all-to-all-start) | async-done | bytes 98336 | tf_op jit(solution)/shard_map/left_terms/all_to_all | solution.py:231
  34.9 0.8 copy-done.6
  35.8 0.8 left_terms.5
  36.6 6.8 %all-to-all-start.1 = ((f32[8,16,128]{2,1,0:T(8,128)}), f32[8,16,128]{2,1,0:T(8,128)S(1)}, u32[]{:S(2)}, u32[]{:S(2)}) async-start(f32[8,16,128]{2,1,0:T(8,128)} %left_terms.5), calls=%async_computation.1 | async-start | bytes 131072 | tf_op jit(solution)/shard_map/left_sum/all_to_all | solution.py:25
  43.4 3.5 %collective-permute-start = (bf16[384,384]{1,0:T(8,128)(2,1)S(1)}, bf16[384,384]{1,0:T(8,128)(2,1)S(1)}, u32[]{:S(2)}, u32[]{:S(2)}) collective-permute-start(bf16[384,384]{1,0:T(8,128)(2,1)S(1)} %copy-done.2), channel_id=1, source_target_pairs={{0,1},{1,0},{2,3},{3,2},{4,5},{5,4},{6,7},{7,6},{8,9},{9,8},{10,11... | collective-permute-start | bytes 884744 | tf_op jit(solution)/shard_map/gather_inputs/ppermute | solution.py:219
  47.0 1.7 %all-to-all-done.1 = f32[8,16,128]{2,1,0:T(8,128)S(1)} async-done(((f32[8,16,128]{2,1,0:T(8,128)}), f32[8,16,128]{2,1,0:T(8,128)S(1)}, u32[]{:S(2)}, u32[]{:S(2)}) %all-to-all-start.1) | async-done | bytes 65568 | tf_op jit(solution)/shard_map/left_sum/all_to_all | solution.py:25
  48.7 14.2 %all_to_all.40 = f32[8,16,128]{2,1,0:T(8,128)S(1)} all-to-all(f32[8,16,128]{2,1,0:T(8,128)S(1)} %broadcast_in_dim.15), channel_id=1, replica_groups=mesh['y'=8,'x'=4,'core'=2,'row'=6,'col'=2] {'y'}, dimensions={0} | all-to-all | bytes 131072 | tf_op jit(solution)/shard_map/left_sum/all_to_all | solution.py:17
  63.0 23.1 %all_to_all.41 = f32[6,16,128]{2,1,0:T(8,128)S(1)} all-to-all(f32[6,16,128]{2,1,0:T(8,128)S(1)} %broadcast_in_dim.16), channel_id=1, replica_groups=mesh['y'=8,'x'=4,'core'=2,'row'=6,'col'=2] {'row'}, dimensions={0} | all-to-all | bytes 98304 | tf_op jit(solution)/shard_map/left_sum/all_to_all | solution.py:17
  86.0 0.0 copy-start.4
  86.1 0.7 copy-done.4
  86.8 9.5 %all_to_all.42.refs_4_.left_ref = f32[8,16,128]{2,1,0:T(8,128)S(1)} all-to-all(f32[8,16,128]{2,1,0:T(8,128)S(1)} %broadcast_in_dim.17), channel_id=1, replica_groups=mesh['y'=8,'x'=4,'core'=2,'row'=6,'col'=2] {'x','core'}, dimensions={0} | all-to-all | bytes 131072 | tf_op jit(solution)/shard_map/left_sum/all_to_all | solution.py:17
  96.3 1.4 copy-done.1
  97.7 1.0 copy-done.5
  98.6 2.2 %target.1 = (f32[1024,384]{1,0:T(8,128)S(1)}, f32[8,8,128]{2,1,0:T(8,128)S(1)}) custom-call(s32[1]{0:T(128)} %bitcast.col_ref, bf16[768,1024]{1,0:T(8,128)(2,1)S(1)} %copy-done.1, bf16[384,384]{1,0:T(8,128)(2,1)S(1)} %copy-done.2, bf16[384,384]{1,0:T(8,128)(2,1)S(1)} %copy-done.5, f32[1024,384]{1,0:T(8,128)S(1)} %copy-done, ...), custom_call_target="tpu_custom_call" | custom-call | tf_op jit(solution)/shard_map/target/pallas_call | solution.py:142
  100.8 7.9 %all_to_all.43 = f32[8,8,128]{2,1,0:T(8,128)S(1)} all-to-all(f32[8,8,128]{2,1,0:T(8,128)S(1)} %get-tuple-element.10), channel_id=1, replica_groups=mesh['y'=8,'x'=4,'core'=2,'row'=6,'col'=2] {'x','core'}, dimensions={0} | all-to-all | bytes 65536 | tf_op jit(solution)/shard_map/right_sum/all_to_all | solution.py:25
  108.7 25.1 %all_to_all.44 = f32[16,8,128]{2,1,0:T(8,128)S(1)} all-to-all(f32[16,8,128]{2,1,0:T(8,128)S(1)} %broadcast_in_dim.18), channel_id=1, replica_groups=mesh['y'=8,'x'=4,'core'=2,'row'=6,'col'=2] {'y','col'}, dimensions={0} | all-to-all | bytes 131072 | tf_op jit(solution)/shard_map/right_sum/all_to_all | solution.py:17
  133.8 9.2 %all_to_all.45.joint_ref = f32[8,8,128]{2,1,0:T(8,128)S(1)} all-to-all(f32[8,8,128]{2,1,0:T(8,128)S(1)} %broadcast_in_dim.19), channel_id=1, replica_groups=mesh['y'=8,'x'=4,'core'=2,'row'=6,'col'=2] {'x','core'}, dimensions={0} | all-to-all | bytes 65536 | tf_op jit(solution)/shard_map/right_sum/all_to_all | solution.py:17
  143.1 3.3 %finish.1 = (f32[1024,384]{1,0:T(8,128)}, f32[16,384]{1,0:T(8,128)}) custom-call(f32[8,8,128]{2,1,0:T(8,128)S(1)} %all_to_all.45.joint_ref, f32[8,16,128]{2,1,0:T(8,128)S(1)} %all_to_all.42.refs_4_.left_ref, f32[1024,384]{1,0:T(8,128)S(1)} %get-tuple-element.11.target_ref), custom_call_target="tpu_custom_call" | custom-call | tf_op jit(solution)/shard_map/finish/pallas_call | solution.py:192
  (20 shorter events, 0.1 us)
Async XLA Ops:
  7.2 27.8 %copy-start.3 = (bf16[128,1024]{1,0:T(8,128)(2,1)S(1)}, bf16[128,1024]{1,0:T(8,128)(2,1)}, u32[]{:S(2)}) copy-start(bf16[128,1024]{1,0:T(8,128)(2,1)} %acts_ref.1) | copy-start | bytes 786436
  7.2 36.2 %copy-start.2 = (bf16[384,384]{1,0:T(8,128)(2,1)S(1)}, bf16[384,384]{1,0:T(8,128)(2,1)}, u32[]{:S(2)}) copy-start(bf16[384,384]{1,0:T(8,128)(2,1)} %refs_1_.1) | copy-start | bytes 884740
  7.2 89.1 %all-gather.2.cloned.1.call-start = ((), (), s32[]{:S(2)}) async-start(), calls=%async_computation.8 | async-start | bytes 1835008 | tf_op jit(solution)/shard_map/gather_inputs/all_gather | solution.py:218
  9.8 25.1 %all-to-all-start = ((f32[12,16,128]{2,1,0:T(8,128)}), f32[12,16,128]{2,1,0:T(8,128)S(1)}, u32[]{:S(2)}, u32[]{:S(2)}) async-start(f32[12,16,128]{2,1,0:T(8,128)} %left_terms.3), calls=%async_computation | async-start | bytes 196608 | tf_op jit(solution)/shard_map/left_terms/all_to_all | solution.py:231
  25.5 70.7 %copy-start = (f32[1024,384]{1,0:T(8,128)S(1)}, f32[1024,384]{1,0:T(8,128)}, u32[]{:S(2)}) copy-start(f32[1024,384]{1,0:T(8,128)} %refs_3_.1) | copy-start | bytes 4718596
  34.9 0.8 copy-start.6
  36.6 12.1 %all-to-all-start.1 = ((f32[8,16,128]{2,1,0:T(8,128)}), f32[8,16,128]{2,1,0:T(8,128)S(1)}, u32[]{:S(2)}, u32[]{:S(2)}) async-start(f32[8,16,128]{2,1,0:T(8,128)} %left_terms.5), calls=%async_computation.1 | async-start | bytes 131072 | tf_op jit(solution)/shard_map/left_sum/all_to_all | solution.py:25
  43.4 42.6 %collective-permute-start = (bf16[384,384]{1,0:T(8,128)(2,1)S(1)}, bf16[384,384]{1,0:T(8,128)(2,1)S(1)}, u32[]{:S(2)}, u32[]{:S(2)}) collective-permute-start(bf16[384,384]{1,0:T(8,128)(2,1)S(1)} %copy-done.2), channel_id=1, source_target_pairs={{0,1},{1,0},{2,3},{3,2},{4,5},{5,4},{6,7},{7,6},{8,9},{9,8},{10,11... | collective-permute-start | bytes 884744 | tf_op jit(solution)/shard_map/gather_inputs/ppermute | solution.py:219
  86.0 0.7 copy-start.4
  96.2 1.4 copy-start.1
  97.7 1.0 copy-start.5
Sparse Core Ops, SparseCore 0:
  10.4 81.1 all-gather.1

commit v5 on v4

--- a/solution.py
+++ b/solution.py
@@ -97,14 +97,19 @@
     )(*args)
 
 
-def target_kernel(replicas, n_acts, col_ref, *refs):
-    acts_refs, refs = refs[:n_acts], refs[n_acts:]
-    mine_ref, other_ref, err_ref, left_ref, target_ref, joint_ref = refs
-    half = mine_ref.shape[0]
+def target_kernel(
+    replicas, order, col_ref, acts_ref, mine_ref, other_ref, err_ref, left_ref,
+    target_ref, joint_ref, grads,
+):
     rank = left_ref.shape[1]
     wide = 256
-    mine_at = pl.multiple_of(col_ref[0] * half, half)
-    other_at = pl.multiple_of((1 - col_ref[0]) * half, half)
+    half = mine_ref.shape[0]
+    per = len(order) // 2
+    chunk = half // per
+    for k, place in enumerate(order):
+        source = slice(place % per * chunk, place % per * chunk + chunk)
+        is_mine = col_ref[0] == place // per
+        grads[k * chunk : (k + 1) * chunk] = jnp.where(is_mine, mine_ref[source], other_ref[source])
     left = lanes(left_ref, 0, left_ref.shape[0])
     stack = jnp.concatenate(thirds(left), axis=0)
     gram = lax.dot_general(
@@ -117,11 +122,7 @@
     sums = None
     for k in range(err_ref.shape[0] // wide):
         span = slice(k * wide, (k + 1) * wide)
-        acts_ref = acts_refs[k * wide // acts_refs[0].shape[1]]
-        at = k * wide % acts_ref.shape[1]
-        tile = mxu(acts_ref[pl.ds(mine_at, half), at : at + wide], mine_ref[...], ((0,), (0,)))
-        tile += mxu(acts_ref[pl.ds(other_at, half), at : at + wide], other_ref[...], ((0,), (0,)))
-        tile += err_ref[span]
+        tile = mxu(acts_ref[:, span], grads[...], ((0,), (0,))) + err_ref[span]
         target_ref[span] = tile
         high, mid, low = thirds(tile)
         terms = mxu(stack[:, span], high, ((1,), (0,))) + mxu(stack[:, span], mid, ((1,), (0,)))
@@ -134,21 +135,22 @@
         joint_ref[k] = both[first : first + rank // 2, at : at + 128]
 
 
-def target_and_terms(acts, mine, other, err, left, col, replicas):
+def target_and_terms(acts, mine, other, err, left, col, replicas, order):
     rows, cols = err.shape
     rank = left.shape[1]
     tiles = cols // 128 + 1
     in_vmem = pl.BlockSpec(memory_space=pltpu.VMEM)
     return pl.pallas_call(
-        functools.partial(target_kernel, replicas, len(acts)),
-        in_specs=[pl.BlockSpec(memory_space=pltpu.SMEM)] + [in_vmem] * (4 + len(acts)),
+        functools.partial(target_kernel, replicas, order),
+        in_specs=[pl.BlockSpec(memory_space=pltpu.SMEM)] + [in_vmem] * 5,
         out_specs=[in_vmem, in_vmem],
         out_shape=[
             jax.ShapeDtypeStruct((rows, cols), jnp.float32),
             jax.ShapeDtypeStruct((2 * tiles, rank // 2, 128), jnp.float32),
         ],
+        scratch_shapes=[pltpu.VMEM((2 * mine.shape[0], cols), mine.dtype)],
         compiler_params=pltpu.CompilerParams(vmem_limit_bytes=24 * 2**20),
-    )(col.reshape(1), *acts, mine, other, err, left)
+    )(col.reshape(1), acts, mine, other, err, left)
 
 
 def finish_kernel(replicas, joint_ref, left_ref, target_ref, error_ref, right_ref, error, sems):
@@ -215,7 +217,8 @@
     right_t = right.T
 
     with jax.named_scope("gather_inputs"):
-        all_acts = [lax.all_gather(acts, "row", axis=0, tiled=True)]
+        order = [*range(0, n_row, 2), *reversed(range(1, n_row, 2))]
+        all_acts = lax.all_gather(acts, "row", axis=0, tiled=True, axis_index_groups=[order])
         other = lax.ppermute(grads, "col", [(0, 1), (1, 0)])
 
     with jax.named_scope("left_terms"):
@@ -240,7 +243,9 @@
         left = to_all(part, NEAR)
 
     with jax.named_scope("target"):
-        target, joint = target_and_terms(all_acts, grads, other, err, left, col, replicas)
+        target, joint = target_and_terms(
+            all_acts, grads, other, err, left, col, replicas, order
+        )
 
     with jax.named_scope("right_sum"):
         part = split_and_summed(joint, NEAR)

time: 154 us -> 152 us (0.987)
  no operation moved by 1% of the time
where the time goes in v5:
time: 152 us
  blocking collectives  88.1 us (58%)
  starting transfers between devices  26.1 us (17%)
  between operations  14.2 us (9%)
  Pallas kernels  10.9 us (7%)
  waiting for transfers between devices  8.43 us (6%)
  local copies, waits for them, and re-layouts  3.97 us (3%)
    all_to_all x5, blocking collectives, to_all(): return lax.all_to_all(copies, axes, split_axis=0, concat_axis=0, tiled=True)  80.2 us
    all_to_all x1, starting transfers between devices, body(): lax.all_to_all(sends, ('row', 'col'), split_axis=0, concat_axis=0, tiled=...  15.7 us
    all_to_all x1, blocking collectives, split_and_summed(): lax.all_to_all(blocks, axes, split_axis=0, concat_axis=0, tiled=True)  7.86 us
    all_to_all x1, starting transfers between devices, split_and_summed(): lax.all_to_all(blocks, axes, split_axis=0, concat_axis=0, tiled=True)  6.83 us
    all_to_all x1, waiting for transfers between devices, body(): lax.all_to_all(sends, ('row', 'col'), split_axis=0, concat_axis=0, tiled=...  6.46 us
    pallas_call x3, Pallas kernels, local_call(): pl.pallas_call(kernel, in_specs=[pl.BlockSpec(memory_space=pltpu.SMEM)] *...  5.61 us
    unnamed x14, local copies, waits for them, and re-layouts  3.94 us
    ppermute x1, starting transfers between devices, body(): other = lax.ppermute(grads, 'col', [(0, 1), (1, 0)])  3.55 us
  transfers between devices with their start and end apart: 4, of which 2 were waited for; matrix products, arithmetic and copies ran while one was open for 0% of the time, Pallas kernels for 4%

profile of v5, /device:TPU:1, one launch (start us, length us, event | category | flops | bytes accessed | tf_op | source)
XLA Modules:
  0.0 151.7 jit_solution(9958959657217223139)
XLA Ops:
  7.2 0.0 all-gather.2.cloned.1.call-start
  7.2 0.7 all-gather.2.cloned.1.call-update
  7.9 1.9 %left_terms.3 = f32[12,16,128]{2,1,0:T(8,128)} custom-call(s32[1]{0:T(128)} %bitcast.col_ref, f32[16,384]{1,0:T(8,128)} %bitcast.3, bf16[384,384]{1,0:T(8,128)(2,1)} %mine_ref.1), custom_call_target="tpu_custom_call" | custom-call | tf_op jit(solution)/shard_map/left_terms/pallas_call | solution.py:90
  9.8 15.7 %all-to-all-start = ((f32[12,16,128]{2,1,0:T(8,128)}), f32[12,16,128]{2,1,0:T(8,128)S(1)}, u32[]{:S(2)}, u32[]{:S(2)}) async-start(f32[12,16,128]{2,1,0:T(8,128)} %left_terms.3), calls=%async_computation | async-start | bytes 196608 | tf_op jit(solution)/shard_map/left_terms/all_to_all | solution.py:234
  25.5 0.0 copy-start
  25.5 2.9 %left_terms.4.part_ref = f32[16,1024]{1,0:T(8,128)} custom-call(f32[16,384]{1,0:T(8,128)} %bitcast.4, f32[1024,384]{1,0:T(8,128)} %err_ref.3), custom_call_target="tpu_custom_call" | custom-call | tf_op jit(solution)/shard_map/left_terms/pallas_call | solution.py:90
  28.5 6.5 %all-to-all-done.mine_ref = f32[12,16,128]{2,1,0:T(8,128)S(1)} async-done(((f32[12,16,128]{2,1,0:T(8,128)}), f32[12,16,128]{2,1,0:T(8,128)S(1)}, u32[]{:S(2)}, u32[]{:S(2)}) %all-to-all-start) | async-done | bytes 98336 | tf_op jit(solution)/shard_map/left_terms/all_to_all | solution.py:234
  34.9 0.8 copy-done.6
  35.8 0.8 left_terms.5
  36.6 6.8 %all-to-all-start.1 = ((f32[8,16,128]{2,1,0:T(8,128)}), f32[8,16,128]{2,1,0:T(8,128)S(1)}, u32[]{:S(2)}, u32[]{:S(2)}) async-start(f32[8,16,128]{2,1,0:T(8,128)} %left_terms.5), calls=%async_computation.1 | async-start | bytes 131072 | tf_op jit(solution)/shard_map/left_sum/all_to_all | solution.py:25
  43.4 3.5 %collective-permute-start = (bf16[384,384]{1,0:T(8,128)(2,1)S(1)}, bf16[384,384]{1,0:T(8,128)(2,1)S(1)}, u32[]{:S(2)}, u32[]{:S(2)}) collective-permute-start(bf16[384,384]{1,0:T(8,128)(2,1)S(1)} %copy-done.2), channel_id=1, source_target_pairs={{0,1},{1,0},{2,3},{3,2},{4,5},{5,4},{6,7},{7,6},{8,9},{9,8},{10,11... | collective-permute-start | bytes 884744 | tf_op jit(solution)/shard_map/gather_inputs/ppermute | solution.py:222
  47.0 1.3 all-to-all-done.1
  48.3 14.1 %all_to_all.40 = f32[8,16,128]{2,1,0:T(8,128)S(1)} all-to-all(f32[8,16,128]{2,1,0:T(8,128)S(1)} %broadcast_in_dim.15), channel_id=1, replica_groups=mesh['y'=8,'x'=4,'core'=2,'row'=6,'col'=2] {'y'}, dimensions={0} | all-to-all | bytes 131072 | tf_op jit(solution)/shard_map/left_sum/all_to_all | solution.py:17
  62.5 21.1 %all_to_all.41 = f32[6,16,128]{2,1,0:T(8,128)S(1)} all-to-all(f32[6,16,128]{2,1,0:T(8,128)S(1)} %broadcast_in_dim.16), channel_id=1, replica_groups=mesh['y'=8,'x'=4,'core'=2,'row'=6,'col'=2] {'row'}, dimensions={0} | all-to-all | bytes 98304 | tf_op jit(solution)/shard_map/left_sum/all_to_all | solution.py:17
  83.6 0.0 copy-start.4
  83.6 0.7 copy-done.4
  84.3 10.5 %all_to_all.42.left_ref = f32[8,16,128]{2,1,0:T(8,128)S(1)} all-to-all(f32[8,16,128]{2,1,0:T(8,128)S(1)} %broadcast_in_dim.17), channel_id=1, replica_groups=mesh['y'=8,'x'=4,'core'=2,'row'=6,'col'=2] {'x','core'}, dimensions={0} | all-to-all | bytes 131072 | tf_op jit(solution)/shard_map/left_sum/all_to_all | solution.py:17
  94.9 1.4 copy-done.1
  96.3 1.0 copy-done.5
  97.2 2.0 %target.1 = (f32[1024,384]{1,0:T(8,128)S(1)}, f32[8,8,128]{2,1,0:T(8,128)S(1)}) custom-call(s32[1]{0:T(128)} %bitcast.col_ref, bf16[768,1024]{1,0:T(8,128)(2,1)S(1)} %copy-done.1, bf16[384,384]{1,0:T(8,128)(2,1)S(1)} %copy-done.2, bf16[384,384]{1,0:T(8,128)(2,1)S(1)} %copy-done.5, f32[1024,384]{1,0:T(8,128)S(1)} %copy-done, ...), custom_call_target="tpu_custom_call" | custom-call | tf_op jit(solution)/shard_map/target/pallas_call | solution.py:143
  99.2 7.9 %all_to_all.43 = f32[8,8,128]{2,1,0:T(8,128)S(1)} all-to-all(f32[8,8,128]{2,1,0:T(8,128)S(1)} %get-tuple-element.10), channel_id=1, replica_groups=mesh['y'=8,'x'=4,'core'=2,'row'=6,'col'=2] {'x','core'}, dimensions={0} | all-to-all | bytes 65536 | tf_op jit(solution)/shard_map/right_sum/all_to_all | solution.py:25
  107.1 25.2 %all_to_all.44 = f32[16,8,128]{2,1,0:T(8,128)S(1)} all-to-all(f32[16,8,128]{2,1,0:T(8,128)S(1)} %broadcast_in_dim.18), channel_id=1, replica_groups=mesh['y'=8,'x'=4,'core'=2,'row'=6,'col'=2] {'y','col'}, dimensions={0} | all-to-all | bytes 131072 | tf_op jit(solution)/shard_map/right_sum/all_to_all | solution.py:17
  132.3 9.2 %all_to_all.45.joint_ref = f32[8,8,128]{2,1,0:T(8,128)S(1)} all-to-all(f32[8,8,128]{2,1,0:T(8,128)S(1)} %broadcast_in_dim.19), channel_id=1, replica_groups=mesh['y'=8,'x'=4,'core'=2,'row'=6,'col'=2] {'x','core'}, dimensions={0} | all-to-all | bytes 65536 | tf_op jit(solution)/shard_map/right_sum/all_to_all | solution.py:17
  141.5 3.3 %finish.1 = (f32[1024,384]{1,0:T(8,128)}, f32[16,384]{1,0:T(8,128)}) custom-call(f32[8,8,128]{2,1,0:T(8,128)S(1)} %all_to_all.45.joint_ref, f32[8,16,128]{2,1,0:T(8,128)S(1)} %all_to_all.42.left_ref, f32[1024,384]{1,0:T(8,128)S(1)} %get-tuple-element.11.target_ref), custom_call_target="tpu_custom_call" | custom-call | tf_op jit(solution)/shard_map/finish/pallas_call | solution.py:194
  (20 shorter events, 0.1 us)
Async XLA Ops:
  7.2 27.8 %copy-start.3 = (bf16[128,1024]{1,0:T(8,128)(2,1)S(1)}, bf16[128,1024]{1,0:T(8,128)(2,1)}, u32[]{:S(2)}) copy-start(bf16[128,1024]{1,0:T(8,128)(2,1)} %acts_ref.1) | copy-start | bytes 786436
  7.2 36.2 %copy-start.2 = (bf16[384,384]{1,0:T(8,128)(2,1)S(1)}, bf16[384,384]{1,0:T(8,128)(2,1)}, u32[]{:S(2)}) copy-start(bf16[384,384]{1,0:T(8,128)(2,1)} %mine_ref.1) | copy-start | bytes 884740
  7.2 87.7 %all-gather.2.cloned.1.call-start = ((), (), s32[]{:S(2)}) async-start(), calls=%async_computation.8 | async-start | bytes 1835008 | tf_op jit(solution)/shard_map/gather_inputs/all_gather | solution.py:221
  9.8 25.1 %all-to-all-start = ((f32[12,16,128]{2,1,0:T(8,128)}), f32[12,16,128]{2,1,0:T(8,128)S(1)}, u32[]{:S(2)}, u32[]{:S(2)}) async-start(f32[12,16,128]{2,1,0:T(8,128)} %left_terms.3), calls=%async_computation | async-start | bytes 196608 | tf_op jit(solution)/shard_map/left_terms/all_to_all | solution.py:234
  25.5 69.3 %copy-start = (f32[1024,384]{1,0:T(8,128)S(1)}, f32[1024,384]{1,0:T(8,128)}, u32[]{:S(2)}) copy-start(f32[1024,384]{1,0:T(8,128)} %err_ref.3) | copy-start | bytes 4718596
  34.9 0.8 copy-start.6
  36.6 11.7 %all-to-all-start.1 = ((f32[8,16,128]{2,1,0:T(8,128)}), f32[8,16,128]{2,1,0:T(8,128)S(1)}, u32[]{:S(2)}, u32[]{:S(2)}) async-start(f32[8,16,128]{2,1,0:T(8,128)} %left_terms.5), calls=%async_computation.1 | async-start | bytes 131072 | tf_op jit(solution)/shard_map/left_sum/all_to_all | solution.py:25
  43.4 40.2 %collective-permute-start = (bf16[384,384]{1,0:T(8,128)(2,1)S(1)}, bf16[384,384]{1,0:T(8,128)(2,1)S(1)}, u32[]{:S(2)}, u32[]{:S(2)}) collective-permute-start(bf16[384,384]{1,0:T(8,128)(2,1)S(1)} %copy-done.2), channel_id=1, source_target_pairs={{0,1},{1,0},{2,3},{3,2},{4,5},{5,4},{6,7},{7,6},{8,9},{9,8},{10,11... | collective-permute-start | bytes 884744 | tf_op jit(solution)/shard_map/gather_inputs/ppermute | solution.py:222
  83.6 0.7 copy-start.4
  94.9 1.4 copy-start.1
  96.3 1.0 copy-start.5
Sparse Core Ops, SparseCore 0:
  10.4 78.5 all-gather.1

commit v6 on v5

--- a/solution.py
+++ b/solution.py
@@ -9,6 +9,7 @@
 
 REP = ("y", "x", "core")
 NEAR = ("x", "core")
+ROW = ("far", "next")
 HIGHEST = lax.Precision.HIGHEST
 
 
@@ -98,18 +99,17 @@
 
 
 def target_kernel(
-    replicas, order, col_ref, acts_ref, mine_ref, other_ref, err_ref, left_ref,
+    replicas, chunk, same_ref, acts_ref, mine_ref, other_ref, err_ref, left_ref,
     target_ref, joint_ref, grads,
 ):
     rank = left_ref.shape[1]
     wide = 256
-    half = mine_ref.shape[0]
-    per = len(order) // 2
-    chunk = half // per
-    for k, place in enumerate(order):
-        source = slice(place % per * chunk, place % per * chunk + chunk)
-        is_mine = col_ref[0] == place // per
-        grads[k * chunk : (k + 1) * chunk] = jnp.where(is_mine, mine_ref[source], other_ref[source])
+    same = same_ref[0] == 1
+    for k in range(mine_ref.shape[0] // chunk):
+        source = slice(k * chunk, (k + 1) * chunk)
+        mine, other = mine_ref[source], other_ref[source]
+        grads[2 * k * chunk : (2 * k + 1) * chunk] = jnp.where(same, mine, other)
+        grads[(2 * k + 1) * chunk : (2 * k + 2) * chunk] = jnp.where(same, other, mine)
     left = lanes(left_ref, 0, left_ref.shape[0])
     stack = jnp.concatenate(thirds(left), axis=0)
     gram = lax.dot_general(
@@ -135,13 +135,13 @@
         joint_ref[k] = both[first : first + rank // 2, at : at + 128]
 
 
-def target_and_terms(acts, mine, other, err, left, col, replicas, order):
+def target_and_terms(acts, mine, other, err, left, same, replicas, chunk):
     rows, cols = err.shape
     rank = left.shape[1]
     tiles = cols // 128 + 1
     in_vmem = pl.BlockSpec(memory_space=pltpu.VMEM)
     return pl.pallas_call(
-        functools.partial(target_kernel, replicas, order),
+        functools.partial(target_kernel, replicas, chunk),
         in_specs=[pl.BlockSpec(memory_space=pltpu.SMEM)] + [in_vmem] * 5,
         out_specs=[in_vmem, in_vmem],
         out_shape=[
@@ -149,8 +149,8 @@
             jax.ShapeDtypeStruct((2 * tiles, rank // 2, 128), jnp.float32),
         ],
         scratch_shapes=[pltpu.VMEM((2 * mine.shape[0], cols), mine.dtype)],
-        compiler_params=pltpu.CompilerParams(vmem_limit_bytes=24 * 2**20),
-    )(col.reshape(1), acts, mine, other, err, left)
+        compiler_params=pltpu.CompilerParams(vmem_limit_bytes=16 * 2**20),
+    )(same.astype(jnp.int32).reshape(1), acts, mine, other, err, left)
 
 
 def finish_kernel(replicas, joint_ref, left_ref, target_ref, error_ref, right_ref, error, sems):
@@ -203,22 +203,22 @@
             pltpu.VMEM((rows, cols), jnp.float32),
             pltpu.SemaphoreType.DMA((4,)),
         ],
-        compiler_params=pltpu.CompilerParams(vmem_limit_bytes=24 * 2**20),
+        compiler_params=pltpu.CompilerParams(vmem_limit_bytes=16 * 2**20),
     )(joint, left, target)
 
 
 def body(acts, grads, err, right):
     rank = right.shape[1]
     rows = err.shape[0]
-    n_row, n_col, n_near = lax.axis_size("row"), lax.axis_size("col"), lax.axis_size(NEAR)
+    n_row, n_col, n_near = lax.axis_size(ROW), lax.axis_size("col"), lax.axis_size(NEAR)
     col = lax.axis_index("col")
     replicas = lax.axis_size(REP)
     tokens = acts.shape[0]
     right_t = right.T
 
     with jax.named_scope("gather_inputs"):
-        order = [*range(0, n_row, 2), *reversed(range(1, n_row, 2))]
-        all_acts = lax.all_gather(acts, "row", axis=0, tiled=True, axis_index_groups=[order])
+        swapped = lax.ppermute(acts, "far", [(0, 1), (1, 0)])
+        pair = jnp.concatenate([acts, swapped], axis=0)
         other = lax.ppermute(grads, "col", [(0, 1), (1, 0)])
 
     with jax.named_scope("left_terms"):
@@ -231,20 +231,22 @@
             scalars=1,
             limit=56,
         )
-        mine = lax.all_to_all(sends, ("row", "col"), split_axis=0, concat_axis=0, tiled=True)
-        part = local_call(error_kernel, (rank, rows), right_t, err, limit=56)
+        mine = lax.all_to_all(sends, (*ROW, "col"), split_axis=0, concat_axis=0, tiled=True)
+        part = local_call(error_kernel, (rank, rows), right_t, err)
         blocks = local_call(left_kernel, (n_near, rank, rows // n_near), mine, acts, part)
 
     with jax.named_scope("left_sum"):
+        blocks, pair = lax.optimization_barrier((blocks, pair))
+        all_acts = lax.all_gather(pair, "next", axis=0, tiled=True)
         part = split_and_summed(blocks, NEAR)
         part = summed_over(part, "y")
-        part = summed_over(part, "row")
+        part = summed_over(part, ROW)
         part, other = lax.optimization_barrier((part, other))
         left = to_all(part, NEAR)
 
     with jax.named_scope("target"):
         target, joint = target_and_terms(
-            all_acts, grads, other, err, left, col, replicas, order
+            all_acts, grads, other, err, left, col == lax.axis_index("far"), replicas, tokens
         )
 
     with jax.named_scope("right_sum"):
@@ -259,16 +261,19 @@
 
 def solution(mesh):
     rep, row, col = (mesh.shape[name] for name in ("rep", "row", "col"))
-    fine = Mesh(mesh.devices.reshape(rep // 8, 4, 2, row, col), ("y", "x", "core", "row", "col"))
+    fine = Mesh(
+        mesh.devices.reshape(rep // 8, 4, 2, 2, row // 2, col),
+        ("y", "x", "core", "far", "next", "col"),
+    )
     return jax.shard_map(
         body,
         mesh=fine,
         in_specs=(
-            P((*REP, "row"), "col"),
-            P((*REP, "col"), "row"),
-            P((*REP, "col"), "row"),
-            P("row", None),
+            P((*REP, *ROW), "col"),
+            P((*REP, "col"), ROW),
+            P((*REP, "col"), ROW),
+            P(ROW, None),
         ),
-        out_specs=(P((*REP, "col"), "row"), P("row", None)),
+        out_specs=(P((*REP, "col"), ROW), P(ROW, None)),
         check_vma=False,
     )

time: 152 us -> 162 us (1.066)
  blocking collectives: 88.1 us -> 72.9 us
  starting transfers between devices: 26.1 us -> 38.8 us
  waiting for transfers between devices: 8.43 us -> 19.6 us
  Pallas kernels: 10.9 us -> 8.66 us
  local copies, waits for them, and re-layouts: 3.97 us -> 5.88 us
    all_to_all x5 -> x4, blocking collectives: 80.2 us -> 63.5 us  [to_all(): return lax.all_to_all(copies, axes, split_axis=0, concat_axis=0, tiled=True)]
    all_to_all x1 -> x2, waiting for transfers between devices: 6.46 us -> 16.2 us  [the longest x1 11.4 us: body(): lax.all_to_all(sends, (*ROW, 'col'), split_axis=0, concat_axis=0, tiled=T...]
    ppermute x0 -> x1, starting transfers between devices: none -> 8.58 us  [body(): swapped = lax.ppermute(acts, 'far', [(0, 1), (1, 0)])]
    all_to_all x1 -> x2, starting transfers between devices: 15.7 us -> 19.4 us  [the longest x1 12.2 us: body(): lax.all_to_all(sends, (*ROW, 'col'), split_axis=0, concat_axis=0, tiled=T...]
    pallas_call x3, Pallas kernels: 5.61 us -> 3.41 us  [local_call(): pl.pallas_call(kernel, in_specs=[pl.BlockSpec(memory_space=pltpu.SMEM)] *...]
    unnamed x14 -> x16, local copies, waits for them, and re-layouts: 3.94 us -> 5.22 us
  transfers between devices with their start and end apart: 4 -> 6, of which waited for: 2 -> 5; matrix products, arithmetic and copies ran while one was open for 0% -> 1% of each run, Pallas kernels for 4% -> 2%
where the time goes in v6:
time: 162 us; the launch traced here: 161 us
  blocking collectives  72.9 us (45%)
  starting transfers between devices  38.8 us (24%)
  waiting for transfers between devices  19.6 us (12%)
  between operations  14.2 us (9%)
  Pallas kernels  8.66 us (5%)
  local copies, waits for them, and re-layouts  5.88 us (4%)
    all_to_all x4, blocking collectives, to_all(): return lax.all_to_all(copies, axes, split_axis=0, concat_axis=0, tiled=True)  63.5 us
    all_to_all x1, starting transfers between devices, body(): lax.all_to_all(sends, (*ROW, 'col'), split_axis=0, concat_axis=0, tiled=T...  12.2 us
    all_to_all x1, waiting for transfers between devices, body(): lax.all_to_all(sends, (*ROW, 'col'), split_axis=0, concat_axis=0, tiled=T...  11.4 us
    all_to_all x1, blocking collectives, split_and_summed(): lax.all_to_all(blocks, axes, split_axis=0, concat_axis=0, tiled=True)  9.45 us
    ppermute x1, starting transfers between devices, body(): swapped = lax.ppermute(acts, 'far', [(0, 1), (1, 0)])  8.58 us
    all_to_all x1, starting transfers between devices, to_all(): return lax.all_to_all(copies, axes, split_axis=0, concat_axis=0, tiled=True)  7.21 us
    all_to_all x1, starting transfers between devices, split_and_summed(): lax.all_to_all(blocks, axes, split_axis=0, concat_axis=0, tiled=True)  6.39 us
    unnamed x16, local copies, waits for them, and re-layouts  5.22 us
  transfers between devices with their start and end apart: 6, of which 5 were waited for; matrix products, arithmetic and copies ran while one was open for 1% of the time, Pallas kernels for 2%

profile of v6, /device:TPU:1, one launch (start us, length us, event | category | flops | bytes accessed | tf_op | source)
XLA Modules:
  0.0 160.9 jit_solution(5805832463011030435)
XLA Ops:
  7.2 8.6 %collective-permute-start = (bf16[128,1024]{1,0:T(8,128)(2,1)}, bf16[128,1024]{1,0:T(8,128)(2,1)S(1)}, u32[]{:S(2)}, u32[]{:S(2)}) collective-permute-start(bf16[128,1024]{1,0:T(8,128)(2,1)} %acts_ref.1), channel_id=1, source_target_pairs={{0,6},{6,0},{1,7},{7,1},{2,8},{8,2},{3,9},{9,3},{4,10},{10,4},{5,1... | collective-permute-start | bytes 786440 | tf_op jit(solution)/shard_map/gather_inputs/ppermute | solution.py:220
  15.8 1.9 %left_terms.3 = f32[12,16,128]{2,1,0:T(8,128)} custom-call(s32[1]{0:T(128)} %bitcast.1.col_ref, f32[16,384]{1,0:T(8,128)} %bitcast.4, bf16[384,384]{1,0:T(8,128)(2,1)} %mine_ref.1), custom_call_target="tpu_custom_call" | custom-call | tf_op jit(solution)/shard_map/left_terms/pallas_call | solution.py:91
  17.6 12.2 %all-to-all-start = ((f32[12,16,128]{2,1,0:T(8,128)}), f32[12,16,128]{2,1,0:T(8,128)S(1)}, u32[]{:S(2)}, u32[]{:S(2)}) async-start(f32[12,16,128]{2,1,0:T(8,128)} %left_terms.3), calls=%async_computation | async-start | bytes 196608 | tf_op jit(solution)/shard_map/left_terms/all_to_all | solution.py:234
  29.9 1.4 copy-done
  31.3 0.7 copy-done.7
  32.0 0.8 left_terms.4.part_ref
  32.8 0.8 pad_maximum_fusion
  33.6 11.4 %all-to-all-done.mine_ref = f32[12,16,128]{2,1,0:T(8,128)S(1)} async-done(((f32[12,16,128]{2,1,0:T(8,128)}), f32[12,16,128]{2,1,0:T(8,128)S(1)}, u32[]{:S(2)}, u32[]{:S(2)}) %all-to-all-start) | async-done | bytes 98336 | tf_op jit(solution)/shard_map/left_terms/all_to_all | solution.py:234
  45.0 0.8 left_terms.5
  45.8 6.4 %all-to-all-start.1 = ((f32[8,16,128]{2,1,0:T(8,128)}), f32[8,16,128]{2,1,0:T(8,128)S(1)}, u32[]{:S(2)}, u32[]{:S(2)}) async-start(f32[8,16,128]{2,1,0:T(8,128)} %left_terms.5), calls=%async_computation.1 | async-start | bytes 131072 | tf_op jit(solution)/shard_map/left_sum/all_to_all | solution.py:26
  52.2 4.4 %collective-permute-start.1 = (bf16[384,384]{1,0:T(8,128)(2,1)S(1)}, bf16[384,384]{1,0:T(8,128)(2,1)S(1)}, u32[]{:S(2)}, u32[]{:S(2)}) collective-permute-start(bf16[384,384]{1,0:T(8,128)(2,1)S(1)} %copy-done.3), channel_id=1, source_target_pairs={{0,1},{1,0},{2,3},{3,2},{4,5},{5,4},{6,7},{7,6},{8,9},{9,8},{10,11... | collective-permute-start | bytes 884744 | tf_op jit(solution)/shard_map/gather_inputs/ppermute | solution.py:222
  57.1 14.1 %all_to_all.40 = f32[8,16,128]{2,1,0:T(8,128)S(1)} all-to-all(f32[8,16,128]{2,1,0:T(8,128)S(1)} %broadcast_in_dim.15), channel_id=1, replica_groups=mesh['y'=8,'x'=4,'core'=2,'far'=2,'next'=3,'col'=2] {'y'}, dimensions={0} | all-to-all | bytes 131072 | tf_op jit(solution)/shard_map/left_sum/all_to_all | solution.py:18
  71.3 13.4 %all_to_all.41 = f32[6,16,128]{2,1,0:T(8,128)S(1)} all-to-all(f32[6,16,128]{2,1,0:T(8,128)S(1)} %broadcast_in_dim.16), channel_id=1, replica_groups=mesh['y'=8,'x'=4,'core'=2,'far'=2,'next'=3,'col'=2] {'far','next'}, dimensions={0} | all-to-all | bytes 98304 | tf_op jit(solution)/shard_map/left_sum/all_to_all | solution.py:18
  84.7 1.6 collective-permute-done.1.other_ref
  87.6 7.2 %all-to-all-start.4 = ((f32[8,16,128]{2,1,0:T(8,128)}), f32[8,16,128]{2,1,0:T(8,128)S(1)}, u32[]{:S(2)}, u32[]{:S(2)}) async-start(f32[8,16,128]{2,1,0:T(8,128)} %broadcast_in_dim.17), calls=%async_computation.4 | async-start | bytes 131072 | tf_op jit(solution)/shard_map/left_sum/all_to_all | solution.py:18
  94.9 4.9 %all-to-all-done.4.left_ref = f32[8,16,128]{2,1,0:T(8,128)S(1)} async-done(((f32[8,16,128]{2,1,0:T(8,128)}), f32[8,16,128]{2,1,0:T(8,128)S(1)}, u32[]{:S(2)}, u32[]{:S(2)}) %all-to-all-start.4) | async-done | bytes 65568 | tf_op jit(solution)/shard_map/left_sum/all_to_all | solution.py:18
  99.7 1.4 all-gather.2.cloned.1.call-done.acts_ref
  101.1 1.4 copy-done.2
  102.5 1.0 copy-done.6
  103.4 1.9 %target.1 = (f32[1024,384]{1,0:T(8,128)S(1)}, f32[8,8,128]{2,1,0:T(8,128)S(1)}) custom-call(s32[1]{0:T(128)} %bitcast.same_ref, bf16[768,1024]{1,0:T(8,128)(2,1)S(1)} %copy-done.2, bf16[384,384]{1,0:T(8,128)(2,1)S(1)} %copy-done.3, bf16[384,384]{1,0:T(8,128)(2,1)S(1)} %copy-done.6, f32[1024,384]{1,0:T(8,128)S(1)} %copy-done.1, ...), custom_call_target="tpu_custom_call" | custom-call | tf_op jit(solution)/shard_map/target/pallas_call | solution.py:143
  105.4 9.5 %all_to_all.42 = f32[8,8,128]{2,1,0:T(8,128)S(1)} all-to-all(f32[8,8,128]{2,1,0:T(8,128)S(1)} %get-tuple-element.14), channel_id=1, replica_groups=mesh['y'=8,'x'=4,'core'=2,'far'=2,'next'=3,'col'=2] {'x','core'}, dimensions={0} | all-to-all | bytes 65536 | tf_op jit(solution)/shard_map/right_sum/all_to_all | solution.py:26
  114.9 26.6 %all_to_all.43 = f32[16,8,128]{2,1,0:T(8,128)S(1)} all-to-all(f32[16,8,128]{2,1,0:T(8,128)S(1)} %broadcast_in_dim.18), channel_id=1, replica_groups=mesh['y'=8,'x'=4,'core'=2,'far'=2,'next'=3,'col'=2] {'y','col'}, dimensions={0} | all-to-all | bytes 131072 | tf_op jit(solution)/shard_map/right_sum/all_to_all | solution.py:18
  141.5 9.2 %all_to_all.44.joint_ref = f32[8,8,128]{2,1,0:T(8,128)S(1)} all-to-all(f32[8,8,128]{2,1,0:T(8,128)S(1)} %broadcast_in_dim.19), channel_id=1, replica_groups=mesh['y'=8,'x'=4,'core'=2,'far'=2,'next'=3,'col'=2] {'x','core'}, dimensions={0} | all-to-all | bytes 65536 | tf_op jit(solution)/shard_map/right_sum/all_to_all | solution.py:18
  150.8 3.3 %finish.1 = (f32[1024,384]{1,0:T(8,128)}, f32[16,384]{1,0:T(8,128)}) custom-call(f32[8,8,128]{2,1,0:T(8,128)S(1)} %all_to_all.44.joint_ref, f32[8,16,128]{2,1,0:T(8,128)S(1)} %all-to-all-done.4.left_ref, f32[1024,384]{1,0:T(8,128)S(1)} %get-tuple-element.15.target_ref), custom_call_target="tpu_custom_call" | custom-call | tf_op jit(solution)/shard_map/finish/pallas_call | solution.py:194
  (26 shorter events, 1.9 us)
Async XLA Ops:
  7.2 25.6 %copy-start.4 = (bf16[128,1024]{1,0:T(8,128)(2,1)S(1)}, bf16[128,1024]{1,0:T(8,128)(2,1)}, u32[]{:S(2)}) copy-start(bf16[128,1024]{1,0:T(8,128)(2,1)} %acts_ref.1) | copy-start | bytes 786436
  7.2 25.6 %collective-permute-start = (bf16[128,1024]{1,0:T(8,128)(2,1)}, bf16[128,1024]{1,0:T(8,128)(2,1)S(1)}, u32[]{:S(2)}, u32[]{:S(2)}) collective-permute-start(bf16[128,1024]{1,0:T(8,128)(2,1)} %acts_ref.1), channel_id=1, source_target_pairs={{0,6},{6,0},{1,7},{7,1},{2,8},{8,2},{3,9},{9,3},{4,10},{10,4},{5,1... | collective-permute-start | bytes 786440 | tf_op jit(solution)/shard_map/gather_inputs/ppermute | solution.py:220
  17.6 27.4 %all-to-all-start = ((f32[12,16,128]{2,1,0:T(8,128)}), f32[12,16,128]{2,1,0:T(8,128)S(1)}, u32[]{:S(2)}, u32[]{:S(2)}) async-start(f32[12,16,128]{2,1,0:T(8,128)} %left_terms.3), calls=%async_computation | async-start | bytes 196608 | tf_op jit(solution)/shard_map/left_terms/all_to_all | solution.py:234
  29.8 71.3 %all-gather.2.cloned.1.call-start = ((), (), s32[]{:S(2)}) async-start(), calls=%async_computation.8 | async-start | bytes 2097152 | tf_op jit(solution)/shard_map/left_sum/all_gather | solution.py:240
  29.9 1.4 copy-start
  31.3 0.7 copy-start.7
  32.0 20.2 %copy-start.3 = (bf16[384,384]{1,0:T(8,128)(2,1)S(1)}, bf16[384,384]{1,0:T(8,128)(2,1)}, u32[]{:S(2)}) copy-start(bf16[384,384]{1,0:T(8,128)(2,1)} %mine_ref.1) | copy-start | bytes 884740
  32.8 68.3 %copy-start.1 = (f32[1024,384]{1,0:T(8,128)S(1)}, f32[1024,384]{1,0:T(8,128)}, u32[]{:S(2)}) copy-start(f32[1024,384]{1,0:T(8,128)} %err_ref.3) | copy-start | bytes 4718596
  45.8 11.2 %all-to-all-start.1 = ((f32[8,16,128]{2,1,0:T(8,128)}), f32[8,16,128]{2,1,0:T(8,128)S(1)}, u32[]{:S(2)}, u32[]{:S(2)}) async-start(f32[8,16,128]{2,1,0:T(8,128)} %left_terms.5), calls=%async_computation.1 | async-start | bytes 131072 | tf_op jit(solution)/shard_map/left_sum/all_to_all | solution.py:26
  52.2 34.1 %collective-permute-start.1 = (bf16[384,384]{1,0:T(8,128)(2,1)S(1)}, bf16[384,384]{1,0:T(8,128)(2,1)S(1)}, u32[]{:S(2)}, u32[]{:S(2)}) collective-permute-start(bf16[384,384]{1,0:T(8,128)(2,1)S(1)} %copy-done.3), channel_id=1, source_target_pairs={{0,1},{1,0},{2,3},{3,2},{4,5},{5,4},{6,7},{7,6},{8,9},{9,8},{10,11... | collective-permute-start | bytes 884744 | tf_op jit(solution)/shard_map/gather_inputs/ppermute | solution.py:222
  86.3 0.7 copy-start.5
  87.6 12.1 %all-to-all-start.4 = ((f32[8,16,128]{2,1,0:T(8,128)}), f32[8,16,128]{2,1,0:T(8,128)S(1)}, u32[]{:S(2)}, u32[]{:S(2)}) async-start(f32[8,16,128]{2,1,0:T(8,128)} %broadcast_in_dim.17), calls=%async_computation.4 | async-start | bytes 131072 | tf_op jit(solution)/shard_map/left_sum/all_to_all | solution.py:18
  101.1 1.4 copy-start.2
  102.5 1.0 copy-start.6
Sparse Core Ops, SparseCore 0:
  45.9 55.0 all-gather.1

commit v7 on v6

--- a/solution.py
+++ b/solution.py
@@ -24,6 +24,10 @@
 
 def split_and_summed(blocks, axes):
     return jnp.sum(lax.all_to_all(blocks, axes, split_axis=0, concat_axis=0, tiled=True), axis=0)
+
+
+def shifted(size, by):
+    return [(k, (k + by) % size) for k in range(size)]
 
 
 def dot(a, b, dims, precision=HIGHEST):
@@ -98,18 +102,20 @@
     )(*args)
 
 
-def target_kernel(
-    replicas, chunk, same_ref, acts_ref, mine_ref, other_ref, err_ref, left_ref,
-    target_ref, joint_ref, grads,
-):
+def target_kernel(replicas, n_pieces, place_ref, *refs):
+    pieces, refs = refs[:n_pieces], refs[n_pieces:]
+    mine_ref, other_ref, err_ref, left_ref, target_ref, joint_ref, grads = refs
     rank = left_ref.shape[1]
     wide = 256
-    same = same_ref[0] == 1
-    for k in range(mine_ref.shape[0] // chunk):
-        source = slice(k * chunk, (k + 1) * chunk)
+    depth = pieces[0].shape[0]
+    chunk = depth // 2
+    same = place_ref[0] == 1
+    for k in range(n_pieces):
+        source = lax.rem(place_ref[1] + n_pieces - k, n_pieces)
+        source = pl.ds(pl.multiple_of(source * chunk, chunk), chunk)
         mine, other = mine_ref[source], other_ref[source]
-        grads[2 * k * chunk : (2 * k + 1) * chunk] = jnp.where(same, mine, other)
-        grads[(2 * k + 1) * chunk : (2 * k + 2) * chunk] = jnp.where(same, other, mine)
+        grads[k * depth : k * depth + chunk] = jnp.where(same, mine, other)
+        grads[k * depth + chunk : (k + 1) * depth] = jnp.where(same, other, mine)
     left = lanes(left_ref, 0, left_ref.shape[0])
     stack = jnp.concatenate(thirds(left), axis=0)
     gram = lax.dot_general(
@@ -122,7 +128,9 @@
     sums = None
     for k in range(err_ref.shape[0] // wide):
         span = slice(k * wide, (k + 1) * wide)
-        tile = mxu(acts_ref[:, span], grads[...], ((0,), (0,))) + err_ref[span]
+        tile = err_ref[span]
+        for n, piece in enumerate(pieces):
+            tile += mxu(piece[:, span], grads[n * depth : (n + 1) * depth], ((0,), (0,)))
         target_ref[span] = tile
         high, mid, low = thirds(tile)
         terms = mxu(stack[:, span], high, ((1,), (0,))) + mxu(stack[:, span], mid, ((1,), (0,)))
@@ -135,14 +143,14 @@
         joint_ref[k] = both[first : first + rank // 2, at : at + 128]
 
 
-def target_and_terms(acts, mine, other, err, left, same, replicas, chunk):
+def target_and_terms(pieces, mine, other, err, left, place, replicas):
     rows, cols = err.shape
     rank = left.shape[1]
     tiles = cols // 128 + 1
     in_vmem = pl.BlockSpec(memory_space=pltpu.VMEM)
     return pl.pallas_call(
-        functools.partial(target_kernel, replicas, chunk),
-        in_specs=[pl.BlockSpec(memory_space=pltpu.SMEM)] + [in_vmem] * 5,
+        functools.partial(target_kernel, replicas, len(pieces)),
+        in_specs=[pl.BlockSpec(memory_space=pltpu.SMEM)] + [in_vmem] * (4 + len(pieces)),
         out_specs=[in_vmem, in_vmem],
         out_shape=[
             jax.ShapeDtypeStruct((rows, cols), jnp.float32),
@@ -150,7 +158,7 @@
         ],
         scratch_shapes=[pltpu.VMEM((2 * mine.shape[0], cols), mine.dtype)],
         compiler_params=pltpu.CompilerParams(vmem_limit_bytes=16 * 2**20),
-    )(same.astype(jnp.int32).reshape(1), acts, mine, other, err, left)
+    )(place, *pieces, mine, other, err, left)
 
 
 def finish_kernel(replicas, joint_ref, left_ref, target_ref, error_ref, right_ref, error, sems):
@@ -213,6 +221,7 @@
     n_row, n_col, n_near = lax.axis_size(ROW), lax.axis_size("col"), lax.axis_size(NEAR)
     col = lax.axis_index("col")
     replicas = lax.axis_size(REP)
+    n_next = lax.axis_size("next")
     tokens = acts.shape[0]
     right_t = right.T
 
@@ -237,7 +246,7 @@
 
     with jax.named_scope("left_sum"):
         blocks, pair = lax.optimization_barrier((blocks, pair))
-        all_acts = lax.all_gather(pair, "next", axis=0, tiled=True)
+        pieces = [pair, *(lax.ppermute(pair, "next", shifted(n_next, k)) for k in range(1, n_next))]
         part = split_and_summed(blocks, NEAR)
         part = summed_over(part, "y")
         part = summed_over(part, ROW)
@@ -246,7 +255,13 @@
 
     with jax.named_scope("target"):
         target, joint = target_and_terms(
-            all_acts, grads, other, err, left, col == lax.axis_index("far"), replicas, tokens
+            pieces,
+            grads,
+            other,
+            err,
+            left,
+            jnp.stack([(col == lax.axis_index("far")).astype(jnp.int32), lax.axis_index("next")]),
+            replicas,
         )
 
     with jax.named_scope("right_sum"):

time: 162 us -> 150 us (0.926)
  blocking collectives: 72.9 us -> 54.7 us
  between operations: 14.2 us -> 0.77 us
  waiting for transfers between devices: 19.6 us -> 29.7 us
  starting transfers between devices: 38.8 us -> 47.9 us
    all_to_all x4 -> x3, blocking collectives: 63.5 us -> 46.9 us  [to_all(): return lax.all_to_all(copies, axes, split_axis=0, concat_axis=0, tiled=True)]
    all_to_all x1 -> x2, waiting for transfers between devices: 4.85 us -> 16.5 us  [to_all(): return lax.all_to_all(copies, axes, split_axis=0, concat_axis=0, tiled=True)]
    ppermute x0 -> x2, starting transfers between devices: none -> 5.83 us  [body(): lax.ppermute(pair, 'next', shifted(n_next, k))]
    all_to_all x1 -> x2, starting transfers between devices: 7.21 us -> 10.8 us  [to_all(): return lax.all_to_all(copies, axes, split_axis=0, concat_axis=0, tiled=True)]
    unnamed x16 -> x14, local copies, waits for them, and re-layouts: 5.22 us -> 4.7 us
  transfers between devices with their start and end apart: 6 -> 8, of which waited for: 5 -> 4; matrix products, arithmetic and copies ran while one was open for 1% -> 1% of each run, Pallas kernels for 2% -> 2%
where the time goes in v7:
time: 150 us; the launch traced here: 149 us
  blocking collectives  54.7 us (36%)
  starting transfers between devices  47.9 us (32%)
  waiting for transfers between devices  29.7 us (20%)
  Pallas kernels  9.64 us (6%)
  local copies, waits for them, and re-layouts  5.98 us (4%)
    all_to_all x3, blocking collectives, to_all(): return lax.all_to_all(copies, axes, split_axis=0, concat_axis=0, tiled=True)  46.9 us
    all_to_all x2, waiting for transfers between devices, to_all(): return lax.all_to_all(copies, axes, split_axis=0, concat_axis=0, tiled=True)  16.5 us
    all_to_all x1, waiting for transfers between devices, body(): lax.all_to_all(sends, (*ROW, 'col'), split_axis=0, concat_axis=0, tiled=T...  12.2 us
    all_to_all x1, starting transfers between devices, body(): lax.all_to_all(sends, (*ROW, 'col'), split_axis=0, concat_axis=0, tiled=T...  12.2 us
    all_to_all x2, starting transfers between devices, to_all(): return lax.all_to_all(copies, axes, split_axis=0, concat_axis=0, tiled=True)  10.8 us
    ppermute x1, starting transfers between devices, body(): swapped = lax.ppermute(acts, 'far', [(0, 1), (1, 0)])  8.58 us
    all_to_all x1, blocking collectives, split_and_summed(): lax.all_to_all(blocks, axes, split_axis=0, concat_axis=0, tiled=True)  7.85 us
    all_to_all x1, starting transfers between devices, split_and_summed(): lax.all_to_all(blocks, axes, split_axis=0, concat_axis=0, tiled=True)  6.69 us
  transfers between devices with their start and end apart: 8, of which 4 were waited for; matrix products, arithmetic and copies ran while one was open for 1% of the time, Pallas kernels for 2%

profile of v7, /device:TPU:1, one launch (start us, length us, event | category | flops | bytes accessed | tf_op | source)
XLA Modules:
  0.0 148.9 jit_solution(5937907023951323383)
XLA Ops:
  0.6 8.6 %collective-permute-start = (bf16[128,1024]{1,0:T(8,128)(2,1)}, bf16[128,1024]{1,0:T(8,128)(2,1)S(1)}, u32[]{:S(2)}, u32[]{:S(2)}) collective-permute-start(bf16[128,1024]{1,0:T(8,128)(2,1)} %acts_ref.1), channel_id=1, source_target_pairs={{0,6},{6,0},{1,7},{7,1},{2,8},{8,2},{3,9},{9,3},{4,10},{10,4},{5,1... | collective-permute-start | bytes 786440 | tf_op jit(solution)/shard_map/gather_inputs/ppermute | solution.py:229
  9.2 1.9 %left_terms.3 = f32[12,16,128]{2,1,0:T(8,128)} custom-call(s32[1]{0:T(128)} %bitcast.2.col_ref, f32[16,384]{1,0:T(8,128)} %bitcast.5, bf16[384,384]{1,0:T(8,128)(2,1)} %refs_3_.1), custom_call_target="tpu_custom_call" | custom-call | tf_op jit(solution)/shard_map/left_terms/pallas_call | solution.py:95
  11.1 12.2 %all-to-all-start = ((f32[12,16,128]{2,1,0:T(8,128)}), f32[12,16,128]{2,1,0:T(8,128)S(1)}, u32[]{:S(2)}, u32[]{:S(2)}) async-start(f32[12,16,128]{2,1,0:T(8,128)} %left_terms.3), calls=%async_computation | async-start | bytes 196608 | tf_op jit(solution)/shard_map/left_terms/all_to_all | solution.py:243
  23.3 1.4 copy-done
  25.4 0.8 left_terms.4.part_ref
  26.3 12.2 %all-to-all-done.mine_ref = f32[12,16,128]{2,1,0:T(8,128)S(1)} async-done(((f32[12,16,128]{2,1,0:T(8,128)}), f32[12,16,128]{2,1,0:T(8,128)S(1)}, u32[]{:S(2)}, u32[]{:S(2)}) %all-to-all-start) | async-done | bytes 98336 | tf_op jit(solution)/shard_map/left_terms/all_to_all | solution.py:243
  38.5 0.8 left_terms.5
  39.3 3.9 %collective-permute-start.2 = (bf16[256,1024]{1,0:T(8,128)(2,1)S(1)}, bf16[256,1024]{1,0:T(8,128)(2,1)S(1)}, u32[]{:S(2)}, u32[]{:S(2)}) collective-permute-start(bf16[256,1024]{1,0:T(8,128)(2,1)S(1)} %pad_maximum_fusion.refs_0_), channel_id=1, source_target_pairs={{0,4},{2,0},{4,2},{1,5},{3,1},{5,3},{6,10},{8,6},{10,8},{7,11},{9,... | collective-permute-start | bytes 1572872 | tf_op jit(solution)/shard_map/left_sum/ppermute | solution.py:249
  43.2 1.9 %collective-permute-start.1 = (bf16[256,1024]{1,0:T(8,128)(2,1)S(1)}, bf16[256,1024]{1,0:T(8,128)(2,1)S(1)}, u32[]{:S(2)}, u32[]{:S(2)}) collective-permute-start(bf16[256,1024]{1,0:T(8,128)(2,1)S(1)} %pad_maximum_fusion.refs_0_), channel_id=1, source_target_pairs={{0,2},{2,4},{4,0},{1,3},{3,5},{5,1},{6,8},{8,10},{10,6},{7,9},{9,1... | collective-permute-start | bytes 1572872 | tf_op jit(solution)/shard_map/left_sum/ppermute | solution.py:249
  45.1 6.7 %all-to-all-start.1 = ((f32[8,16,128]{2,1,0:T(8,128)}), f32[8,16,128]{2,1,0:T(8,128)S(1)}, u32[]{:S(2)}, u32[]{:S(2)}) async-start(f32[8,16,128]{2,1,0:T(8,128)} %left_terms.5), calls=%async_computation.1 | async-start | bytes 131072 | tf_op jit(solution)/shard_map/left_sum/all_to_all | solution.py:26
  51.8 3.8 %collective-permute-start.3 = (bf16[384,384]{1,0:T(8,128)(2,1)S(1)}, bf16[384,384]{1,0:T(8,128)(2,1)}, u32[]{:S(2)}, u32[]{:S(2)}) collective-permute-start(bf16[384,384]{1,0:T(8,128)(2,1)S(1)} %copy-done.4), channel_id=1, source_target_pairs={{0,1},{1,0},{2,3},{3,2},{4,5},{5,4},{6,7},{7,6},{8,9},{9,8},{10,11... | collective-permute-start | bytes 884744 | tf_op jit(solution)/shard_map/gather_inputs/ppermute | solution.py:231
  55.6 1.0 all-to-all-done.1
  56.7 13.9 %all_to_all.40 = f32[8,16,128]{2,1,0:T(8,128)S(1)} all-to-all(f32[8,16,128]{2,1,0:T(8,128)S(1)} %broadcast_in_dim.15), channel_id=1, replica_groups=mesh['y'=8,'x'=4,'core'=2,'far'=2,'next'=3,'col'=2] {'y'}, dimensions={0} | all-to-all | bytes 131072 | tf_op jit(solution)/shard_map/left_sum/all_to_all | solution.py:18
  71.2 4.9 %all-to-all-start.3 = ((f32[6,16,128]{2,1,0:T(8,128)}), f32[6,16,128]{2,1,0:T(8,128)S(1)}, u32[]{:S(2)}, u32[]{:S(2)}) async-start(f32[6,16,128]{2,1,0:T(8,128)} %broadcast_in_dim.16), calls=%async_computation.3 | async-start | bytes 98304 | tf_op jit(solution)/shard_map/left_sum/all_to_all | solution.py:18
  76.1 11.7 %all-to-all-done.3 = f32[6,16,128]{2,1,0:T(8,128)S(1)} async-done(((f32[6,16,128]{2,1,0:T(8,128)}), f32[6,16,128]{2,1,0:T(8,128)S(1)}, u32[]{:S(2)}, u32[]{:S(2)}) %all-to-all-start.3) | async-done | bytes 49184 | tf_op jit(solution)/shard_map/left_sum/all_to_all | solution.py:18
  88.5 5.9 %all-to-all-start.4 = ((f32[8,16,128]{2,1,0:T(8,128)}), f32[8,16,128]{2,1,0:T(8,128)S(1)}, u32[]{:S(2)}, u32[]{:S(2)}) async-start(f32[8,16,128]{2,1,0:T(8,128)} %broadcast_in_dim.17), calls=%async_computation.4 | async-start | bytes 131072 | tf_op jit(solution)/shard_map/left_sum/all_to_all | solution.py:18
  94.4 4.8 %all-to-all-done.4.refs_6_.left_ref = f32[8,16,128]{2,1,0:T(8,128)S(1)} async-done(((f32[8,16,128]{2,1,0:T(8,128)}), f32[8,16,128]{2,1,0:T(8,128)S(1)}, u32[]{:S(2)}, u32[]{:S(2)}) %all-to-all-start.4) | async-done | bytes 65568 | tf_op jit(solution)/shard_map/left_sum/all_to_all | solution.py:18
  99.2 2.9 %target.1 = (f32[1024,384]{1,0:T(8,128)S(1)}, f32[8,8,128]{2,1,0:T(8,128)S(1)}) custom-call(s32[2]{0:T(128)S(1)} %pad_add_fusion.place_ref, bf16[256,1024]{1,0:T(8,128)(2,1)S(1)} %pad_maximum_fusion.refs_0_, bf16[256,1024]{1,0:T(8,128)(2,1)S(1)} %collective-permute-done.1.refs_1_, bf16[256,1024]{1,0:T(8,128)(2,1)S(1)} %collective-permute-done.2.refs_2_, ...), custom_call_target="tpu_custom_call" | custom-call | tf_op jit(solution)/shard_map/target/pallas_call | solution.py:151
  102.1 1.1 copy-done.2
  103.2 7.8 %all_to_all.41 = f32[8,8,128]{2,1,0:T(8,128)S(1)} all-to-all(f32[8,8,128]{2,1,0:T(8,128)S(1)} %get-tuple-element.14), channel_id=1, replica_groups=mesh['y'=8,'x'=4,'core'=2,'far'=2,'next'=3,'col'=2] {'x','core'}, dimensions={0} | all-to-all | bytes 65536 | tf_op jit(solution)/shard_map/right_sum/all_to_all | solution.py:26
  111.1 23.8 %all_to_all.42 = f32[16,8,128]{2,1,0:T(8,128)S(1)} all-to-all(f32[16,8,128]{2,1,0:T(8,128)S(1)} %broadcast_in_dim.18), channel_id=1, replica_groups=mesh['y'=8,'x'=4,'core'=2,'far'=2,'next'=3,'col'=2] {'y','col'}, dimensions={0} | all-to-all | bytes 131072 | tf_op jit(solution)/shard_map/right_sum/all_to_all | solution.py:18
  134.9 9.2 %all_to_all.43.joint_ref = f32[8,8,128]{2,1,0:T(8,128)S(1)} all-to-all(f32[8,8,128]{2,1,0:T(8,128)S(1)} %broadcast_in_dim.19), channel_id=1, replica_groups=mesh['y'=8,'x'=4,'core'=2,'far'=2,'next'=3,'col'=2] {'x','core'}, dimensions={0} | all-to-all | bytes 65536 | tf_op jit(solution)/shard_map/right_sum/all_to_all | solution.py:18
  144.2 1.4 copy-done.3
  145.6 3.3 %finish.1 = (f32[1024,384]{1,0:T(8,128)}, f32[16,384]{1,0:T(8,128)}) custom-call(f32[8,8,128]{2,1,0:T(8,128)S(1)} %all_to_all.43.joint_ref, f32[8,16,128]{2,1,0:T(8,128)S(1)} %all-to-all-done.4.refs_6_.left_ref, f32[1024,384]{1,0:T(8,128)S(1)} %copy-done.3), custom_call_target="tpu_custom_call" | custom-call | tf_op jit(solution)/shard_map/finish/pallas_call | solution.py:202
  (27 shorter events, 2.2 us)
Async XLA Ops:
  0.6 25.6 %copy-start.5 = (bf16[128,1024]{1,0:T(8,128)(2,1)S(1)}, bf16[128,1024]{1,0:T(8,128)(2,1)}, u32[]{:S(2)}) copy-start(bf16[128,1024]{1,0:T(8,128)(2,1)} %acts_ref.1) | copy-start | bytes 786436
  0.6 25.6 %collective-permute-start = (bf16[128,1024]{1,0:T(8,128)(2,1)}, bf16[128,1024]{1,0:T(8,128)(2,1)S(1)}, u32[]{:S(2)}, u32[]{:S(2)}) collective-permute-start(bf16[128,1024]{1,0:T(8,128)(2,1)} %acts_ref.1), channel_id=1, source_target_pairs={{0,6},{6,0},{1,7},{7,1},{2,8},{8,2},{3,9},{9,3},{4,10},{10,4},{5,1... | collective-permute-start | bytes 786440 | tf_op jit(solution)/shard_map/gather_inputs/ppermute | solution.py:229
  11.1 27.4 %all-to-all-start = ((f32[12,16,128]{2,1,0:T(8,128)}), f32[12,16,128]{2,1,0:T(8,128)S(1)}, u32[]{:S(2)}, u32[]{:S(2)}) async-start(f32[12,16,128]{2,1,0:T(8,128)} %left_terms.3), calls=%async_computation | async-start | bytes 196608 | tf_op jit(solution)/shard_map/left_terms/all_to_all | solution.py:243
  23.3 1.4 copy-start
  24.7 0.7 copy-start.6
  25.4 26.4 %copy-start.4 = (bf16[384,384]{1,0:T(8,128)(2,1)S(1)}, bf16[384,384]{1,0:T(8,128)(2,1)}, u32[]{:S(2)}) copy-start(bf16[384,384]{1,0:T(8,128)(2,1)} %refs_3_.1) | copy-start | bytes 884740
  26.2 73.0 %copy-start.1 = (f32[1024,384]{1,0:T(8,128)S(1)}, f32[1024,384]{1,0:T(8,128)}, u32[]{:S(2)}) copy-start(f32[1024,384]{1,0:T(8,128)} %refs_5_.1) | copy-start | bytes 4718596
  39.3 59.9 %collective-permute-start.2 = (bf16[256,1024]{1,0:T(8,128)(2,1)S(1)}, bf16[256,1024]{1,0:T(8,128)(2,1)S(1)}, u32[]{:S(2)}, u32[]{:S(2)}) collective-permute-start(bf16[256,1024]{1,0:T(8,128)(2,1)S(1)} %pad_maximum_fusion.refs_0_), channel_id=1, source_target_pairs={{0,4},{2,0},{4,2},{1,5},{3,1},{5,3},{6,10},{8,6},{10,8},{7,11},{9,... | collective-permute-start | bytes 1572872 | tf_op jit(solution)/shard_map/left_sum/ppermute | solution.py:249
  43.2 56.0 %collective-permute-start.1 = (bf16[256,1024]{1,0:T(8,128)(2,1)S(1)}, bf16[256,1024]{1,0:T(8,128)(2,1)S(1)}, u32[]{:S(2)}, u32[]{:S(2)}) collective-permute-start(bf16[256,1024]{1,0:T(8,128)(2,1)S(1)} %pad_maximum_fusion.refs_0_), channel_id=1, source_target_pairs={{0,2},{2,4},{4,0},{1,3},{3,5},{5,1},{6,8},{8,10},{10,6},{7,9},{9,1... | collective-permute-start | bytes 1572872 | tf_op jit(solution)/shard_map/left_sum/ppermute | solution.py:249
  45.1 11.5 %all-to-all-start.1 = ((f32[8,16,128]{2,1,0:T(8,128)}), f32[8,16,128]{2,1,0:T(8,128)S(1)}, u32[]{:S(2)}, u32[]{:S(2)}) async-start(f32[8,16,128]{2,1,0:T(8,128)} %left_terms.5), calls=%async_computation.1 | async-start | bytes 131072 | tf_op jit(solution)/shard_map/left_sum/all_to_all | solution.py:26
  51.8 36.0 %collective-permute-start.3 = (bf16[384,384]{1,0:T(8,128)(2,1)S(1)}, bf16[384,384]{1,0:T(8,128)(2,1)}, u32[]{:S(2)}, u32[]{:S(2)}) collective-permute-start(bf16[384,384]{1,0:T(8,128)(2,1)S(1)} %copy-done.4), channel_id=1, source_target_pairs={{0,1},{1,0},{2,3},{3,2},{4,5},{5,4},{6,7},{7,6},{8,9},{9,8},{10,11... | collective-permute-start | bytes 884744 | tf_op jit(solution)/shard_map/gather_inputs/ppermute | solution.py:231
  71.2 16.6 %all-to-all-start.3 = ((f32[6,16,128]{2,1,0:T(8,128)}), f32[6,16,128]{2,1,0:T(8,128)S(1)}, u32[]{:S(2)}, u32[]{:S(2)}) async-start(f32[6,16,128]{2,1,0:T(8,128)} %broadcast_in_dim.16), calls=%async_computation.3 | async-start | bytes 98304 | tf_op jit(solution)/shard_map/left_sum/all_to_all | solution.py:18
  88.5 10.7 %all-to-all-start.4 = ((f32[8,16,128]{2,1,0:T(8,128)}), f32[8,16,128]{2,1,0:T(8,128)S(1)}, u32[]{:S(2)}, u32[]{:S(2)}) async-start(f32[8,16,128]{2,1,0:T(8,128)} %broadcast_in_dim.17), calls=%async_computation.4 | async-start | bytes 131072 | tf_op jit(solution)/shard_map/left_sum/all_to_all | solution.py:18
  102.1 1.1 copy-start.2
  144.2 1.4 copy-start.3

commit v8 on v7

--- a/solution.py
+++ b/solution.py
@@ -104,7 +104,7 @@
 
 def target_kernel(replicas, n_pieces, place_ref, *refs):
     pieces, refs = refs[:n_pieces], refs[n_pieces:]
-    mine_ref, other_ref, err_ref, left_ref, target_ref, joint_ref, grads = refs
+    mine_ref, other_ref, err_ref, left_ref, target_ref, joint_ref, grads, target, sems = refs
     rank = left_ref.shape[1]
     wide = 256
     depth = pieces[0].shape[0]
@@ -125,13 +125,15 @@
         precision=HIGHEST,
         preferred_element_type=jnp.float32,
     )
-    sums = None
+    sums, copies = None, []
     for k in range(err_ref.shape[0] // wide):
         span = slice(k * wide, (k + 1) * wide)
         tile = err_ref[span]
         for n, piece in enumerate(pieces):
             tile += mxu(piece[:, span], grads[n * depth : (n + 1) * depth], ((0,), (0,)))
-        target_ref[span] = tile
+        target[span] = tile
+        copies.append(pltpu.make_async_copy(target.at[span], target_ref.at[span], sems.at[k]))
+        copies[-1].start()
         high, mid, low = thirds(tile)
         terms = mxu(stack[:, span], high, ((1,), (0,))) + mxu(stack[:, span], mid, ((1,), (0,)))
         right = joined(terms, rank) + mxu(stack[:rank, span], low, ((1,), (0,)))
@@ -141,6 +143,8 @@
     for k in range(joint_ref.shape[0]):
         first, at = (k % 2) * (rank // 2), (k // 2) * 128
         joint_ref[k] = both[first : first + rank // 2, at : at + 128]
+    for copy in copies:
+        copy.wait()
 
 
 def target_and_terms(pieces, mine, other, err, left, place, replicas):
@@ -151,18 +155,32 @@
     return pl.pallas_call(
         functools.partial(target_kernel, replicas, len(pieces)),
         in_specs=[pl.BlockSpec(memory_space=pltpu.SMEM)] + [in_vmem] * (4 + len(pieces)),
-        out_specs=[in_vmem, in_vmem],
+        out_specs=[pl.BlockSpec(memory_space=pl.ANY), in_vmem],
         out_shape=[
             jax.ShapeDtypeStruct((rows, cols), jnp.float32),
             jax.ShapeDtypeStruct((2 * tiles, rank // 2, 128), jnp.float32),
         ],
-        scratch_shapes=[pltpu.VMEM((2 * mine.shape[0], cols), mine.dtype)],
+        scratch_shapes=[
+            pltpu.VMEM((2 * mine.shape[0], cols), mine.dtype),
+            pltpu.VMEM((rows, cols), jnp.float32),
+            pltpu.SemaphoreType.DMA((rows // 256,)),
+        ],
         compiler_params=pltpu.CompilerParams(vmem_limit_bytes=16 * 2**20),
     )(place, *pieces, mine, other, err, left)
 
 
-def finish_kernel(replicas, joint_ref, left_ref, target_ref, error_ref, right_ref, error, sems):
+def finish_kernel(
+    replicas, joint_ref, left_ref, target_ref, error_ref, right_ref, error, in_sems, sems
+):
     rank, cols = right_ref.shape
+    wide = error.shape[0] // sems.shape[0]
+    spans = [slice(k * wide, (k + 1) * wide) for k in range(sems.shape[0])]
+    loads = [
+        pltpu.make_async_copy(target_ref.at[span], error.at[span], in_sems.at[k])
+        for k, span in enumerate(spans)
+    ]
+    for load in loads:
+        load.start()
     halves = [
         jnp.concatenate([joint_ref[2 * c + h] for c in range(joint_ref.shape[0] // 2)], axis=1)
         for h in range(2)
@@ -184,11 +202,10 @@
     rights = jnp.concatenate([first, second, first, second, third, first], axis=0)
     first, second, third = thirds(system[:, cols + 128 :])
     orths = jnp.concatenate([first, first, second, second, first, third], axis=0)
-    wide = target_ref.shape[0] // sems.shape[0]
     copies = []
-    for k in range(sems.shape[0]):
-        span = slice(k * wide, (k + 1) * wide)
-        error[span] = target_ref[span] - mxu(orths[:, span], rights, ((0,), (0,)))
+    for k, span in enumerate(spans):
+        loads[k].wait()
+        error[span] = error[span] - mxu(orths[:, span], rights, ((0,), (0,)))
         copies.append(pltpu.make_async_copy(error.at[span], error_ref.at[span], sems.at[k]))
         copies[-1].start()
     for copy in copies:
@@ -201,7 +218,7 @@
     in_vmem = pl.BlockSpec(memory_space=pltpu.VMEM)
     return pl.pallas_call(
         functools.partial(finish_kernel, replicas),
-        in_specs=[in_vmem] * 3,
+        in_specs=[in_vmem, in_vmem, pl.BlockSpec(memory_space=pl.ANY)],
         out_specs=[pl.BlockSpec(memory_space=pl.ANY), in_vmem],
         out_shape=[
             jax.ShapeDtypeStruct((rows, cols), jnp.float32),
@@ -210,7 +227,9 @@
         scratch_shapes=[
             pltpu.VMEM((rows, cols), jnp.float32),
             pltpu.SemaphoreType.DMA((4,)),
+            pltpu.SemaphoreType.DMA((4,)),
         ],
+        input_output_aliases={2: 0},
         compiler_params=pltpu.CompilerParams(vmem_limit_bytes=16 * 2**20),
     )(joint, left, target)
 
@@ -245,12 +264,12 @@
         blocks = local_call(left_kernel, (n_near, rank, rows // n_near), mine, acts, part)
 
     with jax.named_scope("left_sum"):
-        blocks, pair = lax.optimization_barrier((blocks, pair))
+        part = split_and_summed(blocks, NEAR)
+        part, pair = lax.optimization_barrier((part, pair))
         pieces = [pair, *(lax.ppermute(pair, "next", shifted(n_next, k)) for k in range(1, n_next))]
-        part = split_and_summed(blocks, NEAR)
         part = summed_over(part, "y")
+        part, other = lax.optimization_barrier((part, other))
         part = summed_over(part, ROW)
-        part, other = lax.optimization_barrier((part, other))
         left = to_all(part, NEAR)
 
     with jax.named_scope("target"):

time: 150 us -> 151 us (level)
  starting transfers between devices: 47.9 us -> 56.7 us
  blocking collectives: 54.7 us -> 50.7 us
  local copies, waits for them, and re-layouts: 5.98 us -> 3.43 us
  waiting for transfers between devices: 29.7 us -> 27.3 us
    ppermute x1, waiting for transfers between devices: 0.01 us -> 14.9 us  [body(): swapped = lax.ppermute(acts, 'far', [(0, 1), (1, 0)])]
    all_to_all x1, waiting for transfers between devices: 12.2 us -> 0.01 us  [body(): lax.all_to_all(sends, (*ROW, 'col'), split_axis=0, concat_axis=0, tiled=T...]
    all_to_all x2, starting transfers between devices: 10.8 us -> 17.2 us  [to_all(): return lax.all_to_all(copies, axes, split_axis=0, concat_axis=0, tiled=True)]
    all_to_all x2, waiting for transfers between devices: 16.5 us -> 12.4 us  [to_all(): return lax.all_to_all(copies, axes, split_axis=0, concat_axis=0, tiled=True)]
    all_to_all x3, blocking collectives: 46.9 us -> 42.8 us  [to_all(): return lax.all_to_all(copies, axes, split_axis=0, concat_axis=0, tiled=True)]
    all_to_all x1, starting transfers between devices: 12.2 us -> 15.7 us  [body(): lax.all_to_all(sends, (*ROW, 'col'), split_axis=0, concat_axis=0, tiled=T...]
    ppermute x1, starting transfers between devices: 3.82 us -> 7.31 us  [body(): other = lax.ppermute(grads, 'col', [(0, 1), (1, 0)])]
    ppermute x1, starting transfers between devices: 8.58 us -> 5.13 us  [body(): swapped = lax.ppermute(acts, 'far', [(0, 1), (1, 0)])]
  transfers between devices with their start and end apart: 8 -> 8, of which waited for: 4 -> 3; matrix products, arithmetic and copies ran while one was open for 1% -> 1% of each run, Pallas kernels for 2% -> 1%
where the time goes in v8:
time: 151 us; the launch traced here: 150 us
  starting transfers between devices  56.7 us (38%)
  blocking collectives  50.7 us (34%)
  waiting for transfers between devices  27.3 us (18%)
  Pallas kernels  11 us (7%)
  local copies, waits for them, and re-layouts  3.43 us (2%)
    all_to_all x3, blocking collectives, to_all(): return lax.all_to_all(copies, axes, split_axis=0, concat_axis=0, tiled=True)  42.8 us
    all_to_all x2, starting transfers between devices, to_all(): return lax.all_to_all(copies, axes, split_axis=0, concat_axis=0, tiled=True)  17.2 us
    all_to_all x1, starting transfers between devices, body(): lax.all_to_all(sends, (*ROW, 'col'), split_axis=0, concat_axis=0, tiled=T...  15.7 us
    ppermute x1, waiting for transfers between devices, body(): swapped = lax.ppermute(acts, 'far', [(0, 1), (1, 0)])  14.9 us
    all_to_all x2, waiting for transfers between devices, to_all(): return lax.all_to_all(copies, axes, split_axis=0, concat_axis=0, tiled=True)  12.4 us
    all_to_all x1, blocking collectives, split_and_summed(): lax.all_to_all(blocks, axes, split_axis=0, concat_axis=0, tiled=True)  7.86 us
    ppermute x1, starting transfers between devices, body(): other = lax.ppermute(grads, 'col', [(0, 1), (1, 0)])  7.31 us
    all_to_all x1, starting transfers between devices, split_and_summed(): lax.all_to_all(blocks, axes, split_axis=0, concat_axis=0, tiled=True)  6.09 us
  transfers between devices with their start and end apart: 8, of which 3 were waited for; matrix products, arithmetic and copies ran while one was open for 1% of the time, Pallas kernels for 1%

profile of v8, /device:TPU:1, one launch (start us, length us, event | category | flops | bytes accessed | tf_op | source)
XLA Modules:
  0.0 150.0 jit_solution(3299860049474691194)
XLA Ops:
  0.6 1.9 %left_terms.3 = f32[12,16,128]{2,1,0:T(8,128)} custom-call(s32[1]{0:T(128)} %bitcast.2.col_ref, f32[16,384]{1,0:T(8,128)} %bitcast.5, bf16[384,384]{1,0:T(8,128)(2,1)} %refs_3_.1), custom_call_target="tpu_custom_call" | custom-call | tf_op jit(solution)/shard_map/left_terms/pallas_call | solution.py:95
  2.5 15.7 %all-to-all-start = ((f32[12,16,128]{2,1,0:T(8,128)}), f32[12,16,128]{2,1,0:T(8,128)S(1)}, u32[]{:S(2)}, u32[]{:S(2)}) async-start(f32[12,16,128]{2,1,0:T(8,128)} %left_terms.3), calls=%async_computation | async-start | bytes 196608 | tf_op jit(solution)/shard_map/left_terms/all_to_all | solution.py:262
  18.3 5.1 %collective-permute-start = (bf16[128,1024]{1,0:T(8,128)(2,1)}, bf16[128,1024]{1,0:T(8,128)(2,1)S(1)}, u32[]{:S(2)}, u32[]{:S(2)}) collective-permute-start(bf16[128,1024]{1,0:T(8,128)(2,1)} %acts_ref.1), channel_id=1, source_target_pairs={{0,6},{6,0},{1,7},{7,1},{2,8},{8,2},{3,9},{9,3},{4,10},{10,4},{5,1... | collective-permute-start | bytes 786440 | tf_op jit(solution)/shard_map/gather_inputs/ppermute | solution.py:248
  23.4 7.3 %collective-permute-start.3 = (bf16[384,384]{1,0:T(8,128)(2,1)}, bf16[384,384]{1,0:T(8,128)(2,1)}, u32[]{:S(2)}, u32[]{:S(2)}) collective-permute-start(bf16[384,384]{1,0:T(8,128)(2,1)} %refs_3_.1), channel_id=1, source_target_pairs={{0,1},{1,0},{2,3},{3,2},{4,5},{5,4},{6,7},{7,6},{8,9},{9,8},{10,11... | collective-permute-start | bytes 884744 | tf_op jit(solution)/shard_map/gather_inputs/ppermute | solution.py:250
  30.7 1.4 copy-done
  32.1 0.7 copy-done.4
  32.9 0.8 left_terms.4.part_ref
  33.7 0.8 left_terms.5
  34.5 6.1 %all-to-all-start.1 = ((f32[8,16,128]{2,1,0:T(8,128)}), f32[8,16,128]{2,1,0:T(8,128)S(1)}, u32[]{:S(2)}, u32[]{:S(2)}) async-start(f32[8,16,128]{2,1,0:T(8,128)} %left_terms.5), calls=%async_computation.1 | async-start | bytes 131072 | tf_op jit(solution)/shard_map/left_sum/all_to_all | solution.py:26
  40.6 14.9 %collective-permute-done = bf16[128,1024]{1,0:T(8,128)(2,1)S(1)} collective-permute-done((bf16[128,1024]{1,0:T(8,128)(2,1)}, bf16[128,1024]{1,0:T(8,128)(2,1)S(1)}, u32[]{:S(2)}, u32[]{:S(2)}) %collective-permute-start) | collective-permute-done | bytes 262176 | tf_op jit(solution)/shard_map/gather_inputs/ppermute | solution.py:248
  55.5 2.6 %collective-permute-start.2 = (bf16[256,1024]{1,0:T(8,128)(2,1)S(1)}, bf16[256,1024]{1,0:T(8,128)(2,1)S(1)}, u32[]{:S(2)}, u32[]{:S(2)}) collective-permute-start(bf16[256,1024]{1,0:T(8,128)(2,1)S(1)} %pad_maximum_fusion.refs_0_), channel_id=1, source_target_pairs={{0,4},{2,0},{4,2},{1,5},{3,1},{5,3},{6,10},{8,6},{10,8},{7,11},{9,... | collective-permute-start | bytes 1572872 | tf_op jit(solution)/shard_map/left_sum/ppermute | solution.py:269
  58.1 2.7 %collective-permute-start.1 = (bf16[256,1024]{1,0:T(8,128)(2,1)S(1)}, bf16[256,1024]{1,0:T(8,128)(2,1)S(1)}, u32[]{:S(2)}, u32[]{:S(2)}) collective-permute-start(bf16[256,1024]{1,0:T(8,128)(2,1)S(1)} %pad_maximum_fusion.refs_0_), channel_id=1, source_target_pairs={{0,2},{2,4},{4,0},{1,3},{3,5},{5,1},{6,8},{8,10},{10,6},{7,9},{9,1... | collective-permute-start | bytes 1572872 | tf_op jit(solution)/shard_map/left_sum/ppermute | solution.py:269
  60.8 13.8 %all_to_all.40 = f32[8,16,128]{2,1,0:T(8,128)S(1)} all-to-all(f32[8,16,128]{2,1,0:T(8,128)S(1)} %broadcast_in_dim.15), channel_id=1, replica_groups=mesh['y'=8,'x'=4,'core'=2,'far'=2,'next'=3,'col'=2] {'y'}, dimensions={0} | all-to-all | bytes 131072 | tf_op jit(solution)/shard_map/left_sum/all_to_all | solution.py:18
  74.7 0.6 broadcast_in_dim.16
  75.3 8.9 %all-to-all-start.3 = ((f32[6,16,128]{2,1,0:T(8,128)}), f32[6,16,128]{2,1,0:T(8,128)S(1)}, u32[]{:S(2)}, u32[]{:S(2)}) async-start(f32[6,16,128]{2,1,0:T(8,128)} %broadcast_in_dim.16), calls=%async_computation.3 | async-start | bytes 98304 | tf_op jit(solution)/shard_map/left_sum/all_to_all | solution.py:18
  84.2 7.6 %all-to-all-done.3 = f32[6,16,128]{2,1,0:T(8,128)S(1)} async-done(((f32[6,16,128]{2,1,0:T(8,128)}), f32[6,16,128]{2,1,0:T(8,128)S(1)}, u32[]{:S(2)}, u32[]{:S(2)}) %all-to-all-start.3) | async-done | bytes 49184 | tf_op jit(solution)/shard_map/left_sum/all_to_all | solution.py:18
  91.8 0.6 broadcast_in_dim.17
  92.4 8.3 %all-to-all-start.4 = ((f32[8,16,128]{2,1,0:T(8,128)}), f32[8,16,128]{2,1,0:T(8,128)S(1)}, u32[]{:S(2)}, u32[]{:S(2)}) async-start(f32[8,16,128]{2,1,0:T(8,128)} %broadcast_in_dim.17), calls=%async_computation.4 | async-start | bytes 131072 | tf_op jit(solution)/shard_map/left_sum/all_to_all | solution.py:18
  100.8 4.8 %all-to-all-done.4.refs_6_.left_ref = f32[8,16,128]{2,1,0:T(8,128)S(1)} async-done(((f32[8,16,128]{2,1,0:T(8,128)}), f32[8,16,128]{2,1,0:T(8,128)S(1)}, u32[]{:S(2)}, u32[]{:S(2)}) %all-to-all-start.4) | async-done | bytes 65568 | tf_op jit(solution)/shard_map/left_sum/all_to_all | solution.py:18
  105.6 3.5 %target.1 = (f32[1024,384]{1,0:T(8,128)}, f32[8,8,128]{2,1,0:T(8,128)S(1)}) custom-call(s32[2]{0:T(128)S(1)} %pad_add_fusion.place_ref, bf16[256,1024]{1,0:T(8,128)(2,1)S(1)} %pad_maximum_fusion.refs_0_, bf16[256,1024]{1,0:T(8,128)(2,1)S(1)} %collective-permute-done.1.refs_1_, bf16[256,1024]{1,0:T(8,128)(2,1)S(1)} %collective-permute-done.2.refs_2_, ...), custom_call_target="tpu_custom_call" | custom-call | tf_op jit(solution)/shard_map/target/pallas_call | solution.py:155
  109.2 7.9 %all_to_all.41 = f32[8,8,128]{2,1,0:T(8,128)S(1)} all-to-all(f32[8,8,128]{2,1,0:T(8,128)S(1)} %get-tuple-element.14), channel_id=1, replica_groups=mesh['y'=8,'x'=4,'core'=2,'far'=2,'next'=3,'col'=2] {'x','core'}, dimensions={0} | all-to-all | bytes 65536 | tf_op jit(solution)/shard_map/right_sum/all_to_all | solution.py:26
  117.0 19.8 %all_to_all.42 = f32[16,8,128]{2,1,0:T(8,128)S(1)} all-to-all(f32[16,8,128]{2,1,0:T(8,128)S(1)} %broadcast_in_dim.18), channel_id=1, replica_groups=mesh['y'=8,'x'=4,'core'=2,'far'=2,'next'=3,'col'=2] {'y','col'}, dimensions={0} | all-to-all | bytes 131072 | tf_op jit(solution)/shard_map/right_sum/all_to_all | solution.py:18
  136.8 9.2 %all_to_all.43.joint_ref = f32[8,8,128]{2,1,0:T(8,128)S(1)} all-to-all(f32[8,8,128]{2,1,0:T(8,128)S(1)} %broadcast_in_dim.19), channel_id=1, replica_groups=mesh['y'=8,'x'=4,'core'=2,'far'=2,'next'=3,'col'=2] {'x','core'}, dimensions={0} | all-to-all | bytes 65536 | tf_op jit(solution)/shard_map/right_sum/all_to_all | solution.py:18
  146.1 4.0 %finish.1 = (f32[1024,384]{1,0:T(8,128)}, f32[16,384]{1,0:T(8,128)}) custom-call(f32[8,8,128]{2,1,0:T(8,128)S(1)} %all_to_all.43.joint_ref, f32[8,16,128]{2,1,0:T(8,128)S(1)} %all-to-all-done.4.refs_6_.left_ref, f32[1024,384]{1,0:T(8,128)} %get-tuple-element.15.target_ref), custom_call_target="tpu_custom_call", output_to_operand_aliasing={{0}: (2, {})} | custom-call | tf_op jit(solution)/shard_map/finish/pallas_call | solution.py:219
  (23 shorter events, 0.2 us)
Async XLA Ops:
  0.6 33.0 %copy-start.3 = (bf16[128,1024]{1,0:T(8,128)(2,1)S(1)}, bf16[128,1024]{1,0:T(8,128)(2,1)}, u32[]{:S(2)}) copy-start(bf16[128,1024]{1,0:T(8,128)(2,1)} %acts_ref.1) | copy-start | bytes 786436
  2.5 31.1 %all-to-all-start = ((f32[12,16,128]{2,1,0:T(8,128)}), f32[12,16,128]{2,1,0:T(8,128)S(1)}, u32[]{:S(2)}, u32[]{:S(2)}) async-start(f32[12,16,128]{2,1,0:T(8,128)} %left_terms.3), calls=%async_computation | async-start | bytes 196608 | tf_op jit(solution)/shard_map/left_terms/all_to_all | solution.py:262
  18.3 37.2 %collective-permute-start = (bf16[128,1024]{1,0:T(8,128)(2,1)}, bf16[128,1024]{1,0:T(8,128)(2,1)S(1)}, u32[]{:S(2)}, u32[]{:S(2)}) collective-permute-start(bf16[128,1024]{1,0:T(8,128)(2,1)} %acts_ref.1), channel_id=1, source_target_pairs={{0,6},{6,0},{1,7},{7,1},{2,8},{8,2},{3,9},{9,3},{4,10},{10,4},{5,1... | collective-permute-start | bytes 786440 | tf_op jit(solution)/shard_map/gather_inputs/ppermute | solution.py:248
  23.4 51.3 %collective-permute-start.3 = (bf16[384,384]{1,0:T(8,128)(2,1)}, bf16[384,384]{1,0:T(8,128)(2,1)}, u32[]{:S(2)}, u32[]{:S(2)}) collective-permute-start(bf16[384,384]{1,0:T(8,128)(2,1)} %refs_3_.1), channel_id=1, source_target_pairs={{0,1},{1,0},{2,3},{3,2},{4,5},{5,4},{6,7},{7,6},{8,9},{9,8},{10,11... | collective-permute-start | bytes 884744 | tf_op jit(solution)/shard_map/gather_inputs/ppermute | solution.py:250
  30.7 1.4 copy-start
  32.1 0.7 copy-start.4
  33.6 72.0 %copy-start.1 = (f32[1024,384]{1,0:T(8,128)S(1)}, f32[1024,384]{1,0:T(8,128)}, u32[]{:S(2)}) copy-start(f32[1024,384]{1,0:T(8,128)} %refs_5_.1) | copy-start | bytes 4718596
  33.6 72.0 %copy-start.2 = (bf16[384,384]{1,0:T(8,128)(2,1)S(1)}, bf16[384,384]{1,0:T(8,128)(2,1)}, u32[]{:S(2)}) copy-start(bf16[384,384]{1,0:T(8,128)(2,1)} %refs_3_.1) | copy-start | bytes 884740
  34.5 21.0 %all-to-all-start.1 = ((f32[8,16,128]{2,1,0:T(8,128)}), f32[8,16,128]{2,1,0:T(8,128)S(1)}, u32[]{:S(2)}, u32[]{:S(2)}) async-start(f32[8,16,128]{2,1,0:T(8,128)} %left_terms.5), calls=%async_computation.1 | async-start | bytes 131072 | tf_op jit(solution)/shard_map/left_sum/all_to_all | solution.py:26
  55.5 50.1 %collective-permute-start.2 = (bf16[256,1024]{1,0:T(8,128)(2,1)S(1)}, bf16[256,1024]{1,0:T(8,128)(2,1)S(1)}, u32[]{:S(2)}, u32[]{:S(2)}) collective-permute-start(bf16[256,1024]{1,0:T(8,128)(2,1)S(1)} %pad_maximum_fusion.refs_0_), channel_id=1, source_target_pairs={{0,4},{2,0},{4,2},{1,5},{3,1},{5,3},{6,10},{8,6},{10,8},{7,11},{9,... | collective-permute-start | bytes 1572872 | tf_op jit(solution)/shard_map/left_sum/ppermute | solution.py:269
  58.1 47.5 %collective-permute-start.1 = (bf16[256,1024]{1,0:T(8,128)(2,1)S(1)}, bf16[256,1024]{1,0:T(8,128)(2,1)S(1)}, u32[]{:S(2)}, u32[]{:S(2)}) collective-permute-start(bf16[256,1024]{1,0:T(8,128)(2,1)S(1)} %pad_maximum_fusion.refs_0_), channel_id=1, source_target_pairs={{0,2},{2,4},{4,0},{1,3},{3,5},{5,1},{6,8},{8,10},{10,6},{7,9},{9,1... | collective-permute-start | bytes 1572872 | tf_op jit(solution)/shard_map/left_sum/ppermute | solution.py:269
  75.3 16.5 %all-to-all-start.3 = ((f32[6,16,128]{2,1,0:T(8,128)}), f32[6,16,128]{2,1,0:T(8,128)S(1)}, u32[]{:S(2)}, u32[]{:S(2)}) async-start(f32[6,16,128]{2,1,0:T(8,128)} %broadcast_in_dim.16), calls=%async_computation.3 | async-start | bytes 98304 | tf_op jit(solution)/shard_map/left_sum/all_to_all | solution.py:18
  92.4 13.2 %all-to-all-start.4 = ((f32[8,16,128]{2,1,0:T(8,128)}), f32[8,16,128]{2,1,0:T(8,128)S(1)}, u32[]{:S(2)}, u32[]{:S(2)}) async-start(f32[8,16,128]{2,1,0:T(8,128)} %broadcast_in_dim.17), calls=%async_computation.4 | async-start | bytes 131072 | tf_op jit(solution)/shard_map/left_sum/all_to_all | solution.py:18

commit v9 on v8

--- a/solution.py
+++ b/solution.py
@@ -268,8 +268,8 @@
         part, pair = lax.optimization_barrier((part, pair))
         pieces = [pair, *(lax.ppermute(pair, "next", shifted(n_next, k)) for k in range(1, n_next))]
         part = summed_over(part, "y")
+        part = summed_over(part, ROW)
         part, other = lax.optimization_barrier((part, other))
-        part = summed_over(part, ROW)
         left = to_all(part, NEAR)
 
     with jax.named_scope("target"):

time: 151 us -> 154 us (1.020)
  starting transfers between devices: 56.7 us -> 50.6 us
  waiting for transfers between devices: 27.3 us -> 32.3 us
  blocking collectives: 50.7 us -> 55.3 us
    all_to_all x2, waiting for transfers between devices: 12.4 us -> 23.5 us  [to_all(): return lax.all_to_all(copies, axes, split_axis=0, concat_axis=0, tiled=True)]
    all_to_all x2, starting transfers between devices: 17.2 us -> 8.55 us  [to_all(): return lax.all_to_all(copies, axes, split_axis=0, concat_axis=0, tiled=True)]
    ppermute x1, waiting for transfers between devices: 14.9 us -> 7.45 us  [body(): swapped = lax.ppermute(acts, 'far', [(0, 1), (1, 0)])]
    all_to_all x3, blocking collectives: 42.8 us -> 47.4 us  [to_all(): return lax.all_to_all(copies, axes, split_axis=0, concat_axis=0, tiled=True)]
    ppermute x1, starting transfers between devices: 7.31 us -> 9.08 us  [body(): other = lax.ppermute(grads, 'col', [(0, 1), (1, 0)])]
  transfers between devices with their start and end apart: 8 -> 8, of which waited for: 3 -> 4; matrix products, arithmetic and copies ran while one was open for 1% -> 1% of each run, Pallas kernels for 1% -> 1%
where the time goes in v9:
time: 154 us
  blocking collectives  55.3 us (36%)
  starting transfers between devices  50.6 us (33%)
  waiting for transfers between devices  32.3 us (21%)
  Pallas kernels  11 us (7%)
  local copies, waits for them, and re-layouts  3.43 us (2%)
    all_to_all x3, blocking collectives, to_all(): return lax.all_to_all(copies, axes, split_axis=0, concat_axis=0, tiled=True)  47.4 us
    all_to_all x2, waiting for transfers between devices, to_all(): return lax.all_to_all(copies, axes, split_axis=0, concat_axis=0, tiled=True)  23.5 us
    all_to_all x1, starting transfers between devices, body(): lax.all_to_all(sends, (*ROW, 'col'), split_axis=0, concat_axis=0, tiled=T...  15.7 us
    ppermute x1, starting transfers between devices, body(): other = lax.ppermute(grads, 'col', [(0, 1), (1, 0)])  9.08 us
    all_to_all x2, starting transfers between devices, to_all(): return lax.all_to_all(copies, axes, split_axis=0, concat_axis=0, tiled=True)  8.55 us
    all_to_all x1, blocking collectives, split_and_summed(): lax.all_to_all(blocks, axes, split_axis=0, concat_axis=0, tiled=True)  7.86 us
    ppermute x1, waiting for transfers between devices, body(): swapped = lax.ppermute(acts, 'far', [(0, 1), (1, 0)])  7.45 us
    all_to_all x1, starting transfers between devices, split_and_summed(): lax.all_to_all(blocks, axes, split_axis=0, concat_axis=0, tiled=True)  6.85 us
  transfers between devices with their start and end apart: 8, of which 4 were waited for; matrix products, arithmetic and copies ran while one was open for 1% of the time, Pallas kernels for 1%

profile of v9, /device:TPU:1, one launch (start us, length us, event | category | flops | bytes accessed | tf_op | source)
XLA Modules:
  0.0 153.5 jit_solution(2797971575125855032)
XLA Ops:
  0.6 1.9 %left_terms.3 = f32[12,16,128]{2,1,0:T(8,128)} custom-call(s32[1]{0:T(128)} %bitcast.2.col_ref, f32[16,384]{1,0:T(8,128)} %bitcast.5, bf16[384,384]{1,0:T(8,128)(2,1)} %refs_3_.1), custom_call_target="tpu_custom_call" | custom-call | tf_op jit(solution)/shard_map/left_terms/pallas_call | solution.py:95
  2.5 15.7 %all-to-all-start = ((f32[12,16,128]{2,1,0:T(8,128)}), f32[12,16,128]{2,1,0:T(8,128)S(1)}, u32[]{:S(2)}, u32[]{:S(2)}) async-start(f32[12,16,128]{2,1,0:T(8,128)} %left_terms.3), calls=%async_computation | async-start | bytes 196608 | tf_op jit(solution)/shard_map/left_terms/all_to_all | solution.py:262
  18.3 5.1 %collective-permute-start = (bf16[128,1024]{1,0:T(8,128)(2,1)}, bf16[128,1024]{1,0:T(8,128)(2,1)S(1)}, u32[]{:S(2)}, u32[]{:S(2)}) collective-permute-start(bf16[128,1024]{1,0:T(8,128)(2,1)} %acts_ref.1), channel_id=1, source_target_pairs={{0,6},{6,0},{1,7},{7,1},{2,8},{8,2},{3,9},{9,3},{4,10},{10,4},{5,1... | collective-permute-start | bytes 786440 | tf_op jit(solution)/shard_map/gather_inputs/ppermute | solution.py:248
  23.4 1.4 copy-done
  24.8 0.7 copy-done.4
  25.5 0.8 left_terms.4.part_ref
  26.3 1.4 all-to-all-done.mine_ref
  27.7 0.8 left_terms.5
  28.5 6.9 %all-to-all-start.1 = ((f32[8,16,128]{2,1,0:T(8,128)}), f32[8,16,128]{2,1,0:T(8,128)S(1)}, u32[]{:S(2)}, u32[]{:S(2)}) async-start(f32[8,16,128]{2,1,0:T(8,128)} %left_terms.5), calls=%async_computation.1 | async-start | bytes 131072 | tf_op jit(solution)/shard_map/left_sum/all_to_all | solution.py:26
  35.3 7.5 %collective-permute-done = bf16[128,1024]{1,0:T(8,128)(2,1)S(1)} collective-permute-done((bf16[128,1024]{1,0:T(8,128)(2,1)}, bf16[128,1024]{1,0:T(8,128)(2,1)S(1)}, u32[]{:S(2)}, u32[]{:S(2)}) %collective-permute-start) | collective-permute-done | bytes 262176 | tf_op jit(solution)/shard_map/gather_inputs/ppermute | solution.py:248
  42.9 2.6 %collective-permute-start.2 = (bf16[256,1024]{1,0:T(8,128)(2,1)S(1)}, bf16[256,1024]{1,0:T(8,128)(2,1)S(1)}, u32[]{:S(2)}, u32[]{:S(2)}) collective-permute-start(bf16[256,1024]{1,0:T(8,128)(2,1)S(1)} %pad_maximum_fusion.refs_0_), channel_id=1, source_target_pairs={{0,4},{2,0},{4,2},{1,5},{3,1},{5,3},{6,10},{8,6},{10,8},{7,11},{9,... | collective-permute-start | bytes 1572872 | tf_op jit(solution)/shard_map/left_sum/ppermute | solution.py:269
  45.4 2.7 %collective-permute-start.1 = (bf16[256,1024]{1,0:T(8,128)(2,1)S(1)}, bf16[256,1024]{1,0:T(8,128)(2,1)S(1)}, u32[]{:S(2)}, u32[]{:S(2)}) collective-permute-start(bf16[256,1024]{1,0:T(8,128)(2,1)S(1)} %pad_maximum_fusion.refs_0_), channel_id=1, source_target_pairs={{0,2},{2,4},{4,0},{1,3},{3,5},{5,1},{6,8},{8,10},{10,6},{7,9},{9,1... | collective-permute-start | bytes 1572872 | tf_op jit(solution)/shard_map/left_sum/ppermute | solution.py:269
  48.2 9.1 %collective-permute-start.3 = (bf16[384,384]{1,0:T(8,128)(2,1)S(1)}, bf16[384,384]{1,0:T(8,128)(2,1)}, u32[]{:S(2)}, u32[]{:S(2)}) collective-permute-start(bf16[384,384]{1,0:T(8,128)(2,1)S(1)} %copy-done.2), channel_id=1, source_target_pairs={{0,1},{1,0},{2,3},{3,2},{4,5},{5,4},{6,7},{7,6},{8,9},{9,8},{10,11... | collective-permute-start | bytes 884744 | tf_op jit(solution)/shard_map/gather_inputs/ppermute | solution.py:250
  57.3 13.9 %all_to_all.40 = f32[8,16,128]{2,1,0:T(8,128)S(1)} all-to-all(f32[8,16,128]{2,1,0:T(8,128)S(1)} %broadcast_in_dim.15), channel_id=1, replica_groups=mesh['y'=8,'x'=4,'core'=2,'far'=2,'next'=3,'col'=2] {'y'}, dimensions={0} | all-to-all | bytes 131072 | tf_op jit(solution)/shard_map/left_sum/all_to_all | solution.py:18
  71.8 3.5 %all-to-all-start.3 = ((f32[6,16,128]{2,1,0:T(8,128)}), f32[6,16,128]{2,1,0:T(8,128)S(1)}, u32[]{:S(2)}, u32[]{:S(2)}) async-start(f32[6,16,128]{2,1,0:T(8,128)} %broadcast_in_dim.16), calls=%async_computation.3 | async-start | bytes 98304 | tf_op jit(solution)/shard_map/left_sum/all_to_all | solution.py:18
  75.2 18.7 %all-to-all-done.3 = f32[6,16,128]{2,1,0:T(8,128)S(1)} async-done(((f32[6,16,128]{2,1,0:T(8,128)}), f32[6,16,128]{2,1,0:T(8,128)S(1)}, u32[]{:S(2)}, u32[]{:S(2)}) %all-to-all-start.3) | async-done | bytes 49184 | tf_op jit(solution)/shard_map/left_sum/all_to_all | solution.py:18
  94.0 0.6 broadcast_in_dim.17
  94.6 5.1 %all-to-all-start.4 = ((f32[8,16,128]{2,1,0:T(8,128)}), f32[8,16,128]{2,1,0:T(8,128)S(1)}, u32[]{:S(2)}, u32[]{:S(2)}) async-start(f32[8,16,128]{2,1,0:T(8,128)} %broadcast_in_dim.17), calls=%async_computation.4 | async-start | bytes 131072 | tf_op jit(solution)/shard_map/left_sum/all_to_all | solution.py:18
  99.8 4.8 %all-to-all-done.4.refs_6_.left_ref = f32[8,16,128]{2,1,0:T(8,128)S(1)} async-done(((f32[8,16,128]{2,1,0:T(8,128)}), f32[8,16,128]{2,1,0:T(8,128)S(1)}, u32[]{:S(2)}, u32[]{:S(2)}) %all-to-all-start.4) | async-done | bytes 65568 | tf_op jit(solution)/shard_map/left_sum/all_to_all | solution.py:18
  104.6 3.5 %target.1 = (f32[1024,384]{1,0:T(8,128)}, f32[8,8,128]{2,1,0:T(8,128)S(1)}) custom-call(s32[2]{0:T(128)S(1)} %pad_add_fusion.place_ref, bf16[256,1024]{1,0:T(8,128)(2,1)S(1)} %pad_maximum_fusion.refs_0_, bf16[256,1024]{1,0:T(8,128)(2,1)S(1)} %collective-permute-done.1.refs_1_, bf16[256,1024]{1,0:T(8,128)(2,1)S(1)} %collective-permute-done.2.refs_2_, ...), custom_call_target="tpu_custom_call" | custom-call | tf_op jit(solution)/shard_map/target/pallas_call | solution.py:155
  108.1 7.9 %all_to_all.41 = f32[8,8,128]{2,1,0:T(8,128)S(1)} all-to-all(f32[8,8,128]{2,1,0:T(8,128)S(1)} %get-tuple-element.14), channel_id=1, replica_groups=mesh['y'=8,'x'=4,'core'=2,'far'=2,'next'=3,'col'=2] {'x','core'}, dimensions={0} | all-to-all | bytes 65536 | tf_op jit(solution)/shard_map/right_sum/all_to_all | solution.py:26
  116.0 24.3 %all_to_all.42 = f32[16,8,128]{2,1,0:T(8,128)S(1)} all-to-all(f32[16,8,128]{2,1,0:T(8,128)S(1)} %broadcast_in_dim.18), channel_id=1, replica_groups=mesh['y'=8,'x'=4,'core'=2,'far'=2,'next'=3,'col'=2] {'y','col'}, dimensions={0} | all-to-all | bytes 131072 | tf_op jit(solution)/shard_map/right_sum/all_to_all | solution.py:18
  140.3 9.2 %all_to_all.43.joint_ref = f32[8,8,128]{2,1,0:T(8,128)S(1)} all-to-all(f32[8,8,128]{2,1,0:T(8,128)S(1)} %broadcast_in_dim.19), channel_id=1, replica_groups=mesh['y'=8,'x'=4,'core'=2,'far'=2,'next'=3,'col'=2] {'x','core'}, dimensions={0} | all-to-all | bytes 65536 | tf_op jit(solution)/shard_map/right_sum/all_to_all | solution.py:18
  149.5 4.0 %finish.1 = (f32[1024,384]{1,0:T(8,128)}, f32[16,384]{1,0:T(8,128)}) custom-call(f32[8,8,128]{2,1,0:T(8,128)S(1)} %all_to_all.43.joint_ref, f32[8,16,128]{2,1,0:T(8,128)S(1)} %all-to-all-done.4.refs_6_.left_ref, f32[1024,384]{1,0:T(8,128)} %get-tuple-element.15.target_ref), custom_call_target="tpu_custom_call", output_to_operand_aliasing={{0}: (2, {})} | custom-call | tf_op jit(solution)/shard_map/finish/pallas_call | solution.py:219
  (23 shorter events, 0.8 us)
Async XLA Ops:
  0.6 27.0 %copy-start.3 = (bf16[128,1024]{1,0:T(8,128)(2,1)S(1)}, bf16[128,1024]{1,0:T(8,128)(2,1)}, u32[]{:S(2)}) copy-start(bf16[128,1024]{1,0:T(8,128)(2,1)} %acts_ref.1) | copy-start | bytes 786436
  2.5 25.1 %all-to-all-start = ((f32[12,16,128]{2,1,0:T(8,128)}), f32[12,16,128]{2,1,0:T(8,128)S(1)}, u32[]{:S(2)}, u32[]{:S(2)}) async-start(f32[12,16,128]{2,1,0:T(8,128)} %left_terms.3), calls=%async_computation | async-start | bytes 196608 | tf_op jit(solution)/shard_map/left_terms/all_to_all | solution.py:262
  18.3 24.5 %collective-permute-start = (bf16[128,1024]{1,0:T(8,128)(2,1)}, bf16[128,1024]{1,0:T(8,128)(2,1)S(1)}, u32[]{:S(2)}, u32[]{:S(2)}) collective-permute-start(bf16[128,1024]{1,0:T(8,128)(2,1)} %acts_ref.1), channel_id=1, source_target_pairs={{0,6},{6,0},{1,7},{7,1},{2,8},{8,2},{3,9},{9,3},{4,10},{10,4},{5,1... | collective-permute-start | bytes 786440 | tf_op jit(solution)/shard_map/gather_inputs/ppermute | solution.py:248
  23.4 1.4 copy-start
  24.8 0.7 copy-start.4
  25.5 22.6 %copy-start.2 = (bf16[384,384]{1,0:T(8,128)(2,1)S(1)}, bf16[384,384]{1,0:T(8,128)(2,1)}, u32[]{:S(2)}) copy-start(bf16[384,384]{1,0:T(8,128)(2,1)} %refs_3_.1) | copy-start | bytes 884740
  26.3 78.2 %copy-start.1 = (f32[1024,384]{1,0:T(8,128)S(1)}, f32[1024,384]{1,0:T(8,128)}, u32[]{:S(2)}) copy-start(f32[1024,384]{1,0:T(8,128)} %refs_5_.1) | copy-start | bytes 4718596
  28.5 14.3 %all-to-all-start.1 = ((f32[8,16,128]{2,1,0:T(8,128)}), f32[8,16,128]{2,1,0:T(8,128)S(1)}, u32[]{:S(2)}, u32[]{:S(2)}) async-start(f32[8,16,128]{2,1,0:T(8,128)} %left_terms.5), calls=%async_computation.1 | async-start | bytes 131072 | tf_op jit(solution)/shard_map/left_sum/all_to_all | solution.py:26
  42.9 61.7 %collective-permute-start.2 = (bf16[256,1024]{1,0:T(8,128)(2,1)S(1)}, bf16[256,1024]{1,0:T(8,128)(2,1)S(1)}, u32[]{:S(2)}, u32[]{:S(2)}) collective-permute-start(bf16[256,1024]{1,0:T(8,128)(2,1)S(1)} %pad_maximum_fusion.refs_0_), channel_id=1, source_target_pairs={{0,4},{2,0},{4,2},{1,5},{3,1},{5,3},{6,10},{8,6},{10,8},{7,11},{9,... | collective-permute-start | bytes 1572872 | tf_op jit(solution)/shard_map/left_sum/ppermute | solution.py:269
  45.4 59.1 %collective-permute-start.1 = (bf16[256,1024]{1,0:T(8,128)(2,1)S(1)}, bf16[256,1024]{1,0:T(8,128)(2,1)S(1)}, u32[]{:S(2)}, u32[]{:S(2)}) collective-permute-start(bf16[256,1024]{1,0:T(8,128)(2,1)S(1)} %pad_maximum_fusion.refs_0_), channel_id=1, source_target_pairs={{0,2},{2,4},{4,0},{1,3},{3,5},{5,1},{6,8},{8,10},{10,6},{7,9},{9,1... | collective-permute-start | bytes 1572872 | tf_op jit(solution)/shard_map/left_sum/ppermute | solution.py:269
  48.2 45.8 %collective-permute-start.3 = (bf16[384,384]{1,0:T(8,128)(2,1)S(1)}, bf16[384,384]{1,0:T(8,128)(2,1)}, u32[]{:S(2)}, u32[]{:S(2)}) collective-permute-start(bf16[384,384]{1,0:T(8,128)(2,1)S(1)} %copy-done.2), channel_id=1, source_target_pairs={{0,1},{1,0},{2,3},{3,2},{4,5},{5,4},{6,7},{7,6},{8,9},{9,8},{10,11... | collective-permute-start | bytes 884744 | tf_op jit(solution)/shard_map/gather_inputs/ppermute | solution.py:250
  71.8 22.2 %all-to-all-start.3 = ((f32[6,16,128]{2,1,0:T(8,128)}), f32[6,16,128]{2,1,0:T(8,128)S(1)}, u32[]{:S(2)}, u32[]{:S(2)}) async-start(f32[6,16,128]{2,1,0:T(8,128)} %broadcast_in_dim.16), calls=%async_computation.3 | async-start | bytes 98304 | tf_op jit(solution)/shard_map/left_sum/all_to_all | solution.py:18
  94.6 9.9 %all-to-all-start.4 = ((f32[8,16,128]{2,1,0:T(8,128)}), f32[8,16,128]{2,1,0:T(8,128)S(1)}, u32[]{:S(2)}, u32[]{:S(2)}) async-start(f32[8,16,128]{2,1,0:T(8,128)} %broadcast_in_dim.17), calls=%async_computation.4 | async-start | bytes 131072 | tf_op jit(solution)/shard_map/left_sum/all_to_all | solution.py:18

commit v10 on v9

--- a/solution.py
+++ b/solution.py
@@ -102,10 +102,9 @@
     )(*args)
 
 
-def target_kernel(replicas, n_pieces, place_ref, *refs):
+def target_kernel(n_pieces, place_ref, *refs):
     pieces, refs = refs[:n_pieces], refs[n_pieces:]
-    mine_ref, other_ref, err_ref, left_ref, target_ref, joint_ref, grads, target, sems = refs
-    rank = left_ref.shape[1]
+    mine_ref, other_ref, err_ref, target_ref, grads, target, sems = refs
     wide = 256
     depth = pieces[0].shape[0]
     chunk = depth // 2
@@ -116,6 +115,49 @@
         mine, other = mine_ref[source], other_ref[source]
         grads[k * depth : k * depth + chunk] = jnp.where(same, mine, other)
         grads[k * depth + chunk : (k + 1) * depth] = jnp.where(same, other, mine)
+    copies = []
+    for k in range(err_ref.shape[0] // wide):
+        span = slice(k * wide, (k + 1) * wide)
+        tile = err_ref[span]
+        for n, piece in enumerate(pieces):
+            tile += mxu(piece[:, span], grads[n * depth : (n + 1) * depth], ((0,), (0,)))
+        target[span] = tile
+        copies.append(pltpu.make_async_copy(target.at[span], target_ref.at[span], sems.at[k]))
+        copies[-1].start()
+    for copy in copies:
+        copy.wait()
+
+
+def target_of(pieces, mine, other, err, place):
+    rows, cols = err.shape
+    in_vmem = pl.BlockSpec(memory_space=pltpu.VMEM)
+    return pl.pallas_call(
+        functools.partial(target_kernel, len(pieces)),
+        in_specs=[pl.BlockSpec(memory_space=pltpu.SMEM)] + [in_vmem] * (3 + len(pieces)),
+        out_specs=pl.BlockSpec(memory_space=pl.ANY),
+        out_shape=jax.ShapeDtypeStruct((rows, cols), jnp.float32),
+        scratch_shapes=[
+            pltpu.VMEM((2 * mine.shape[0], cols), mine.dtype),
+            pltpu.VMEM((rows, cols), jnp.float32),
+            pltpu.SemaphoreType.DMA((rows // 256,)),
+        ],
+        compiler_params=pltpu.CompilerParams(vmem_limit_bytes=16 * 2**20),
+        cost_estimate=pl.CostEstimate(
+            flops=2 * rows * cols * 2 * mine.shape[0], bytes_accessed=8 * rows * cols, transcendentals=0
+        ),
+    )(place, *pieces, mine, other, err)
+
+
+def terms_kernel(replicas, left_ref, target_ref, joint_ref, target, sems):
+    rank = left_ref.shape[1]
+    wide = target.shape[0] // sems.shape[0]
+    spans = [slice(k * wide, (k + 1) * wide) for k in range(sems.shape[0])]
+    loads = [
+        pltpu.make_async_copy(target_ref.at[span], target.at[span], sems.at[k])
+        for k, span in enumerate(spans)
+    ]
+    for load in loads:
+        load.start()
     left = lanes(left_ref, 0, left_ref.shape[0])
     stack = jnp.concatenate(thirds(left), axis=0)
     gram = lax.dot_general(
@@ -125,48 +167,32 @@
         precision=HIGHEST,
         preferred_element_type=jnp.float32,
     )
-    sums, copies = None, []
-    for k in range(err_ref.shape[0] // wide):
-        span = slice(k * wide, (k + 1) * wide)
-        tile = err_ref[span]
-        for n, piece in enumerate(pieces):
-            tile += mxu(piece[:, span], grads[n * depth : (n + 1) * depth], ((0,), (0,)))
-        target[span] = tile
-        copies.append(pltpu.make_async_copy(target.at[span], target_ref.at[span], sems.at[k]))
-        copies[-1].start()
-        high, mid, low = thirds(tile)
+    right = None
+    for load, span in zip(loads, spans):
+        load.wait()
+        high, mid, low = thirds(target[span])
         terms = mxu(stack[:, span], high, ((1,), (0,))) + mxu(stack[:, span], mid, ((1,), (0,)))
-        right = joined(terms, rank) + mxu(stack[:rank, span], low, ((1,), (0,)))
-        sums = right if sums is None else sums + right
+        terms = joined(terms, rank) + mxu(stack[:rank, span], low, ((1,), (0,)))
+        right = terms if right is None else right + terms
     gram = jnp.concatenate([gram, jnp.zeros((rank, 128 - rank), jnp.float32)], axis=1) / replicas
-    both = jnp.concatenate([sums, gram], axis=1)
+    both = jnp.concatenate([right, gram], axis=1)
     for k in range(joint_ref.shape[0]):
         first, at = (k % 2) * (rank // 2), (k // 2) * 128
         joint_ref[k] = both[first : first + rank // 2, at : at + 128]
-    for copy in copies:
-        copy.wait()
-
-
-def target_and_terms(pieces, mine, other, err, left, place, replicas):
-    rows, cols = err.shape
+
+
+def terms_of(left, target, replicas):
+    rows, cols = target.shape
     rank = left.shape[1]
-    tiles = cols // 128 + 1
     in_vmem = pl.BlockSpec(memory_space=pltpu.VMEM)
     return pl.pallas_call(
-        functools.partial(target_kernel, replicas, len(pieces)),
-        in_specs=[pl.BlockSpec(memory_space=pltpu.SMEM)] + [in_vmem] * (4 + len(pieces)),
-        out_specs=[pl.BlockSpec(memory_space=pl.ANY), in_vmem],
-        out_shape=[
-            jax.ShapeDtypeStruct((rows, cols), jnp.float32),
-            jax.ShapeDtypeStruct((2 * tiles, rank // 2, 128), jnp.float32),
-        ],
-        scratch_shapes=[
-            pltpu.VMEM((2 * mine.shape[0], cols), mine.dtype),
-            pltpu.VMEM((rows, cols), jnp.float32),
-            pltpu.SemaphoreType.DMA((rows // 256,)),
-        ],
-        compiler_params=pltpu.CompilerParams(vmem_limit_bytes=16 * 2**20),
-    )(place, *pieces, mine, other, err, left)
+        functools.partial(terms_kernel, replicas),
+        in_specs=[in_vmem, pl.BlockSpec(memory_space=pl.ANY)],
+        out_specs=in_vmem,
+        out_shape=jax.ShapeDtypeStruct((2 * (cols // 128 + 1), rank // 2, 128), jnp.float32),
+        scratch_shapes=[pltpu.VMEM((rows, cols), jnp.float32), pltpu.SemaphoreType.DMA((4,))],
+        compiler_params=pltpu.CompilerParams(vmem_limit_bytes=56 * 2**20),
+    )(left, target)
 
 
 def finish_kernel(
@@ -264,24 +290,18 @@
         blocks = local_call(left_kernel, (n_near, rank, rows // n_near), mine, acts, part)
 
     with jax.named_scope("left_sum"):
+        blocks, pair = lax.optimization_barrier((blocks, pair))
+        pieces = [pair, *(lax.ppermute(pair, "next", shifted(n_next, k)) for k in range(1, n_next))]
         part = split_and_summed(blocks, NEAR)
-        part, pair = lax.optimization_barrier((part, pair))
-        pieces = [pair, *(lax.ppermute(pair, "next", shifted(n_next, k)) for k in range(1, n_next))]
         part = summed_over(part, "y")
         part = summed_over(part, ROW)
         part, other = lax.optimization_barrier((part, other))
         left = to_all(part, NEAR)
 
     with jax.named_scope("target"):
-        target, joint = target_and_terms(
-            pieces,
-            grads,
-            other,
-            err,
-            left,
-            jnp.stack([(col == lax.axis_index("far")).astype(jnp.int32), lax.axis_index("next")]),
-            replicas,
-        )
+        place = jnp.stack([(col == lax.axis_index("far")).astype(jnp.int32), lax.axis_index("next")])
+        target = target_of(pieces, grads, other, err, place)
+        joint = terms_of(left, target, replicas)
 
     with jax.named_scope("right_sum"):
         part = split_and_summed(joint, NEAR)

time: 154 us -> 150 us (0.974)
  waiting for transfers between devices: 32.3 us -> 28.1 us
  starting transfers between devices: 50.6 us -> 47.7 us
  Pallas kernels: 11 us -> 13.5 us
  blocking collectives: 55.3 us -> 53.1 us
    all_to_all x1, waiting for transfers between devices: 1.36 us -> 12.2 us  [body(): lax.all_to_all(sends, (*ROW, 'col'), split_axis=0, concat_axis=0, tiled=T...]
    all_to_all x2, waiting for transfers between devices: 23.5 us -> 15.9 us  [to_all(): return lax.all_to_all(copies, axes, split_axis=0, concat_axis=0, tiled=True)]
    ppermute x1, waiting for transfers between devices: 7.45 us -> 0.01 us  [body(): swapped = lax.ppermute(acts, 'far', [(0, 1), (1, 0)])]
    ppermute x1, starting transfers between devices: 9.08 us -> 5.33 us  [body(): other = lax.ppermute(grads, 'col', [(0, 1), (1, 0)])]
    all_to_all x1, starting transfers between devices: 15.7 us -> 12.2 us  [body(): lax.all_to_all(sends, (*ROW, 'col'), split_axis=0, concat_axis=0, tiled=T...]
    ppermute x1, starting transfers between devices: 5.13 us -> 8.58 us  [body(): swapped = lax.ppermute(acts, 'far', [(0, 1), (1, 0)])]
    all_to_all x3, blocking collectives: 47.4 us -> 44.3 us  [to_all(): return lax.all_to_all(copies, axes, split_axis=0, concat_axis=0, tiled=True)]
    pallas_call x1 -> x2, Pallas kernels: 3.54 us -> 6.1 us  [the longest x1 3.32 us: terms_of(): pl.pallas_call(functools.partial(terms_kernel, replicas), in_specs=[in_vm...]
  transfers between devices with their start and end apart: 8 -> 8, of which waited for: 4 -> 3; matrix products, arithmetic and copies ran while one was open for 1% -> 1% of each run, Pallas kernels for 1% -> 4%
where the time goes in v10:
time: 150 us; the launch traced here: 148 us
  blocking collectives  53.1 us (35%)
  starting transfers between devices  47.7 us (32%)
  waiting for transfers between devices  28.1 us (19%)
  Pallas kernels  13.5 us (9%)
  local copies, waits for them, and re-layouts  4.88 us (3%)
    all_to_all x3, blocking collectives, to_all(): return lax.all_to_all(copies, axes, split_axis=0, concat_axis=0, tiled=True)  44.3 us
    all_to_all x2, waiting for transfers between devices, to_all(): return lax.all_to_all(copies, axes, split_axis=0, concat_axis=0, tiled=True)  15.9 us
    all_to_all x1, waiting for transfers between devices, body(): lax.all_to_all(sends, (*ROW, 'col'), split_axis=0, concat_axis=0, tiled=T...  12.2 us
    all_to_all x1, starting transfers between devices, body(): lax.all_to_all(sends, (*ROW, 'col'), split_axis=0, concat_axis=0, tiled=T...  12.2 us
    all_to_all x1, blocking collectives, split_and_summed(): lax.all_to_all(blocks, axes, split_axis=0, concat_axis=0, tiled=True)  8.73 us
    ppermute x1, starting transfers between devices, body(): swapped = lax.ppermute(acts, 'far', [(0, 1), (1, 0)])  8.58 us
    all_to_all x2, starting transfers between devices, to_all(): return lax.all_to_all(copies, axes, split_axis=0, concat_axis=0, tiled=True)  8.49 us
    all_to_all x1, starting transfers between devices, split_and_summed(): lax.all_to_all(blocks, axes, split_axis=0, concat_axis=0, tiled=True)  6.95 us
  transfers between devices with their start and end apart: 8, of which 3 were waited for; matrix products, arithmetic and copies ran while one was open for 1% of the time, Pallas kernels for 4%

profile of v10, /device:TPU:1, one launch (start us, length us, event | category | flops | bytes accessed | tf_op | source)
XLA Modules:
  0.0 148.2 jit_solution(2217397270527780634)
XLA Ops:
  0.6 8.6 %collective-permute-start = (bf16[128,1024]{1,0:T(8,128)(2,1)}, bf16[128,1024]{1,0:T(8,128)(2,1)S(1)}, u32[]{:S(2)}, u32[]{:S(2)}) collective-permute-start(bf16[128,1024]{1,0:T(8,128)(2,1)} %acts_ref.1), channel_id=1, source_target_pairs={{0,6},{6,0},{1,7},{7,1},{2,8},{8,2},{3,9},{9,3},{4,10},{10,4},{5,1... | collective-permute-start | bytes 786440 | tf_op jit(solution)/shard_map/gather_inputs/ppermute | solution.py:274
  9.2 1.9 %left_terms.3 = f32[12,16,128]{2,1,0:T(8,128)} custom-call(s32[1]{0:T(128)} %bitcast.col_ref, f32[16,384]{1,0:T(8,128)} %bitcast.5, bf16[384,384]{1,0:T(8,128)(2,1)} %refs_3_.1), custom_call_target="tpu_custom_call" | custom-call | tf_op jit(solution)/shard_map/left_terms/pallas_call | solution.py:95
  11.1 12.2 %all-to-all-start = ((f32[12,16,128]{2,1,0:T(8,128)}), f32[12,16,128]{2,1,0:T(8,128)S(1)}, u32[]{:S(2)}, u32[]{:S(2)}) async-start(f32[12,16,128]{2,1,0:T(8,128)} %left_terms.3), calls=%async_computation | async-start | bytes 196608 | tf_op jit(solution)/shard_map/left_terms/all_to_all | solution.py:288
  23.3 1.4 copy-done
  24.7 0.7 copy-done.6
  25.4 0.8 left_terms.4.part_ref
  26.3 12.2 %all-to-all-done.mine_ref = f32[12,16,128]{2,1,0:T(8,128)S(1)} async-done(((f32[12,16,128]{2,1,0:T(8,128)}), f32[12,16,128]{2,1,0:T(8,128)S(1)}, u32[]{:S(2)}, u32[]{:S(2)}) %all-to-all-start) | async-done | bytes 98336 | tf_op jit(solution)/shard_map/left_terms/all_to_all | solution.py:288
  38.5 0.8 left_terms.5
  39.3 2.8 %collective-permute-start.2 = (bf16[256,1024]{1,0:T(8,128)(2,1)S(1)}, bf16[256,1024]{1,0:T(8,128)(2,1)S(1)}, u32[]{:S(2)}, u32[]{:S(2)}) collective-permute-start(bf16[256,1024]{1,0:T(8,128)(2,1)S(1)} %pad_maximum_fusion.refs_0_), channel_id=1, source_target_pairs={{0,2},{2,4},{4,0},{1,3},{3,5},{5,1},{6,8},{8,10},{10,6},{7,9},{9,1... | collective-permute-start | bytes 1572872 | tf_op jit(solution)/shard_map/left_sum/ppermute | solution.py:294
  42.1 3.3 %collective-permute-start.3 = (bf16[256,1024]{1,0:T(8,128)(2,1)S(1)}, bf16[256,1024]{1,0:T(8,128)(2,1)S(1)}, u32[]{:S(2)}, u32[]{:S(2)}) collective-permute-start(bf16[256,1024]{1,0:T(8,128)(2,1)S(1)} %pad_maximum_fusion.refs_0_), channel_id=1, source_target_pairs={{0,4},{2,0},{4,2},{1,5},{3,1},{5,3},{6,10},{8,6},{10,8},{7,11},{9,... | collective-permute-start | bytes 1572872 | tf_op jit(solution)/shard_map/left_sum/ppermute | solution.py:294
  45.5 7.0 %all-to-all-start.1 = ((f32[8,16,128]{2,1,0:T(8,128)}), f32[8,16,128]{2,1,0:T(8,128)S(1)}, u32[]{:S(2)}, u32[]{:S(2)}) async-start(f32[8,16,128]{2,1,0:T(8,128)} %left_terms.5), calls=%async_computation.1 | async-start | bytes 131072 | tf_op jit(solution)/shard_map/left_sum/all_to_all | solution.py:26
  52.4 5.3 %collective-permute-start.1 = (bf16[384,384]{1,0:T(8,128)(2,1)S(1)}, bf16[384,384]{1,0:T(8,128)(2,1)}, u32[]{:S(2)}, u32[]{:S(2)}) collective-permute-start(bf16[384,384]{1,0:T(8,128)(2,1)S(1)} %copy-done.2), channel_id=1, source_target_pairs={{0,1},{1,0},{2,3},{3,2},{4,5},{5,4},{6,7},{7,6},{8,9},{9,8},{10,11... | collective-permute-start | bytes 884744 | tf_op jit(solution)/shard_map/gather_inputs/ppermute | solution.py:276
  57.8 13.9 %all_to_all.40 = f32[8,16,128]{2,1,0:T(8,128)S(1)} all-to-all(f32[8,16,128]{2,1,0:T(8,128)S(1)} %broadcast_in_dim.15), channel_id=1, replica_groups=mesh['y'=8,'x'=4,'core'=2,'far'=2,'next'=3,'col'=2] {'y'}, dimensions={0} | all-to-all | bytes 131072 | tf_op jit(solution)/shard_map/left_sum/all_to_all | solution.py:18
  72.3 3.6 %all-to-all-start.3 = ((f32[6,16,128]{2,1,0:T(8,128)}), f32[6,16,128]{2,1,0:T(8,128)S(1)}, u32[]{:S(2)}, u32[]{:S(2)}) async-start(f32[6,16,128]{2,1,0:T(8,128)} %broadcast_in_dim.16), calls=%async_computation.3 | async-start | bytes 98304 | tf_op jit(solution)/shard_map/left_sum/all_to_all | solution.py:18
  75.9 13.9 %all-to-all-done.3 = f32[6,16,128]{2,1,0:T(8,128)S(1)} async-done(((f32[6,16,128]{2,1,0:T(8,128)}), f32[6,16,128]{2,1,0:T(8,128)S(1)}, u32[]{:S(2)}, u32[]{:S(2)}) %all-to-all-start.3) | async-done | bytes 49184 | tf_op jit(solution)/shard_map/left_sum/all_to_all | solution.py:18
  90.5 4.9 %all-to-all-start.4 = ((f32[8,16,128]{2,1,0:T(8,128)}), f32[8,16,128]{2,1,0:T(8,128)S(1)}, u32[]{:S(2)}, u32[]{:S(2)}) async-start(f32[8,16,128]{2,1,0:T(8,128)} %broadcast_in_dim.17), calls=%async_computation.4 | async-start | bytes 131072 | tf_op jit(solution)/shard_map/left_sum/all_to_all | solution.py:18
  95.4 2.8 %target.2.target_ref = f32[1024,384]{1,0:T(8,128)} custom-call(s32[2]{0:T(128)S(1)} %pad_add_fusion.place_ref, bf16[256,1024]{1,0:T(8,128)(2,1)S(1)} %pad_maximum_fusion.refs_0_, bf16[256,1024]{1,0:T(8,128)(2,1)S(1)} %collective-permute-done.2.refs_1_, bf16[256,1024]{1,0:T(8,128)(2,1)S(1)} %collective-permute-done.3.refs_2_, bf16[384,384]{1,0:T(8,128)(2,1)S(1)} %copy-done.2, ...), custom_call_target="tpu_custom_call" | custom-call | flops 603979776 | bytes 3145728 | tf_op jit(solution)/shard_map/target/pallas_call | solution.py:134
  98.2 2.0 %all-to-all-done.4.left_ref = f32[8,16,128]{2,1,0:T(8,128)S(1)} async-done(((f32[8,16,128]{2,1,0:T(8,128)}), f32[8,16,128]{2,1,0:T(8,128)S(1)}, u32[]{:S(2)}, u32[]{:S(2)}) %all-to-all-start.4) | async-done | bytes 65568 | tf_op jit(solution)/shard_map/left_sum/all_to_all | solution.py:18
  100.8 3.3 %target.3 = f32[8,8,128]{2,1,0:T(8,128)} custom-call(f32[8,16,128]{2,1,0:T(8,128)} %copy-done.4, f32[1024,384]{1,0:T(8,128)} %target.2.target_ref), custom_call_target="tpu_custom_call" | custom-call | tf_op jit(solution)/shard_map/target/pallas_call | solution.py:188
  104.1 8.7 %all_to_all.41 = f32[8,8,128]{2,1,0:T(8,128)S(1)} all-to-all(f32[8,8,128]{2,1,0:T(8,128)} %target.3), channel_id=1, replica_groups=mesh['y'=8,'x'=4,'core'=2,'far'=2,'next'=3,'col'=2] {'x','core'}, dimensions={0} | all-to-all | bytes 65536 | tf_op jit(solution)/shard_map/right_sum/all_to_all | solution.py:26
  112.9 21.3 %all_to_all.42 = f32[16,8,128]{2,1,0:T(8,128)S(1)} all-to-all(f32[16,8,128]{2,1,0:T(8,128)S(1)} %broadcast_in_dim.18), channel_id=1, replica_groups=mesh['y'=8,'x'=4,'core'=2,'far'=2,'next'=3,'col'=2] {'y','col'}, dimensions={0} | all-to-all | bytes 131072 | tf_op jit(solution)/shard_map/right_sum/all_to_all | solution.py:18
  134.2 9.2 %all_to_all.43.joint_ref = f32[8,8,128]{2,1,0:T(8,128)S(1)} all-to-all(f32[8,8,128]{2,1,0:T(8,128)S(1)} %broadcast_in_dim.19), channel_id=1, replica_groups=mesh['y'=8,'x'=4,'core'=2,'far'=2,'next'=3,'col'=2] {'x','core'}, dimensions={0} | all-to-all | bytes 65536 | tf_op jit(solution)/shard_map/right_sum/all_to_all | solution.py:18
  143.4 0.8 copy-done.5
  144.2 4.0 %finish.1 = (f32[1024,384]{1,0:T(8,128)}, f32[16,384]{1,0:T(8,128)}) custom-call(f32[8,8,128]{2,1,0:T(8,128)S(1)} %all_to_all.43.joint_ref, f32[8,16,128]{2,1,0:T(8,128)S(1)} %copy-done.5, f32[1024,384]{1,0:T(8,128)} %target.2.target_ref), custom_call_target="tpu_custom_call", output_to_operand_aliasing={{0}: (2, {})} | custom-call | tf_op jit(solution)/shard_map/finish/pallas_call | solution.py:245
  (28 shorter events, 2.1 us)
Async XLA Ops:
  0.6 25.6 %copy-start.3 = (bf16[128,1024]{1,0:T(8,128)(2,1)S(1)}, bf16[128,1024]{1,0:T(8,128)(2,1)}, u32[]{:S(2)}) copy-start(bf16[128,1024]{1,0:T(8,128)(2,1)} %acts_ref.1) | copy-start | bytes 786436
  0.6 25.6 %collective-permute-start = (bf16[128,1024]{1,0:T(8,128)(2,1)}, bf16[128,1024]{1,0:T(8,128)(2,1)S(1)}, u32[]{:S(2)}, u32[]{:S(2)}) collective-permute-start(bf16[128,1024]{1,0:T(8,128)(2,1)} %acts_ref.1), channel_id=1, source_target_pairs={{0,6},{6,0},{1,7},{7,1},{2,8},{8,2},{3,9},{9,3},{4,10},{10,4},{5,1... | collective-permute-start | bytes 786440 | tf_op jit(solution)/shard_map/gather_inputs/ppermute | solution.py:274
  11.1 27.4 %all-to-all-start = ((f32[12,16,128]{2,1,0:T(8,128)}), f32[12,16,128]{2,1,0:T(8,128)S(1)}, u32[]{:S(2)}, u32[]{:S(2)}) async-start(f32[12,16,128]{2,1,0:T(8,128)} %left_terms.3), calls=%async_computation | async-start | bytes 196608 | tf_op jit(solution)/shard_map/left_terms/all_to_all | solution.py:288
  23.3 1.4 copy-start
  24.7 0.7 copy-start.6
  25.4 27.0 %copy-start.2 = (bf16[384,384]{1,0:T(8,128)(2,1)S(1)}, bf16[384,384]{1,0:T(8,128)(2,1)}, u32[]{:S(2)}) copy-start(bf16[384,384]{1,0:T(8,128)(2,1)} %refs_3_.1) | copy-start | bytes 884740
  26.2 69.2 %copy-start.1 = (f32[1024,384]{1,0:T(8,128)S(1)}, f32[1024,384]{1,0:T(8,128)}, u32[]{:S(2)}) copy-start(f32[1024,384]{1,0:T(8,128)} %refs_5_.1) | copy-start | bytes 4718596
  39.3 56.1 %collective-permute-start.2 = (bf16[256,1024]{1,0:T(8,128)(2,1)S(1)}, bf16[256,1024]{1,0:T(8,128)(2,1)S(1)}, u32[]{:S(2)}, u32[]{:S(2)}) collective-permute-start(bf16[256,1024]{1,0:T(8,128)(2,1)S(1)} %pad_maximum_fusion.refs_0_), channel_id=1, source_target_pairs={{0,2},{2,4},{4,0},{1,3},{3,5},{5,1},{6,8},{8,10},{10,6},{7,9},{9,1... | collective-permute-start | bytes 1572872 | tf_op jit(solution)/shard_map/left_sum/ppermute | solution.py:294
  42.1 53.3 %collective-permute-start.3 = (bf16[256,1024]{1,0:T(8,128)(2,1)S(1)}, bf16[256,1024]{1,0:T(8,128)(2,1)S(1)}, u32[]{:S(2)}, u32[]{:S(2)}) collective-permute-start(bf16[256,1024]{1,0:T(8,128)(2,1)S(1)} %pad_maximum_fusion.refs_0_), channel_id=1, source_target_pairs={{0,4},{2,0},{4,2},{1,5},{3,1},{5,3},{6,10},{8,6},{10,8},{7,11},{9,... | collective-permute-start | bytes 1572872 | tf_op jit(solution)/shard_map/left_sum/ppermute | solution.py:294
  45.5 12.3 %all-to-all-start.1 = ((f32[8,16,128]{2,1,0:T(8,128)}), f32[8,16,128]{2,1,0:T(8,128)S(1)}, u32[]{:S(2)}, u32[]{:S(2)}) async-start(f32[8,16,128]{2,1,0:T(8,128)} %left_terms.5), calls=%async_computation.1 | async-start | bytes 131072 | tf_op jit(solution)/shard_map/left_sum/all_to_all | solution.py:26
  52.4 37.4 %collective-permute-start.1 = (bf16[384,384]{1,0:T(8,128)(2,1)S(1)}, bf16[384,384]{1,0:T(8,128)(2,1)}, u32[]{:S(2)}, u32[]{:S(2)}) collective-permute-start(bf16[384,384]{1,0:T(8,128)(2,1)S(1)} %copy-done.2), channel_id=1, source_target_pairs={{0,1},{1,0},{2,3},{3,2},{4,5},{5,4},{6,7},{7,6},{8,9},{9,8},{10,11... | collective-permute-start | bytes 884744 | tf_op jit(solution)/shard_map/gather_inputs/ppermute | solution.py:276
  72.3 17.5 %all-to-all-start.3 = ((f32[6,16,128]{2,1,0:T(8,128)}), f32[6,16,128]{2,1,0:T(8,128)S(1)}, u32[]{:S(2)}, u32[]{:S(2)}) async-start(f32[6,16,128]{2,1,0:T(8,128)} %broadcast_in_dim.16), calls=%async_computation.3 | async-start | bytes 98304 | tf_op jit(solution)/shard_map/left_sum/all_to_all | solution.py:18
  90.5 9.7 %all-to-all-start.4 = ((f32[8,16,128]{2,1,0:T(8,128)}), f32[8,16,128]{2,1,0:T(8,128)S(1)}, u32[]{:S(2)}, u32[]{:S(2)}) async-start(f32[8,16,128]{2,1,0:T(8,128)} %broadcast_in_dim.17), calls=%async_computation.4 | async-start | bytes 131072 | tf_op jit(solution)/shard_map/left_sum/all_to_all | solution.py:18
  100.2 0.6 copy-start.4
  143.4 0.8 copy-start.5

commit v11 on v9

--- a/solution.py
+++ b/solution.py
@@ -245,8 +245,6 @@
     right_t = right.T
 
     with jax.named_scope("gather_inputs"):
-        swapped = lax.ppermute(acts, "far", [(0, 1), (1, 0)])
-        pair = jnp.concatenate([acts, swapped], axis=0)
         other = lax.ppermute(grads, "col", [(0, 1), (1, 0)])
 
     with jax.named_scope("left_terms"):
@@ -260,16 +258,19 @@
             limit=56,
         )
         mine = lax.all_to_all(sends, (*ROW, "col"), split_axis=0, concat_axis=0, tiled=True)
+        mine, own = lax.optimization_barrier((mine, acts))
+        swapped = lax.ppermute(own, "far", [(0, 1), (1, 0)])
+        pair = jnp.concatenate([acts, swapped], axis=0)
         part = local_call(error_kernel, (rank, rows), right_t, err)
         blocks = local_call(left_kernel, (n_near, rank, rows // n_near), mine, acts, part)
 
     with jax.named_scope("left_sum"):
         part = split_and_summed(blocks, NEAR)
+        part, other = lax.optimization_barrier((part, other))
+        part = summed_over(part, "y")
         part, pair = lax.optimization_barrier((part, pair))
         pieces = [pair, *(lax.ppermute(pair, "next", shifted(n_next, k)) for k in range(1, n_next))]
-        part = summed_over(part, "y")
         part = summed_over(part, ROW)
-        part, other = lax.optimization_barrier((part, other))
         left = to_all(part, NEAR)
 
     with jax.named_scope("target"):

time: 154 us -> 160 us (1.039)
  blocking collectives: 55.3 us -> 71.9 us
  waiting for transfers between devices: 32.3 us -> 21.4 us
  local copies, waits for them, and re-layouts: 3.43 us -> 5.09 us
    all_to_all x1 -> x2, blocking collectives: 7.86 us -> 19.9 us  [split_and_summed(): lax.all_to_all(blocks, axes, split_axis=0, concat_axis=0, tiled=True)]
    all_to_all x1 -> x0, starting transfers between devices: 6.85 us -> none  [split_and_summed(): lax.all_to_all(blocks, axes, split_axis=0, concat_axis=0, tiled=True)]
    all_to_all x2, starting transfers between devices: 8.55 us -> 15.3 us  [to_all(): return lax.all_to_all(copies, axes, split_axis=0, concat_axis=0, tiled=True)]
    all_to_all x2, waiting for transfers between devices: 23.5 us -> 16.9 us  [to_all(): return lax.all_to_all(copies, axes, split_axis=0, concat_axis=0, tiled=True)]
    all_to_all x3, blocking collectives: 47.4 us -> 52 us  [to_all(): return lax.all_to_all(copies, axes, split_axis=0, concat_axis=0, tiled=True)]
    ppermute x1, waiting for transfers between devices: 7.45 us -> 3.71 us  [body(): swapped = lax.ppermute(own, 'far', [(0, 1), (1, 0)])]
    ppermute x1, starting transfers between devices: 5.13 us -> 2.62 us  [body(): swapped = lax.ppermute(own, 'far', [(0, 1), (1, 0)])]
    unnamed x10 -> x14, local copies, waits for them, and re-layouts: 2.15 us -> 3.83 us
  transfers between devices with their start and end apart: 8 -> 7, of which waited for: 4 -> 4; matrix products, arithmetic and copies ran while one was open for 1% -> 1% of each run, Pallas kernels for 1% -> 1%
where the time goes in v11:
time: 160 us; the launch traced here: 159 us
  blocking collectives  71.9 us (45%)
  starting transfers between devices  49.5 us (31%)
  waiting for transfers between devices  21.4 us (13%)
  Pallas kernels  9.88 us (6%)
  local copies, waits for them, and re-layouts  5.09 us (3%)
    all_to_all x3, blocking collectives, to_all(): return lax.all_to_all(copies, axes, split_axis=0, concat_axis=0, tiled=True)  52 us
    all_to_all x2, blocking collectives, split_and_summed(): lax.all_to_all(blocks, axes, split_axis=0, concat_axis=0, tiled=True)  19.9 us
    all_to_all x2, waiting for transfers between devices, to_all(): return lax.all_to_all(copies, axes, split_axis=0, concat_axis=0, tiled=True)  16.9 us
    all_to_all x1, starting transfers between devices, body(): lax.all_to_all(sends, (*ROW, 'col'), split_axis=0, concat_axis=0, tiled=T...  15.7 us
    all_to_all x2, starting transfers between devices, to_all(): return lax.all_to_all(copies, axes, split_axis=0, concat_axis=0, tiled=True)  15.3 us
    ppermute x1, starting transfers between devices, body(): other = lax.ppermute(grads, 'col', [(0, 1), (1, 0)])  9.64 us
    ppermute x2, starting transfers between devices, body(): lax.ppermute(pair, 'next', shifted(n_next, k))  6.23 us
    pallas_call x1, Pallas kernels, finish(): pl.pallas_call(functools.partial(finish_kernel, replicas), in_specs=[in_v...  3.97 us
  transfers between devices with their start and end apart: 7, of which 4 were waited for; matrix products, arithmetic and copies ran while one was open for 1% of the time, Pallas kernels for 1%

profile of v11, /device:TPU:1, one launch (start us, length us, event | category | flops | bytes accessed | tf_op | source)
XLA Modules:
  0.0 158.7 jit_solution(11820097946211496451)
XLA Ops:
  0.6 1.9 %left_terms.3 = f32[12,16,128]{2,1,0:T(8,128)} custom-call(s32[1]{0:T(128)} %bitcast.2.col_ref, f32[16,384]{1,0:T(8,128)} %bitcast.5, bf16[384,384]{1,0:T(8,128)(2,1)} %refs_3_.1), custom_call_target="tpu_custom_call" | custom-call | tf_op jit(solution)/shard_map/left_terms/pallas_call | solution.py:95
  2.5 15.7 %all-to-all-start = ((f32[12,16,128]{2,1,0:T(8,128)}), f32[12,16,128]{2,1,0:T(8,128)S(1)}, u32[]{:S(2)}, u32[]{:S(2)}) async-start(f32[12,16,128]{2,1,0:T(8,128)} %left_terms.3), calls=%async_computation | async-start | bytes 196608 | tf_op jit(solution)/shard_map/left_terms/all_to_all | solution.py:260
  18.3 9.6 %collective-permute-start = (bf16[384,384]{1,0:T(8,128)(2,1)}, bf16[384,384]{1,0:T(8,128)(2,1)S(1)}, u32[]{:S(2)}, u32[]{:S(2)}) collective-permute-start(bf16[384,384]{1,0:T(8,128)(2,1)} %refs_3_.1), channel_id=1, source_target_pairs={{0,1},{1,0},{2,3},{3,2},{4,5},{5,4},{6,7},{7,6},{8,9},{9,8},{10,11... | collective-permute-start | bytes 884744 | tf_op jit(solution)/shard_map/gather_inputs/ppermute | solution.py:248
  27.9 2.6 %collective-permute-start.1 = (bf16[128,1024]{1,0:T(8,128)(2,1)}, bf16[128,1024]{1,0:T(8,128)(2,1)S(1)}, u32[]{:S(2)}, u32[]{:S(2)}) collective-permute-start(bf16[128,1024]{1,0:T(8,128)(2,1)} %acts_ref.1), channel_id=1, source_target_pairs={{0,6},{6,0},{1,7},{7,1},{2,8},{8,2},{3,9},{9,3},{4,10},{10,4},{5,1... | collective-permute-start | bytes 786440 | tf_op jit(solution)/shard_map/left_terms/ppermute | solution.py:262
  30.5 1.4 copy-done
  31.9 0.7 copy-done.6
  32.7 0.8 left_terms.4.part_ref
  33.6 12.1 %all_to_all.40 = f32[8,16,128]{2,1,0:T(8,128)S(1)} all-to-all(f32[8,16,128]{2,1,0:T(8,128)S(1)} %left_terms.5), channel_id=1, replica_groups=mesh['y'=8,'x'=4,'core'=2,'far'=2,'next'=3,'col'=2] {'x','core'}, dimensions={0} | all-to-all | bytes 131072 | tf_op jit(solution)/shard_map/left_sum/all_to_all | solution.py:26
  45.7 0.8 collective-permute-done.refs_4_
  46.5 0.7 copy-done.4
  47.2 13.9 %all_to_all.41 = f32[8,16,128]{2,1,0:T(8,128)S(1)} all-to-all(f32[8,16,128]{2,1,0:T(8,128)S(1)} %broadcast_in_dim.15), channel_id=1, replica_groups=mesh['y'=8,'x'=4,'core'=2,'far'=2,'next'=3,'col'=2] {'y'}, dimensions={0} | all-to-all | bytes 131072 | tf_op jit(solution)/shard_map/left_sum/all_to_all | solution.py:18
  61.2 3.7 %collective-permute-done.1 = bf16[128,1024]{1,0:T(8,128)(2,1)S(1)} collective-permute-done((bf16[128,1024]{1,0:T(8,128)(2,1)}, bf16[128,1024]{1,0:T(8,128)(2,1)S(1)}, u32[]{:S(2)}, u32[]{:S(2)}) %collective-permute-start.1) | collective-permute-done | bytes 262176 | tf_op jit(solution)/shard_map/left_terms/ppermute | solution.py:262
  64.9 4.3 %collective-permute-start.3 = (bf16[256,1024]{1,0:T(8,128)(2,1)S(1)}, bf16[256,1024]{1,0:T(8,128)(2,1)S(1)}, u32[]{:S(2)}, u32[]{:S(2)}) collective-permute-start(bf16[256,1024]{1,0:T(8,128)(2,1)S(1)} %pad_maximum_fusion.refs_0_), channel_id=1, source_target_pairs={{0,4},{2,0},{4,2},{1,5},{3,1},{5,3},{6,10},{8,6},{10,8},{7,11},{9,... | collective-permute-start | bytes 1572872 | tf_op jit(solution)/shard_map/left_sum/ppermute | solution.py:272
  69.2 1.9 %collective-permute-start.2 = (bf16[256,1024]{1,0:T(8,128)(2,1)S(1)}, bf16[256,1024]{1,0:T(8,128)(2,1)S(1)}, u32[]{:S(2)}, u32[]{:S(2)}) collective-permute-start(bf16[256,1024]{1,0:T(8,128)(2,1)S(1)} %pad_maximum_fusion.refs_0_), channel_id=1, source_target_pairs={{0,2},{2,4},{4,0},{1,3},{3,5},{5,1},{6,8},{8,10},{10,6},{7,9},{9,1... | collective-permute-start | bytes 1572872 | tf_op jit(solution)/shard_map/left_sum/ppermute | solution.py:272
  71.8 4.8 %all-to-all-start.3 = ((f32[6,16,128]{2,1,0:T(8,128)}), f32[6,16,128]{2,1,0:T(8,128)S(1)}, u32[]{:S(2)}, u32[]{:S(2)}) async-start(f32[6,16,128]{2,1,0:T(8,128)} %broadcast_in_dim.16), calls=%async_computation.3 | async-start | bytes 98304 | tf_op jit(solution)/shard_map/left_sum/all_to_all | solution.py:18
  76.6 12.1 %all-to-all-done.3 = f32[6,16,128]{2,1,0:T(8,128)S(1)} async-done(((f32[6,16,128]{2,1,0:T(8,128)}), f32[6,16,128]{2,1,0:T(8,128)S(1)}, u32[]{:S(2)}, u32[]{:S(2)}) %all-to-all-start.3) | async-done | bytes 49184 | tf_op jit(solution)/shard_map/left_sum/all_to_all | solution.py:18
  89.3 10.5 %all-to-all-start.4 = ((f32[8,16,128]{2,1,0:T(8,128)}), f32[8,16,128]{2,1,0:T(8,128)S(1)}, u32[]{:S(2)}, u32[]{:S(2)}) async-start(f32[8,16,128]{2,1,0:T(8,128)} %broadcast_in_dim.17), calls=%async_computation.4 | async-start | bytes 131072 | tf_op jit(solution)/shard_map/left_sum/all_to_all | solution.py:18
  99.9 4.8 %all-to-all-done.4.refs_6_.left_ref = f32[8,16,128]{2,1,0:T(8,128)S(1)} async-done(((f32[8,16,128]{2,1,0:T(8,128)}), f32[8,16,128]{2,1,0:T(8,128)S(1)}, u32[]{:S(2)}, u32[]{:S(2)}) %all-to-all-start.4) | async-done | bytes 65568 | tf_op jit(solution)/shard_map/left_sum/all_to_all | solution.py:18
  104.8 1.0 copy-done.5
  105.7 3.1 %target.1 = (f32[1024,384]{1,0:T(8,128)}, f32[8,8,128]{2,1,0:T(8,128)S(1)}) custom-call(s32[2]{0:T(128)S(1)} %pad_add_fusion.place_ref, bf16[256,1024]{1,0:T(8,128)(2,1)S(1)} %pad_maximum_fusion.refs_0_, bf16[256,1024]{1,0:T(8,128)(2,1)S(1)} %collective-permute-done.2.refs_1_, bf16[256,1024]{1,0:T(8,128)(2,1)S(1)} %collective-permute-done.3.refs_2_, ...), custom_call_target="tpu_custom_call" | custom-call | tf_op jit(solution)/shard_map/target/pallas_call | solution.py:155
  108.8 7.9 %all_to_all.42 = f32[8,8,128]{2,1,0:T(8,128)S(1)} all-to-all(f32[8,8,128]{2,1,0:T(8,128)S(1)} %get-tuple-element.18), channel_id=1, replica_groups=mesh['y'=8,'x'=4,'core'=2,'far'=2,'next'=3,'col'=2] {'x','core'}, dimensions={0} | all-to-all | bytes 65536 | tf_op jit(solution)/shard_map/right_sum/all_to_all | solution.py:26
  116.7 28.8 %all_to_all.43 = f32[16,8,128]{2,1,0:T(8,128)S(1)} all-to-all(f32[16,8,128]{2,1,0:T(8,128)S(1)} %broadcast_in_dim.18), channel_id=1, replica_groups=mesh['y'=8,'x'=4,'core'=2,'far'=2,'next'=3,'col'=2] {'y','col'}, dimensions={0} | all-to-all | bytes 131072 | tf_op jit(solution)/shard_map/right_sum/all_to_all | solution.py:18
  145.5 9.2 %all_to_all.44.joint_ref = f32[8,8,128]{2,1,0:T(8,128)S(1)} all-to-all(f32[8,8,128]{2,1,0:T(8,128)S(1)} %broadcast_in_dim.19), channel_id=1, replica_groups=mesh['y'=8,'x'=4,'core'=2,'far'=2,'next'=3,'col'=2] {'x','core'}, dimensions={0} | all-to-all | bytes 65536 | tf_op jit(solution)/shard_map/right_sum/all_to_all | solution.py:18
  154.7 4.0 %finish.1 = (f32[1024,384]{1,0:T(8,128)}, f32[16,384]{1,0:T(8,128)}) custom-call(f32[8,8,128]{2,1,0:T(8,128)S(1)} %all_to_all.44.joint_ref, f32[8,16,128]{2,1,0:T(8,128)S(1)} %all-to-all-done.4.refs_6_.left_ref, f32[1024,384]{1,0:T(8,128)} %get-tuple-element.19.target_ref), custom_call_target="tpu_custom_call", output_to_operand_aliasing={{0}: (2, {})} | custom-call | tf_op jit(solution)/shard_map/finish/pallas_call | solution.py:219
  (26 shorter events, 1.6 us)
Async XLA Ops:
  0.6 32.8 %copy-start.3 = (bf16[128,1024]{1,0:T(8,128)(2,1)S(1)}, bf16[128,1024]{1,0:T(8,128)(2,1)}, u32[]{:S(2)}) copy-start(bf16[128,1024]{1,0:T(8,128)(2,1)} %acts_ref.1) | copy-start | bytes 786436
  2.5 25.4 %all-to-all-start = ((f32[12,16,128]{2,1,0:T(8,128)}), f32[12,16,128]{2,1,0:T(8,128)S(1)}, u32[]{:S(2)}, u32[]{:S(2)}) async-start(f32[12,16,128]{2,1,0:T(8,128)} %left_terms.3), calls=%async_computation | async-start | bytes 196608 | tf_op jit(solution)/shard_map/left_terms/all_to_all | solution.py:260
  18.3 28.3 %collective-permute-start = (bf16[384,384]{1,0:T(8,128)(2,1)}, bf16[384,384]{1,0:T(8,128)(2,1)S(1)}, u32[]{:S(2)}, u32[]{:S(2)}) collective-permute-start(bf16[384,384]{1,0:T(8,128)(2,1)} %refs_3_.1), channel_id=1, source_target_pairs={{0,1},{1,0},{2,3},{3,2},{4,5},{5,4},{6,7},{7,6},{8,9},{9,8},{10,11... | collective-permute-start | bytes 884744 | tf_op jit(solution)/shard_map/gather_inputs/ppermute | solution.py:248
  27.9 37.0 %collective-permute-start.1 = (bf16[128,1024]{1,0:T(8,128)(2,1)}, bf16[128,1024]{1,0:T(8,128)(2,1)S(1)}, u32[]{:S(2)}, u32[]{:S(2)}) collective-permute-start(bf16[128,1024]{1,0:T(8,128)(2,1)} %acts_ref.1), channel_id=1, source_target_pairs={{0,6},{6,0},{1,7},{7,1},{2,8},{8,2},{3,9},{9,3},{4,10},{10,4},{5,1... | collective-permute-start | bytes 786440 | tf_op jit(solution)/shard_map/left_terms/ppermute | solution.py:262
  30.5 1.4 copy-start
  31.9 0.7 copy-start.6
  33.5 71.3 %copy-start.1 = (f32[1024,384]{1,0:T(8,128)S(1)}, f32[1024,384]{1,0:T(8,128)}, u32[]{:S(2)}) copy-start(f32[1024,384]{1,0:T(8,128)} %refs_5_.1) | copy-start | bytes 4718596
  33.5 71.3 %copy-start.2 = (bf16[384,384]{1,0:T(8,128)(2,1)S(1)}, bf16[384,384]{1,0:T(8,128)(2,1)}, u32[]{:S(2)}) copy-start(bf16[384,384]{1,0:T(8,128)(2,1)} %refs_3_.1) | copy-start | bytes 884740
  46.5 0.7 copy-start.4
  64.9 39.8 %collective-permute-start.3 = (bf16[256,1024]{1,0:T(8,128)(2,1)S(1)}, bf16[256,1024]{1,0:T(8,128)(2,1)S(1)}, u32[]{:S(2)}, u32[]{:S(2)}) collective-permute-start(bf16[256,1024]{1,0:T(8,128)(2,1)S(1)} %pad_maximum_fusion.refs_0_), channel_id=1, source_target_pairs={{0,4},{2,0},{4,2},{1,5},{3,1},{5,3},{6,10},{8,6},{10,8},{7,11},{9,... | collective-permute-start | bytes 1572872 | tf_op jit(solution)/shard_map/left_sum/ppermute | solution.py:272
  69.2 35.5 %collective-permute-start.2 = (bf16[256,1024]{1,0:T(8,128)(2,1)S(1)}, bf16[256,1024]{1,0:T(8,128)(2,1)S(1)}, u32[]{:S(2)}, u32[]{:S(2)}) collective-permute-start(bf16[256,1024]{1,0:T(8,128)(2,1)S(1)} %pad_maximum_fusion.refs_0_), channel_id=1, source_target_pairs={{0,2},{2,4},{4,0},{1,3},{3,5},{5,1},{6,8},{8,10},{10,6},{7,9},{9,1... | collective-permute-start | bytes 1572872 | tf_op jit(solution)/shard_map/left_sum/ppermute | solution.py:272
  71.8 16.9 %all-to-all-start.3 = ((f32[6,16,128]{2,1,0:T(8,128)}), f32[6,16,128]{2,1,0:T(8,128)S(1)}, u32[]{:S(2)}, u32[]{:S(2)}) async-start(f32[6,16,128]{2,1,0:T(8,128)} %broadcast_in_dim.16), calls=%async_computation.3 | async-start | bytes 98304 | tf_op jit(solution)/shard_map/left_sum/all_to_all | solution.py:18
  89.3 15.4 %all-to-all-start.4 = ((f32[8,16,128]{2,1,0:T(8,128)}), f32[8,16,128]{2,1,0:T(8,128)S(1)}, u32[]{:S(2)}, u32[]{:S(2)}) async-start(f32[8,16,128]{2,1,0:T(8,128)} %broadcast_in_dim.17), calls=%async_computation.4 | async-start | bytes 131072 | tf_op jit(solution)/shard_map/left_sum/all_to_all | solution.py:18
  104.7 1.0 copy-start.5

commit v12 on v9

--- a/solution.py
+++ b/solution.py
@@ -264,9 +264,9 @@
         blocks = local_call(left_kernel, (n_near, rank, rows // n_near), mine, acts, part)
 
     with jax.named_scope("left_sum"):
+        blocks, pair = lax.optimization_barrier((blocks, pair))
+        pieces = [pair, *(lax.ppermute(pair, "next", shifted(n_next, k)) for k in range(1, n_next))]
         part = split_and_summed(blocks, NEAR)
-        part, pair = lax.optimization_barrier((part, pair))
-        pieces = [pair, *(lax.ppermute(pair, "next", shifted(n_next, k)) for k in range(1, n_next))]
         part = summed_over(part, "y")
         part = summed_over(part, ROW)
         part, other = lax.optimization_barrier((part, other))

time: 154 us -> 148 us (0.961)
  starting transfers between devices: 50.6 us -> 47.9 us
  waiting for transfers between devices: 32.3 us -> 29.7 us
    all_to_all x1, waiting for transfers between devices: 1.36 us -> 12.2 us  [body(): lax.all_to_all(sends, (*ROW, 'col'), split_axis=0, concat_axis=0, tiled=T...]
    ppermute x1, waiting for transfers between devices: 7.45 us -> 0.01 us  [body(): swapped = lax.ppermute(acts, 'far', [(0, 1), (1, 0)])]
    all_to_all x2, waiting for transfers between devices: 23.5 us -> 16.5 us  [to_all(): return lax.all_to_all(copies, axes, split_axis=0, concat_axis=0, tiled=True)]
    ppermute x1, starting transfers between devices: 9.08 us -> 3.82 us  [body(): other = lax.ppermute(grads, 'col', [(0, 1), (1, 0)])]
    all_to_all x1, starting transfers between devices: 15.7 us -> 12.2 us  [body(): lax.all_to_all(sends, (*ROW, 'col'), split_axis=0, concat_axis=0, tiled=T...]
    ppermute x1, starting transfers between devices: 5.13 us -> 8.58 us  [body(): swapped = lax.ppermute(acts, 'far', [(0, 1), (1, 0)])]
    all_to_all x2, starting transfers between devices: 8.55 us -> 10.8 us  [to_all(): return lax.all_to_all(copies, axes, split_axis=0, concat_axis=0, tiled=True)]
  transfers between devices with their start and end apart: 8 -> 8, of which waited for: 4 -> 4; matrix products, arithmetic and copies ran while one was open for 1% -> 1% of each run, Pallas kernels for 1% -> 2%
where the time goes in v12:
time: 148 us
  blocking collectives  54.7 us (37%)
  starting transfers between devices  47.9 us (32%)
  waiting for transfers between devices  29.7 us (20%)
  Pallas kernels  10.9 us (7%)
  local copies, waits for them, and re-layouts  3.43 us (2%)
    all_to_all x3, blocking collectives, to_all(): return lax.all_to_all(copies, axes, split_axis=0, concat_axis=0, tiled=True)  46.9 us
    all_to_all x2, waiting for transfers between devices, to_all(): return lax.all_to_all(copies, axes, split_axis=0, concat_axis=0, tiled=True)  16.5 us
    all_to_all x1, waiting for transfers between devices, body(): lax.all_to_all(sends, (*ROW, 'col'), split_axis=0, concat_axis=0, tiled=T...  12.2 us
    all_to_all x1, starting transfers between devices, body(): lax.all_to_all(sends, (*ROW, 'col'), split_axis=0, concat_axis=0, tiled=T...  12.2 us
    all_to_all x2, starting transfers between devices, to_all(): return lax.all_to_all(copies, axes, split_axis=0, concat_axis=0, tiled=True)  10.8 us
    ppermute x1, starting transfers between devices, body(): swapped = lax.ppermute(acts, 'far', [(0, 1), (1, 0)])  8.58 us
    all_to_all x1, blocking collectives, split_and_summed(): lax.all_to_all(blocks, axes, split_axis=0, concat_axis=0, tiled=True)  7.86 us
    all_to_all x1, starting transfers between devices, split_and_summed(): lax.all_to_all(blocks, axes, split_axis=0, concat_axis=0, tiled=True)  6.69 us
  transfers between devices with their start and end apart: 8, of which 4 were waited for; matrix products, arithmetic and copies ran while one was open for 1% of the time, Pallas kernels for 2%

profile of v12, /device:TPU:1, one launch (start us, length us, event | category | flops | bytes accessed | tf_op | source)
XLA Modules:
  0.0 147.6 jit_solution(17554874183798824978)
XLA Ops:
  0.6 8.6 %collective-permute-start = (bf16[128,1024]{1,0:T(8,128)(2,1)}, bf16[128,1024]{1,0:T(8,128)(2,1)S(1)}, u32[]{:S(2)}, u32[]{:S(2)}) collective-permute-start(bf16[128,1024]{1,0:T(8,128)(2,1)} %acts_ref.1), channel_id=1, source_target_pairs={{0,6},{6,0},{1,7},{7,1},{2,8},{8,2},{3,9},{9,3},{4,10},{10,4},{5,1... | collective-permute-start | bytes 786440 | tf_op jit(solution)/shard_map/gather_inputs/ppermute | solution.py:248
  9.2 1.9 %left_terms.3 = f32[12,16,128]{2,1,0:T(8,128)} custom-call(s32[1]{0:T(128)} %bitcast.2.col_ref, f32[16,384]{1,0:T(8,128)} %bitcast.5, bf16[384,384]{1,0:T(8,128)(2,1)} %refs_3_.1), custom_call_target="tpu_custom_call" | custom-call | tf_op jit(solution)/shard_map/left_terms/pallas_call | solution.py:95
  11.1 12.2 %all-to-all-start = ((f32[12,16,128]{2,1,0:T(8,128)}), f32[12,16,128]{2,1,0:T(8,128)S(1)}, u32[]{:S(2)}, u32[]{:S(2)}) async-start(f32[12,16,128]{2,1,0:T(8,128)} %left_terms.3), calls=%async_computation | async-start | bytes 196608 | tf_op jit(solution)/shard_map/left_terms/all_to_all | solution.py:262
  23.3 1.4 copy-done
  24.7 0.7 copy-done.4
  25.4 0.8 left_terms.4.part_ref
  26.3 12.2 %all-to-all-done.mine_ref = f32[12,16,128]{2,1,0:T(8,128)S(1)} async-done(((f32[12,16,128]{2,1,0:T(8,128)}), f32[12,16,128]{2,1,0:T(8,128)S(1)}, u32[]{:S(2)}, u32[]{:S(2)}) %all-to-all-start) | async-done | bytes 98336 | tf_op jit(solution)/shard_map/left_terms/all_to_all | solution.py:262
  38.5 0.8 left_terms.5
  39.3 3.9 %collective-permute-start.2 = (bf16[256,1024]{1,0:T(8,128)(2,1)S(1)}, bf16[256,1024]{1,0:T(8,128)(2,1)S(1)}, u32[]{:S(2)}, u32[]{:S(2)}) collective-permute-start(bf16[256,1024]{1,0:T(8,128)(2,1)S(1)} %pad_maximum_fusion.refs_0_), channel_id=1, source_target_pairs={{0,4},{2,0},{4,2},{1,5},{3,1},{5,3},{6,10},{8,6},{10,8},{7,11},{9,... | collective-permute-start | bytes 1572872 | tf_op jit(solution)/shard_map/left_sum/ppermute | solution.py:268
  43.2 1.9 %collective-permute-start.1 = (bf16[256,1024]{1,0:T(8,128)(2,1)S(1)}, bf16[256,1024]{1,0:T(8,128)(2,1)S(1)}, u32[]{:S(2)}, u32[]{:S(2)}) collective-permute-start(bf16[256,1024]{1,0:T(8,128)(2,1)S(1)} %pad_maximum_fusion.refs_0_), channel_id=1, source_target_pairs={{0,2},{2,4},{4,0},{1,3},{3,5},{5,1},{6,8},{8,10},{10,6},{7,9},{9,1... | collective-permute-start | bytes 1572872 | tf_op jit(solution)/shard_map/left_sum/ppermute | solution.py:268
  45.1 6.7 %all-to-all-start.1 = ((f32[8,16,128]{2,1,0:T(8,128)}), f32[8,16,128]{2,1,0:T(8,128)S(1)}, u32[]{:S(2)}, u32[]{:S(2)}) async-start(f32[8,16,128]{2,1,0:T(8,128)} %left_terms.5), calls=%async_computation.1 | async-start | bytes 131072 | tf_op jit(solution)/shard_map/left_sum/all_to_all | solution.py:26
  51.8 3.8 %collective-permute-start.3 = (bf16[384,384]{1,0:T(8,128)(2,1)S(1)}, bf16[384,384]{1,0:T(8,128)(2,1)}, u32[]{:S(2)}, u32[]{:S(2)}) collective-permute-start(bf16[384,384]{1,0:T(8,128)(2,1)S(1)} %copy-done.2), channel_id=1, source_target_pairs={{0,1},{1,0},{2,3},{3,2},{4,5},{5,4},{6,7},{7,6},{8,9},{9,8},{10,11... | collective-permute-start | bytes 884744 | tf_op jit(solution)/shard_map/gather_inputs/ppermute | solution.py:250
  55.6 1.0 all-to-all-done.1
  56.7 13.9 %all_to_all.40 = f32[8,16,128]{2,1,0:T(8,128)S(1)} all-to-all(f32[8,16,128]{2,1,0:T(8,128)S(1)} %broadcast_in_dim.15), channel_id=1, replica_groups=mesh['y'=8,'x'=4,'core'=2,'far'=2,'next'=3,'col'=2] {'y'}, dimensions={0} | all-to-all | bytes 131072 | tf_op jit(solution)/shard_map/left_sum/all_to_all | solution.py:18
  71.2 4.9 %all-to-all-start.3 = ((f32[6,16,128]{2,1,0:T(8,128)}), f32[6,16,128]{2,1,0:T(8,128)S(1)}, u32[]{:S(2)}, u32[]{:S(2)}) async-start(f32[6,16,128]{2,1,0:T(8,128)} %broadcast_in_dim.16), calls=%async_computation.3 | async-start | bytes 98304 | tf_op jit(solution)/shard_map/left_sum/all_to_all | solution.py:18
  76.1 11.7 %all-to-all-done.3 = f32[6,16,128]{2,1,0:T(8,128)S(1)} async-done(((f32[6,16,128]{2,1,0:T(8,128)}), f32[6,16,128]{2,1,0:T(8,128)S(1)}, u32[]{:S(2)}, u32[]{:S(2)}) %all-to-all-start.3) | async-done | bytes 49184 | tf_op jit(solution)/shard_map/left_sum/all_to_all | solution.py:18
  87.8 0.6 broadcast_in_dim.17
  88.5 5.9 %all-to-all-start.4 = ((f32[8,16,128]{2,1,0:T(8,128)}), f32[8,16,128]{2,1,0:T(8,128)S(1)}, u32[]{:S(2)}, u32[]{:S(2)}) async-start(f32[8,16,128]{2,1,0:T(8,128)} %broadcast_in_dim.17), calls=%async_computation.4 | async-start | bytes 131072 | tf_op jit(solution)/shard_map/left_sum/all_to_all | solution.py:18
  94.4 4.8 %all-to-all-done.4.refs_6_.left_ref = f32[8,16,128]{2,1,0:T(8,128)S(1)} async-done(((f32[8,16,128]{2,1,0:T(8,128)}), f32[8,16,128]{2,1,0:T(8,128)S(1)}, u32[]{:S(2)}, u32[]{:S(2)}) %all-to-all-start.4) | async-done | bytes 65568 | tf_op jit(solution)/shard_map/left_sum/all_to_all | solution.py:18
  99.2 3.5 %target.1 = (f32[1024,384]{1,0:T(8,128)}, f32[8,8,128]{2,1,0:T(8,128)S(1)}) custom-call(s32[2]{0:T(128)S(1)} %pad_add_fusion.place_ref, bf16[256,1024]{1,0:T(8,128)(2,1)S(1)} %pad_maximum_fusion.refs_0_, bf16[256,1024]{1,0:T(8,128)(2,1)S(1)} %collective-permute-done.1.refs_1_, bf16[256,1024]{1,0:T(8,128)(2,1)S(1)} %collective-permute-done.2.refs_2_, ...), custom_call_target="tpu_custom_call" | custom-call | tf_op jit(solution)/shard_map/target/pallas_call | solution.py:155
  102.7 7.9 %all_to_all.41 = f32[8,8,128]{2,1,0:T(8,128)S(1)} all-to-all(f32[8,8,128]{2,1,0:T(8,128)S(1)} %get-tuple-element.14), channel_id=1, replica_groups=mesh['y'=8,'x'=4,'core'=2,'far'=2,'next'=3,'col'=2] {'x','core'}, dimensions={0} | all-to-all | bytes 65536 | tf_op jit(solution)/shard_map/right_sum/all_to_all | solution.py:26
  110.6 23.8 %all_to_all.42 = f32[16,8,128]{2,1,0:T(8,128)S(1)} all-to-all(f32[16,8,128]{2,1,0:T(8,128)S(1)} %broadcast_in_dim.18), channel_id=1, replica_groups=mesh['y'=8,'x'=4,'core'=2,'far'=2,'next'=3,'col'=2] {'y','col'}, dimensions={0} | all-to-all | bytes 131072 | tf_op jit(solution)/shard_map/right_sum/all_to_all | solution.py:18
  134.4 9.2 %all_to_all.43.joint_ref = f32[8,8,128]{2,1,0:T(8,128)S(1)} all-to-all(f32[8,8,128]{2,1,0:T(8,128)S(1)} %broadcast_in_dim.19), channel_id=1, replica_groups=mesh['y'=8,'x'=4,'core'=2,'far'=2,'next'=3,'col'=2] {'x','core'}, dimensions={0} | all-to-all | bytes 65536 | tf_op jit(solution)/shard_map/right_sum/all_to_all | solution.py:18
  143.7 4.0 %finish.1 = (f32[1024,384]{1,0:T(8,128)}, f32[16,384]{1,0:T(8,128)}) custom-call(f32[8,8,128]{2,1,0:T(8,128)S(1)} %all_to_all.43.joint_ref, f32[8,16,128]{2,1,0:T(8,128)S(1)} %all-to-all-done.4.refs_6_.left_ref, f32[1024,384]{1,0:T(8,128)} %get-tuple-element.15.target_ref), custom_call_target="tpu_custom_call", output_to_operand_aliasing={{0}: (2, {})} | custom-call | tf_op jit(solution)/shard_map/finish/pallas_call | solution.py:219
  (23 shorter events, 0.8 us)
Async XLA Ops:
  0.6 25.6 %copy-start.3 = (bf16[128,1024]{1,0:T(8,128)(2,1)S(1)}, bf16[128,1024]{1,0:T(8,128)(2,1)}, u32[]{:S(2)}) copy-start(bf16[128,1024]{1,0:T(8,128)(2,1)} %acts_ref.1) | copy-start | bytes 786436
  0.6 25.6 %collective-permute-start = (bf16[128,1024]{1,0:T(8,128)(2,1)}, bf16[128,1024]{1,0:T(8,128)(2,1)S(1)}, u32[]{:S(2)}, u32[]{:S(2)}) collective-permute-start(bf16[128,1024]{1,0:T(8,128)(2,1)} %acts_ref.1), channel_id=1, source_target_pairs={{0,6},{6,0},{1,7},{7,1},{2,8},{8,2},{3,9},{9,3},{4,10},{10,4},{5,1... | collective-permute-start | bytes 786440 | tf_op jit(solution)/shard_map/gather_inputs/ppermute | solution.py:248
  11.1 27.4 %all-to-all-start = ((f32[12,16,128]{2,1,0:T(8,128)}), f32[12,16,128]{2,1,0:T(8,128)S(1)}, u32[]{:S(2)}, u32[]{:S(2)}) async-start(f32[12,16,128]{2,1,0:T(8,128)} %left_terms.3), calls=%async_computation | async-start | bytes 196608 | tf_op jit(solution)/shard_map/left_terms/all_to_all | solution.py:262
  23.3 1.4 copy-start
  24.7 0.7 copy-start.4
  25.4 26.4 %copy-start.2 = (bf16[384,384]{1,0:T(8,128)(2,1)S(1)}, bf16[384,384]{1,0:T(8,128)(2,1)}, u32[]{:S(2)}) copy-start(bf16[384,384]{1,0:T(8,128)(2,1)} %refs_3_.1) | copy-start | bytes 884740
  26.2 73.0 %copy-start.1 = (f32[1024,384]{1,0:T(8,128)S(1)}, f32[1024,384]{1,0:T(8,128)}, u32[]{:S(2)}) copy-start(f32[1024,384]{1,0:T(8,128)} %refs_5_.1) | copy-start | bytes 4718596
  39.3 59.9 %collective-permute-start.2 = (bf16[256,1024]{1,0:T(8,128)(2,1)S(1)}, bf16[256,1024]{1,0:T(8,128)(2,1)S(1)}, u32[]{:S(2)}, u32[]{:S(2)}) collective-permute-start(bf16[256,1024]{1,0:T(8,128)(2,1)S(1)} %pad_maximum_fusion.refs_0_), channel_id=1, source_target_pairs={{0,4},{2,0},{4,2},{1,5},{3,1},{5,3},{6,10},{8,6},{10,8},{7,11},{9,... | collective-permute-start | bytes 1572872 | tf_op jit(solution)/shard_map/left_sum/ppermute | solution.py:268
  43.2 56.0 %collective-permute-start.1 = (bf16[256,1024]{1,0:T(8,128)(2,1)S(1)}, bf16[256,1024]{1,0:T(8,128)(2,1)S(1)}, u32[]{:S(2)}, u32[]{:S(2)}) collective-permute-start(bf16[256,1024]{1,0:T(8,128)(2,1)S(1)} %pad_maximum_fusion.refs_0_), channel_id=1, source_target_pairs={{0,2},{2,4},{4,0},{1,3},{3,5},{5,1},{6,8},{8,10},{10,6},{7,9},{9,1... | collective-permute-start | bytes 1572872 | tf_op jit(solution)/shard_map/left_sum/ppermute | solution.py:268
  45.1 11.5 %all-to-all-start.1 = ((f32[8,16,128]{2,1,0:T(8,128)}), f32[8,16,128]{2,1,0:T(8,128)S(1)}, u32[]{:S(2)}, u32[]{:S(2)}) async-start(f32[8,16,128]{2,1,0:T(8,128)} %left_terms.5), calls=%async_computation.1 | async-start | bytes 131072 | tf_op jit(solution)/shard_map/left_sum/all_to_all | solution.py:26
  51.8 36.0 %collective-permute-start.3 = (bf16[384,384]{1,0:T(8,128)(2,1)S(1)}, bf16[384,384]{1,0:T(8,128)(2,1)}, u32[]{:S(2)}, u32[]{:S(2)}) collective-permute-start(bf16[384,384]{1,0:T(8,128)(2,1)S(1)} %copy-done.2), channel_id=1, source_target_pairs={{0,1},{1,0},{2,3},{3,2},{4,5},{5,4},{6,7},{7,6},{8,9},{9,8},{10,11... | collective-permute-start | bytes 884744 | tf_op jit(solution)/shard_map/gather_inputs/ppermute | solution.py:250
  71.2 16.6 %all-to-all-start.3 = ((f32[6,16,128]{2,1,0:T(8,128)}), f32[6,16,128]{2,1,0:T(8,128)S(1)}, u32[]{:S(2)}, u32[]{:S(2)}) async-start(f32[6,16,128]{2,1,0:T(8,128)} %broadcast_in_dim.16), calls=%async_computation.3 | async-start | bytes 98304 | tf_op jit(solution)/shard_map/left_sum/all_to_all | solution.py:18
  88.5 10.7 %all-to-all-start.4 = ((f32[8,16,128]{2,1,0:T(8,128)}), f32[8,16,128]{2,1,0:T(8,128)S(1)}, u32[]{:S(2)}, u32[]{:S(2)}) async-start(f32[8,16,128]{2,1,0:T(8,128)} %broadcast_in_dim.17), calls=%async_computation.4 | async-start | bytes 131072 | tf_op jit(solution)/shard_map/left_sum/all_to_all | solution.py:18
